TPU v7x, 32 devices: a whole 2x2x4 slice. The times are simulated.
32 devices in a mesh: dp: 2 (over core), expert: 16 (over z, y, x).
Axes of the slice: x: 2, y: 2, z: 4, core: 2. Of those that a mesh axis runs over, the one named last changes fastest.
Arguments:
- tokens: bfloat16 [16384, 768], P(('dp', 'expert')), may hold values from -6 to 6
- cotangent: bfloat16 [16384, 768], P(('dp', 'expert')), may hold values from -6 to 6
- routes: int32 [16384, 1], P(('dp', 'expert')), may hold values from 0 to 15; in each aligned block of 512 rows (0 to 511, 512 to 1023, ...) at most 64 rows name the same one
- buckets: int32 [512, 512], replicated, may hold values from 0 to 31, as said below
- gain_attn: bfloat16 [768], P(('dp', 'expert')), may hold values from 0.099609375 to 1.8984375
- w_qkv: bfloat16 [768, 2304], P(('dp', 'expert')), may hold values from -0.21875 to 0.21875
- w_att: bfloat16 [768, 768], P(('dp', 'expert')), may hold values from -1.25 to 1.25
- rel_bias: float32 [32, 12], replicated, may hold values from -4 to 4
- gain_moe: bfloat16 [768], P(('dp', 'expert')), may hold values from 0.099609375 to 1.8984375
- w_router: bfloat16 [768, 16], P(('dp', 'expert')), may hold values from -0.15625 to 0.15625
- w_in: bfloat16 [16, 768, 3072], P('expert'), may hold values from -0.21875 to 0.21875
- w_out: bfloat16 [16, 768, 3072], P('expert'), may hold values from -1.75 to 1.75
Outputs:
- mixed: bfloat16 [16384, 768], P(('dp', 'expert'))
- grad_tokens: float32 [16384, 768], P(('dp', 'expert'))
- grad_gain_attn: float32 [768], P(('dp', 'expert'))
- grad_qkv: float32 [768, 2304], P(('dp', 'expert'))
- grad_att: float32 [768, 768], P(('dp', 'expert'))
- grad_bias: float32 [32, 12], replicated
- grad_gain_moe: float32 [768], P(('dp', 'expert'))
- grad_router: float32 [768, 16], P(('dp', 'expert'))
- grad_in: float32 [16, 768, 3072], P('expert', None, 'dp')
- grad_out: float32 [16, 768, 3072], P('expert', None, 'dp')
Inputs may be any that keep to these rules, and one draw needn't show every extreme that they name: `routes`: among the tokens of one device no expert is named more than 64 times; some experts are named far more often than the mean. buckets[i, j] depends only on j - i, never falls as |j - i| grows on either side, is below 16 for j <= i and 16 or more for j > i, and is 0 for j = i.
All inputs are finite; a program needn't handle non-finite values.
Results may differ from a plain program's by a relative error of at most 0.019.
Values may be sent and summed in bfloat16 or wider, within the bound.
A program may use at most 256 MiB of HBM per device.

v0:
```python
import jax
import jax.numpy as jnp
from jax import lax
from jax.sharding import PartitionSpec as P

EPSILON = 1e-06
PRECISE = lax.Precision.HIGHEST


def rms_scale(values, gains):
    return values * lax.rsqrt(jnp.mean(values * values, axis=-1, keepdims=True) + EPSILON) * gains


def split_heads(packed, width, heads):
    rows_here = packed.shape[0]
    head_dim = width // heads
    return (
        packed[:, :width].reshape(rows_here, heads, head_dim),
        packed[:, width : 2 * width].reshape(rows_here, heads, head_dim),
        packed[:, 2 * width :].reshape(rows_here, heads, head_dim),
    )


def shards(
    tokens,
    cotangent,
    routes,
    buckets,
    gain_attn,
    w_qkv,
    w_att,
    rel_bias,
    gain_moe,
    w_router,
    w_in,
    w_out,
):
    full_gain_attn, full_qkv, full_att, full_gain_moe, full_router = (
        lax.all_gather(gain_attn, ("dp", "expert"), axis=0, tiled=True),
        lax.all_gather(w_qkv, ("dp", "expert"), axis=0, tiled=True),
        lax.all_gather(w_att, ("dp", "expert"), axis=0, tiled=True),
        lax.all_gather(gain_moe, ("dp", "expert"), axis=0, tiled=True),
        lax.all_gather(w_router, ("dp", "expert"), axis=0, tiled=True),
    )
    tok_count, width = tokens.shape
    seq_len = buckets.shape[0]
    seq_count = tok_count // seq_len
    heads = rel_bias.shape[1]
    score_scale = (width // heads) ** (-0.5)
    experts = full_router.shape[1]
    capacity = max(2, 2 * tok_count // experts)
    kinds = jnp.arange(rel_bias.shape[0], dtype=jnp.int32)
    bucket_hits = (buckets[None, :, :] == kinds[:, None, None]).astype(jnp.bfloat16)
    bias_table = jnp.einsum(
        "bij,bh->hij",
        (buckets[None, :, :] == kinds[:, None, None]).astype(jnp.float32),
        rel_bias,
        precision=PRECISE,
    )
    inputs = tokens.astype(jnp.float32)
    normed_f, attn_norm_pull = jax.vjp(rms_scale, inputs, full_gain_attn.astype(jnp.float32))
    normed = normed_f.astype(jnp.bfloat16)
    packed = jnp.dot(normed, full_qkv, preferred_element_type=jnp.float32).astype(jnp.bfloat16)
    packed_seqs = packed.reshape(seq_count, seq_len, 3 * width)

    def scores_of(query_rows, key_rows):
        return (
            jnp.einsum("qhd,khd->hqk", query_rows, key_rows, preferred_element_type=jnp.float32)
            * score_scale
            + bias_table
        )

    def attend(block):
        query_rows, key_rows, value_rows = split_heads(block, width, heads)
        scores = scores_of(query_rows, key_rows)
        log_total = jax.nn.logsumexp(scores, axis=-1, keepdims=True)
        weights = jnp.exp(scores - log_total).astype(jnp.bfloat16)
        mixed_heads = jnp.einsum(
            "hqk,khd->qhd", weights, value_rows, preferred_element_type=jnp.float32
        )
        return (mixed_heads.reshape(seq_len, width).astype(jnp.bfloat16), log_total)

    attended, log_totals = lax.map(attend, packed_seqs)
    attended = attended.reshape(tok_count, width)
    middle = inputs + jnp.dot(attended, full_att, preferred_element_type=jnp.float32)
    moe_f, moe_norm_pull = jax.vjp(rms_scale, middle, full_gain_moe.astype(jnp.float32))
    moe_in = moe_f.astype(jnp.bfloat16)
    logits = jnp.dot(moe_in, full_router, preferred_element_type=jnp.float32)
    router_prob = jax.nn.softmax(logits, axis=-1)
    chosen = routes[:, 0]
    picked = (chosen[:, None] == jnp.arange(experts, dtype=jnp.int32)[None, :]).astype(jnp.int32)
    gate_value = jnp.sum(router_prob * picked, axis=-1)
    ranks = jnp.sum(
        (jnp.cumsum(picked, axis=0, dtype=jnp.int32) - 1) * picked, axis=1, dtype=jnp.int32
    )
    slot_of = chosen * capacity + ranks
    slot_token = (
        jnp.zeros((experts * capacity,), jnp.int32)
        .at[slot_of]
        .set(jnp.arange(tok_count, dtype=jnp.int32))
    )
    outgoing = jnp.take(moe_in, slot_token, axis=0).reshape(experts, capacity, width)
    arrived = lax.all_to_all(
        jnp.sum(picked, axis=0, dtype=jnp.int32).reshape(experts, 1),
        "expert",
        split_axis=0,
        concat_axis=0,
        tiled=True,
    )
    slot_mask = (jnp.arange(capacity, dtype=jnp.int32)[None, :] < arrived).astype(jnp.bfloat16)
    upstream = cotangent.astype(jnp.float32)
    row_grad = (gate_value[:, None] * upstream).astype(jnp.bfloat16)
    grad_slots = jnp.take(row_grad, slot_token, axis=0).reshape(experts, capacity, width)
    expert_in = w_in[0]
    expert_out = w_out[0]
    received = lax.all_to_all(outgoing, "expert", split_axis=0, concat_axis=0, tiled=True)
    hidden = jnp.einsum("nmd,df->nmf", received, expert_in, preferred_element_type=jnp.float32)
    active = jax.nn.gelu(hidden).astype(jnp.bfloat16)
    produced = jnp.einsum(
        "nmf,df->nmd", active, expert_out, preferred_element_type=jnp.float32
    ).astype(jnp.bfloat16)
    returned = lax.all_to_all(produced, "expert", split_axis=0, concat_axis=0, tiled=True)
    grad_rows = lax.all_to_all(grad_slots, "expert", split_axis=0, concat_axis=0, tiled=True)
    grad_rows = grad_rows * slot_mask[:, :, None]
    expert_back = jnp.take(returned.reshape(experts * capacity, width), slot_of, axis=0).astype(
        jnp.float32
    )
    mixed = (middle + gate_value[:, None] * expert_back).astype(jnp.bfloat16)
    gate_grad = jnp.sum(upstream * expert_back, axis=-1)
    hidden = jnp.einsum("nmd,df->nmf", received, expert_in, preferred_element_type=jnp.float32)
    active_f, gelu_pull = jax.vjp(jax.nn.gelu, hidden)
    active = active_f.astype(jnp.bfloat16)
    active_grad = jnp.einsum(
        "nmd,df->nmf", grad_rows, expert_out, preferred_element_type=jnp.float32
    )
    hidden_grad = gelu_pull(active_grad)[0].astype(jnp.bfloat16)
    row_back = jnp.einsum(
        "nmf,df->nmd", hidden_grad, expert_in, preferred_element_type=jnp.float32
    ).astype(jnp.bfloat16)
    came_back = lax.all_to_all(row_back, "expert", split_axis=0, concat_axis=0, tiled=True)
    partial_in = jnp.einsum(
        "nmd,nmf->df", received, hidden_grad, preferred_element_type=jnp.float32
    )
    partial_out = jnp.einsum("nmd,nmf->df", grad_rows, active, preferred_element_type=jnp.float32)
    grad_in, grad_out = (
        lax.psum_scatter(
            partial_in[None].astype(jnp.bfloat16), "dp", scatter_dimension=2, tiled=True
        ).astype(jnp.float32),
        lax.psum_scatter(
            partial_out[None].astype(jnp.bfloat16), "dp", scatter_dimension=2, tiled=True
        ).astype(jnp.float32),
    )
    logit_grad = ((gate_value * gate_grad)[:, None] * (picked - router_prob)).astype(jnp.bfloat16)
    router_grad = jnp.einsum("td,te->de", moe_in, logit_grad, preferred_element_type=jnp.float32)
    moe_in_grad = jnp.take(came_back.reshape(experts * capacity, width), slot_of, axis=0).astype(
        jnp.float32
    )
    moe_in_grad = moe_in_grad + jnp.einsum(
        "te,de->td", logit_grad, full_router, preferred_element_type=jnp.float32
    )
    middle_norm_grad, gain_moe_grad = moe_norm_pull(moe_in_grad)
    middle_grad = upstream + middle_norm_grad
    attn_grad = middle_grad.astype(jnp.bfloat16)
    att_weight_grad = jnp.einsum(
        "td,te->de", attended, attn_grad, preferred_element_type=jnp.float32
    )
    attended_grad = jnp.einsum(
        "te,de->td", attn_grad, full_att, preferred_element_type=jnp.float32
    ).astype(jnp.bfloat16)

    def attend_back(pieces):
        block, block_grad, log_total = pieces
        query_rows, key_rows, value_rows = split_heads(block, width, heads)
        grad_heads = block_grad.reshape(seq_len, heads, width // heads)
        scores = scores_of(query_rows, key_rows)
        chance = jnp.exp(scores - log_total)
        weight_grad = jnp.einsum(
            "qhd,khd->hqk", grad_heads, value_rows, preferred_element_type=jnp.float32
        )
        score_grad = (
            chance * (weight_grad - jnp.sum(chance * weight_grad, axis=-1, keepdims=True))
        ).astype(jnp.bfloat16)
        query_grad = (
            jnp.einsum("hqk,khd->qhd", score_grad, key_rows, preferred_element_type=jnp.float32)
            * score_scale
        )
        key_grad = (
            jnp.einsum("hqk,qhd->khd", score_grad, query_rows, preferred_element_type=jnp.float32)
            * score_scale
        )
        value_grad = jnp.einsum(
            "hqk,qhd->khd",
            chance.astype(jnp.bfloat16),
            grad_heads,
            preferred_element_type=jnp.float32,
        )
        packed_grad = jnp.concatenate(
            [
                query_grad.reshape(seq_len, width),
                key_grad.reshape(seq_len, width),
                value_grad.reshape(seq_len, width),
            ],
            axis=1,
        ).astype(jnp.bfloat16)
        bias_grad = jnp.einsum(
            "hij,bij->bh", score_grad, bucket_hits, preferred_element_type=jnp.float32
        )
        return (packed_grad, bias_grad)

    packed_grads, bias_grads = lax.map(
        attend_back, (packed_seqs, attended_grad.reshape(seq_count, seq_len, width), log_totals)
    )
    packed_grads = packed_grads.reshape(tok_count, 3 * width)
    qkv_weight_grad = jnp.einsum(
        "td,te->de", normed, packed_grads, preferred_element_type=jnp.float32
    )
    normed_grad = jnp.einsum(
        "te,de->td", packed_grads, full_qkv, preferred_element_type=jnp.float32
    )
    input_norm_grad, gain_attn_grad = attn_norm_pull(normed_grad)
    grad_tokens = middle_grad + input_norm_grad
    summed = (
        lax.psum_scatter(gain_attn_grad, ("dp", "expert"), scatter_dimension=0, tiled=True),
        lax.psum_scatter(qkv_weight_grad, ("dp", "expert"), scatter_dimension=0, tiled=True),
        lax.psum_scatter(att_weight_grad, ("dp", "expert"), scatter_dimension=0, tiled=True),
        lax.psum_scatter(gain_moe_grad, ("dp", "expert"), scatter_dimension=0, tiled=True),
        lax.psum_scatter(router_grad, ("dp", "expert"), scatter_dimension=0, tiled=True),
    )
    grad_bias = lax.psum(jnp.sum(bias_grads, axis=0), ("dp", "expert"))
    return (
        mixed,
        grad_tokens,
        summed[0],
        summed[1],
        summed[2],
        grad_bias,
        summed[3],
        summed[4],
        grad_in,
        grad_out,
    )


def solution(mesh):
    return jax.shard_map(
        shards,
        mesh=mesh,
        in_specs=(
            P(("dp", "expert"), None),
            P(("dp", "expert"), None),
            P(("dp", "expert"), None),
            P(),
            P(("dp", "expert")),
            P(("dp", "expert"), None),
            P(("dp", "expert"), None),
            P(),
            P(("dp", "expert")),
            P(("dp", "expert"), None),
            P("expert", None, None),
            P("expert", None, None),
        ),
        out_specs=(
            P(("dp", "expert"), None),
            P(("dp", "expert"), None),
            P(("dp", "expert")),
            P(("dp", "expert"), None),
            P(("dp", "expert"), None),
            P(),
            P(("dp", "expert")),
            P(("dp", "expert"), None),
            P("expert", None, "dp"),
            P("expert", None, "dp"),
        ),
        check_vma=False,
    )
```

profile of v0, /device:TPU:0, one launch (start us, length us, event | category | flops | bytes accessed | tf_op | source)
XLA Modules:
  0.0 687.8 jit_solution(1135365246357981863)
XLA Ops:
  8.0 0.7 all-gather.6.cloned.1.call-update
  8.7 0.7 fusion.70
  9.4 1.1 reduce-window.6
  10.8 0.9 convert_reduce_fusion
  11.7 0.7 compare_select_fusion
  12.3 2.4 scatter_custom_fusion
  14.8 1.4 fusion.43
  16.2 0.8 dynamic-update-slice
  17.1 0.8 dynamic-update-slice.1
  17.9 42.2 %all-reduce.6 = (bf16[768]{0:T(1024)(128)(2,1)S(1)}, bf16[768]{0:T(1024)(128)(2,1)S(1)}) all-reduce(bf16[768]{0:T(1024)(128)(2,1)S(1)} %dynamic-update-slice, bf16[768]{0:T(1024)(128)(2,1)S(1)} %dynamic-update-slice.1), channel_id=1, replica_groups=mesh['dp'=2,'expert'=16] {'dp','expert'}, use_global_device_ids=true, to_apply=%add | all-reduce | flops 1536 | bytes 6144
  60.1 14.9 %fusion.1 = f32[512,512,12]{1,2,0:T(8,128)} fusion(s32[512,512]{1,0:T(8,128)} %param.19, f32[32,12]{0,1:T(8,128)S(1)} %copy-done), kind=kOutput, calls=%fused_computation.7 | convolution fusion | flops 1216348160 | bytes 13633024 | tf_op jit(solution)/shard_map/bij,bh->hij/dot_general | solution.py:54
  75.0 17.9 %copy.65 = f32[512,512,12]{0,1,2:T(8,128)} copy(f32[512,512,12]{1,2,0:T(8,128)} %fusion.1) | data formatting | bytes 25165824 | tf_op jit(solution)/shard_map/bij,bh->hij/dot_general | solution.py:54
  92.9 4.1 convolution_convert_fusion
  98.0 6.3 fusion.86
  104.4 1.9 exponential_reduce_fusion
  106.3 2.6 copy-done.2
  108.9 2.1 fusion.45
  111.0 18.8 %all-gather.6.cloned.1.call-done = bf16[768,768]{1,0:T(8,128)(2,1)} async-done(((bf16[24,768]{1,0:T(8,128)(2,1)}), bf16[768,768]{1,0:T(8,128)(2,1)}) %all-gather.6.cloned.1.call-update) | async-done | bytes 1179664 | tf_op jit(solution)/shard_map/all_gather | solution.py:41
  129.8 2.2 multiply_reduce_fusion.3
  132.0 1.1 copy-done.4
  133.4 4.0 gather_fusion
  137.6 42.6 %all_to_all.29 = bf16[16,64,768]{2,1,0:T(8,128)(2,1)S(1)} all-to-all(bf16[16,64,768]{2,1,0:T(8,128)(2,1)S(1)} %bitcast.120), channel_id=1, replica_groups=mesh['dp'=2,'expert'=16] {'expert'}, dimensions={0} | all-to-all | bytes 3145728 | tf_op jit(solution)/shard_map/all_to_all | solution.py:116
  180.2 1.1 copy-done.17
  181.3 7.0 %fusion.18 = f32[16,64,3072]{2,1,0:T(8,128)S(1)} fusion(bf16[16,64,768]{2,1,0:T(8,128)(2,1)S(1)} %all_to_all.29, bf16[1,768,3072]{2,1,0:T(8,128)(2,1)} %param.26), kind=kOutput, calls=%fused_computation.34 | convolution fusion | flops 4831838208 | bytes 18874368 | tf_op jit(solution)/shard_map/nmd,df->nmf/dot_general | solution.py:117
  188.3 4.5 copy-done.28
  192.8 8.6 %fusion.29 = bf16[16,64,768]{2,1,0:T(8,128)(2,1)} fusion(bf16[1,768,3072]{2,1,0:T(8,128)(2,1)S(1)} %bitcast.140, f32[16,64,3072]{2,1,0:T(8,128)S(1)} %fusion.18), kind=kOutput, calls=%fused_computation.54 | convolution fusion | flops 4860936192 | bytes 18874368 | tf_op jit(solution)/shard_map/nmf,df->nmd/dot_general | solution.py:119
  201.3 4.0 all-to-all-start.1
  205.3 0.7 copy.69
  206.0 87.9 %all-gather = bf16[32,24,16]{1,2,0:T(8,128)(2,1)S(1)} all-gather(bf16[1,24,16]{1,2,0:T(8,128)(2,1)S(1)} %bitcast.136), channel_id=1, replica_groups=mesh['dp'=2,'expert'=16] {'dp','expert'}, dimensions={0}, use_global_device_ids=true | all-gather | bytes 25344 | tf_op jit(solution)/shard_map/all_gather | solution.py:43
  294.5 4.3 all-to-all-start.3
  298.8 2.7 gather_fusion.1
  301.5 2.0 fusion.41
  303.6 5.2 gather_fusion.2
  308.8 2.8 broadcast_select_fusion
  311.5 7.0 %all-to-all-start.2 = ((bf16[16,64,768]{2,1,0:T(8,128)(2,1)}), bf16[16,64,768]{2,1,0:T(8,128)(2,1)}, u32[]{:S(2)}, u32[]{:S(2)}) async-start(bf16[16,64,768]{2,1,0:T(8,128)(2,1)} %bitcast.19), calls=%async_computation.2 | async-start | bytes 3145728 | tf_op jit(solution)/shard_map/all_to_all | solution.py:123
  319.1 33.1 %all-to-all-done.2 = bf16[16,64,768]{2,1,0:T(8,128)(2,1)} async-done(((bf16[16,64,768]{2,1,0:T(8,128)(2,1)}), bf16[16,64,768]{2,1,0:T(8,128)(2,1)}, u32[]{:S(2)}, u32[]{:S(2)}) %all-to-all-start.2) | async-done | bytes 1572896 | tf_op jit(solution)/shard_map/all_to_all | solution.py:123
  352.2 15.3 %fusion.10 = bf16[16,64,3072]{2,1,0:T(8,128)(2,1)S(1)} fusion(f32[16,64,3072]{2,1,0:T(8,128)} %copy-done.28, bf16[1,768,3072]{2,1,0:T(8,128)(2,1)} %param.27, bf16[16,64,768]{2,1,0:T(8,128)(2,1)} %all-to-all-done.2, bf16[16,64]{1,0:T(8,128)(2,1)S(1)} %fusion.74), kind=kOutput, calls=%fused_computation.18 | convolution fusion | flops 4895539200 | bytes 25167872 | tf_op jit(solution)/shard_map/nmd,df->nmf/dot_general | solution.py:133
  367.4 2.7 copy-done.27
  370.1 6.8 fusion.20
  377.0 11.0 %fusion.21 = bf16[1,768,3072]{2,1,0:T(8,128)(2,1)} fusion(bf16[16,64,768]{2,1,0:T(8,128)(2,1)} %all-to-all-done.2, bf16[16,64]{1,0:T(8,128)(2,1)S(1)} %fusion.74, f32[16,64,3072]{2,1,0:T(8,128)} %copy-done.28), kind=kOutput, calls=%fused_computation.37 | convolution fusion | flops 4863295488 | bytes 18876416 | tf_op jit(solution)/shard_map/nmd,nmf->df/dot_general | solution.py:144
  388.0 10.2 %fusion.26 = bf16[16,64,768]{2,1,0:T(8,128)(2,1)} fusion(bf16[16,64,3072]{2,1,0:T(8,128)(2,1)} %copy-done.27, bf16[1,768,3072]{2,1,0:T(8,128)(2,1)} %param.26), kind=kOutput, calls=%fused_computation.53 | convolution fusion | flops 4832624640 | bytes 12582912 | tf_op jit(solution)/shard_map/nmf,df->nmd/dot_general | solution.py:137
  398.2 7.0 %all-to-all-start.4 = ((bf16[16,64,768]{2,1,0:T(8,128)(2,1)}), bf16[16,64,768]{2,1,0:T(8,128)(2,1)S(1)}, u32[]{:S(2)}, u32[]{:S(2)}) async-start(bf16[16,64,768]{2,1,0:T(8,128)(2,1)} %fusion.26), calls=%async_computation.4 | async-start | bytes 3145728 | tf_op jit(solution)/shard_map/all_to_all | solution.py:140
  405.2 33.4 %all-to-all-done.4 = bf16[16,64,768]{2,1,0:T(8,128)(2,1)S(1)} async-done(((bf16[16,64,768]{2,1,0:T(8,128)(2,1)}), bf16[16,64,768]{2,1,0:T(8,128)(2,1)S(1)}, u32[]{:S(2)}, u32[]{:S(2)}) %all-to-all-start.4) | async-done | bytes 1572896 | tf_op jit(solution)/shard_map/all_to_all | solution.py:140
  438.7 2.7 gather_fusion.3
  441.4 2.5 multiply_reduce_fusion.1
  443.9 3.0 convert_add_fusion.1
  446.9 1.7 convolution_convert_fusion.1
  448.6 2.3 copy.70
  450.9 3.4 fusion.58
  454.4 12.1 %multiply_reduce_fusion = (f32[12,512]{1,0:T(8,128)S(1)}, f32[12,512,512]{1,2,0:T(8,128)}) fusion(f32[12,512,512]{1,2,0:T(8,128)} %copy-done.2, f32[12,512]{1,0:T(8,128)S(1)} %log_add_fusion, bf16[512,12,64]{0,2,1:T(8,128)(2,1)} %bitcast.116, bf16[512,12,64]{0,2,1:T(8,128)(2,1)} %bitcast.115), kind=kOutput, calls=%fused_computation.21 | convolution fusion | flops 412084224 | bytes 26787840 | tf_op jit(solution)/shard_map/while/body/eval_jaxpr/qhd,khd->hqk/dot_general | solution.py:177
  466.6 7.2 %multiply_convert_fusion = bf16[12,512,512]{1,2,0:T(8,128)(2,1)S(1)} fusion(f32[12,512,512]{1,2,0:T(8,128)} %get-tuple-element.80, f32[12,512,512]{1,2,0:T(8,128)S(1)} %bitcast.109, f32[12,512]{1,0:T(8,128)S(1)} %get-tuple-element.79, f32[12,512]{1,0:T(8,128)S(1)} %log_add_fusion), kind=kLoop, calls=%fused_computation.20 | loop fusion | flops 12582912 | bytes 31506432 | tf_op jit(solution)/shard_map/while/body/eval_jaxpr/convert_element_type | solution.py:182
  473.8 2.0 multiply_convert_fusion.2
  475.8 1.1 multiply_convert_fusion.3
  477.4 2.0 fusion.48
  479.4 0.9 copy-done.20
  480.3 5.2 fusion.54
  485.7 14.7 %copy.74 = bf16[12,512,512]{2,0,1:T(8,128)(2,1)} copy(bf16[12,512,512]{1,2,0:T(8,128)(2,1)} %copy-done.3) | data formatting | bytes 12582912 | tf_op jit(solution)/shard_map/while/body/eval_jaxpr/convert_element_type | solution.py:182
  500.5 6.0 fusion.37
  506.5 5.0 fusion.53
  511.5 44.0 %all-reduce.5 = (f32[768]{0:T(1024)S(1)}, f32[32,12]{0,1:T(8,128)}, f32[768]{0:T(1024)S(1)}, f32[768,16]{0,1:T(8,128)S(1)}) all-reduce(f32[768]{0:T(1024)S(1)} %get-tuple-element.53, f32[32,12]{0,1:T(8,128)S(1)} %fusion.53, f32[768]{0:T(1024)S(1)} %get-tuple-element.43, ...), channel_id=2, replica_groups=mesh['dp'=2,'expert'=16] {'dp','expert'}, use_global_device_ids=true, to_apply=%region_17.20.clone | all-reduce | flops 14208 | bytes 113664
  557.3 3.0 fusion.42
  560.3 4.5 convert_element_type.144
  564.8 4.5 convert_element_type.147
  569.3 111.2 %reduce-scatter.6.cloned.1.call-done = f32[24,2304]{1,0:T(8,128)} async-done(((f32[768,2304]{1,0:T(8,128)}), f32[24,2304]{1,0:T(8,128)}) %reduce-scatter.6.cloned.1.call-update) | async-done | bytes 221200 | tf_op jit(solution)/shard_map/reduce_scatter | solution.py:224
  (117 shorter events, 6.5 us)
Async XLA Ops:
  7.2 52.9 %copy-start = (f32[32,12]{0,1:T(8,128)S(1)}, f32[32,12]{0,1:T(8,128)}, u32[]{:S(2)}) copy-start(f32[32,12]{0,1:T(8,128)} %param.23) | copy-start | bytes 4612
  7.2 85.7 %all-gather.4.cloned.1.call-start = ((), (), s32[]{:S(2)}) async-start(), calls=%async_computation.9 | async-start | bytes 3649536 | tf_op jit(solution)/shard_map/all_gather | solution.py:40
  7.9 121.9 %all-gather.6.cloned.1.call-start = ((), (), s32[]{:S(2)}) async-start(), calls=%async_computation.10 | async-start | bytes 1216512 | tf_op jit(solution)/shard_map/all_gather | solution.py:41
  16.2 43.9 %copy-start.23 = (f32[512]{0:T(512)}, f32[512]{0:T(512)S(1)}, u32[]{:S(2)}) copy-start(f32[512]{0:T(512)S(1)} %fusion.43) | copy-start | bytes 6148
  75.0 17.9 %copy-start.12 = (bf16[512,768]{1,0:T(8,128)(2,1)S(1)}, bf16[512,768]{1,0:T(8,128)(2,1)}, u32[]{:S(2)}) copy-start(bf16[512,768]{1,0:T(8,128)(2,1)} %param.16) | copy-start | bytes 2359300
  97.7 6.7 copy-start.9
  98.0 8.3 %copy-start.7 = (bf16[512,768]{0,1:T(8,128)(2,1)}, bf16[512,768]{0,1:T(8,128)(2,1)S(1)}, u32[]{:S(2)}) copy-start(bf16[512,768]{0,1:T(8,128)(2,1)S(1)} %copy.62) | copy-start | bytes 2359300
  104.4 4.6 copy-start.2
  108.9 20.9 %copy-start.13 = (bf16[512,768]{1,0:T(8,128)(2,1)S(1)}, bf16[512,768]{1,0:T(8,128)(2,1)}, u32[]{:S(2)}) copy-start(bf16[512,768]{1,0:T(8,128)(2,1)} %param.16) | copy-start | bytes 2359300
  111.0 21.0 %copy-start.11 = (bf16[12,64,512]{2,1,0:T(8,128)(2,1)}, bf16[12,64,512]{2,1,0:T(8,128)(2,1)S(1)}, u32[]{:S(2)}) copy-start(bf16[12,64,512]{2,1,0:T(8,128)(2,1)S(1)} %fusion.45) | copy-start | bytes 2359300
  132.0 1.1 copy-start.4
  137.6 55.1 %slice-start.3 = ((s8[4718592]{0:T(1024)(128)(4,1)}), s8[4194304]{0:T(1024)(128)(4,1)S(1)}, s32[]{:S(2)}) async-start(s8[4718592]{0:T(1024)(128)(4,1)} %bitcast.139), calls=%async_computation.18 | async-start | bytes 8388608
  180.2 1.1 copy-start.17
  181.3 11.4 %slice-start.4 = ((s8[4718592]{0:T(1024)(128)(4,1)}), s8[524288]{0:T(1024)(128)(4,1)S(1)}, s32[]{:S(2)}) async-start(s8[4718592]{0:T(1024)(128)(4,1)} %bitcast.139), calls=%async_computation.19 | async-start | bytes 1048576
  188.3 4.5 copy-start.28
  192.7 13.3 %copy-start.25 = (bf16[24,16]{0,1:T(8,128)(2,1)S(1)}, bf16[24,16]{0,1:T(8,128)(2,1)}, u32[]{:S(2)}) copy-start(bf16[24,16]{0,1:T(8,128)(2,1)} %param.25) | copy-start | bytes 2308
  192.8 101.3 %copy-start.22 = (s32[512,1]{0,1:T(1,128)S(1)}, s32[512,1]{0,1:T(1,128)}, u32[]{:S(2)}) copy-start(s32[512,1]{0,1:T(1,128)} %param.18) | copy-start | bytes 6148
  201.3 93.2 %all-to-all-start.1 = ((bf16[16,64,768]{2,1,0:T(8,128)(2,1)}), bf16[16,64,768]{2,1,0:T(8,128)(2,1)S(1)}, u32[]{:S(2)}, u32[]{:S(2)}) async-start(bf16[16,64,768]{2,1,0:T(8,128)(2,1)} %fusion.29), calls=%async_computation.1 | async-start | bytes 3145728 | tf_op jit(solution)/shard_map/all_to_all | solution.py:122
  294.5 17.0 %all-to-all-start.3 = ((s32[16,1,1]{2,1,0:T(1,128)}), s32[16,1,1]{2,1,0:T(1,128)S(1)}, u32[]{:S(2)}, u32[]{:S(2)}) async-start(s32[16,1,1]{2,1,0:T(1,128)} %copy.69), calls=%async_computation.3 | async-start | bytes 16384 | tf_op jit(solution)/shard_map/all_to_all | solution.py:103
  311.5 40.6 %all-to-all-start.2 = ((bf16[16,64,768]{2,1,0:T(8,128)(2,1)}), bf16[16,64,768]{2,1,0:T(8,128)(2,1)}, u32[]{:S(2)}, u32[]{:S(2)}) async-start(bf16[16,64,768]{2,1,0:T(8,128)(2,1)} %bitcast.19), calls=%async_computation.2 | async-start | bytes 3145728 | tf_op jit(solution)/shard_map/all_to_all | solution.py:123
  318.6 241.7 %reduce-scatter.10.cloned.1.call-start = ((), (), s32[]{:S(2)}) async-start(), calls=%async_computation.13 | async-start | bytes 7077888 | tf_op jit(solution)/shard_map/reduce_scatter | solution.py:146
  319.1 51.0 %copy-start.18 = (bf16[16,64,768]{2,1,0:T(8,128)(2,1)S(1)}, bf16[16,64,768]{2,1,0:T(8,128)(2,1)}, u32[]{:S(2)}) copy-start(bf16[16,64,768]{2,1,0:T(8,128)(2,1)} %copy-done.17) | copy-start | bytes 4718596
  367.4 2.7 copy-start.27
  377.0 187.9 %reduce-scatter.12.cloned.1.call-start = ((), (), s32[]{:S(2)}) async-start(), calls=%async_computation.14 | async-start | bytes 7077888 | tf_op jit(solution)/shard_map/reduce_scatter | solution.py:149
  398.2 40.5 %all-to-all-start.4 = ((bf16[16,64,768]{2,1,0:T(8,128)(2,1)}), bf16[16,64,768]{2,1,0:T(8,128)(2,1)S(1)}, u32[]{:S(2)}, u32[]{:S(2)}) async-start(bf16[16,64,768]{2,1,0:T(8,128)(2,1)} %fusion.26), calls=%async_computation.4 | async-start | bytes 3145728 | tf_op jit(solution)/shard_map/all_to_all | solution.py:140
  405.2 164.2 %reduce-scatter.8.cloned.1.call-start = ((), (), s32[]{:S(2)}) async-start(), calls=%async_computation.12 | async-start | bytes 2433024 | tf_op jit(solution)/shard_map/reduce_scatter | solution.py:225
  441.4 2.6 copy-start.5
  441.4 5.5 copy-start.26
  454.3 226.2 %reduce-scatter.6.cloned.1.call-start = ((), (), s32[]{:S(2)}) async-start(), calls=%async_computation.11 | async-start | bytes 7299072 | tf_op jit(solution)/shard_map/reduce_scatter | solution.py:224
  454.4 12.2 %slice-start = ((s8[12582912]{0:T(1024)(128)(4,1)}), s8[4194304]{0:T(1024)(128)(4,1)S(1)}, s32[]{:S(2)}) async-start(s8[12582912]{0:T(1024)(128)(4,1)} %bitcast.108), calls=%async_computation.15 | async-start | bytes 8388608
  454.4 12.2 %slice-start.1 = ((s8[12582912]{0:T(1024)(128)(4,1)}), s8[4194304]{0:T(1024)(128)(4,1)S(1)}, s32[]{:S(2)}) async-start(s8[12582912]{0:T(1024)(128)(4,1)} %bitcast.108), calls=%async_computation.16 | async-start | bytes 8388608
  454.4 12.1 %slice-start.2 = ((s8[12582912]{0:T(1024)(128)(4,1)}), s8[4194304]{0:T(1024)(128)(4,1)S(1)}, s32[]{:S(2)}) async-start(s8[12582912]{0:T(1024)(128)(4,1)} %bitcast.108), calls=%async_computation.17 | async-start | bytes 8388608
  466.5 7.2 %copy-start.10 = (bf16[512,768]{0,1:T(8,128)(2,1)S(1)}, bf16[512,768]{0,1:T(8,128)(2,1)}, u32[]{:S(2)}) copy-start(bf16[512,768]{0,1:T(8,128)(2,1)} %copy-done.9) | copy-start | bytes 2359300
  473.8 3.2 copy-start.3
  475.8 3.6 copy-start.21
  475.8 1.6 copy-start.8
  477.4 2.1 copy-start.15
  477.4 2.9 copy-start.14
  479.4 0.9 copy-start.20
  485.7 14.8 %copy-start.16 = (bf16[12,64,512]{2,1,0:T(8,128)(2,1)S(1)}, bf16[12,64,512]{2,1,0:T(8,128)(2,1)}, u32[]{:S(2)}) copy-start(bf16[12,64,512]{2,1,0:T(8,128)(2,1)} %copy-done.15) | copy-start | bytes 2359300
  500.5 6.0 copy-start.6
  500.5 6.0 copy-start.19
  506.5 50.8 %copy-start.24 = (f32[512]{0:T(512)S(1)}, f32[512]{0:T(512)}, u32[]{:S(2)}) copy-start(f32[512]{0:T(512)} %copy-done.23) | copy-start | bytes 6148
  560.3 120.2 %copy-start.1 = (f32[32,12]{0,1:T(8,128)S(1)}, f32[32,12]{0,1:T(8,128)}, u32[]{:S(2)}) copy-start(f32[32,12]{0,1:T(8,128)} %param.23) | copy-start | bytes 4612
Sparse Core Ops, SparseCore 0:
  10.9 62.9 all-gather.3
  76.8 52.9 all-gather.5
  377.1 14.2 reduce-scatter.9
  393.7 13.7 reduce-scatter.11
  454.4 100.8 reduce-scatter.7
  562.4 118.1 reduce-scatter.5
where the time goes:
time: 697 us; the launch traced here: 688 us
  blocking collectives  217 us (31%)
  waiting for transfers between devices  198 us (28%)
  matrix products  130 us (19%)
  local copies, waits for them, and re-layouts  71.1 us (10%)
  other arithmetic  34.6 us (5%)
  starting transfers between devices  22.5 us (3%)
  between operations  15.1 us (2%)
    reduce_scatter x1, waiting for transfers between devices, shards(): lax.psum_scatter(qkv_weight_grad, ('dp', 'expert'), scatter_dimension=0,...  111 us
    all_gather x1, blocking collectives, shards(): lax.all_gather(w_router, ('dp', 'expert'), axis=0, tiled=True)  87.9 us
    unnamed x2, blocking collectives  86.1 us
    all_to_all x1, blocking collectives, shards(): lax.all_to_all(outgoing, 'expert', split_axis=0, concat_axis=0, tiled=True)  42.6 us
    all_to_all x1, waiting for transfers between devices, shards(): lax.all_to_all(row_back, 'expert', split_axis=0, concat_axis=0, tiled=True)  33.4 us
    all_to_all x1, waiting for transfers between devices, shards(): lax.all_to_all(grad_slots, 'expert', split_axis=0, concat_axis=0, tiled=T...  33.1 us
    all_gather x1, waiting for transfers between devices, shards(): lax.all_gather(w_att, ('dp', 'expert'), axis=0, tiled=True)  18.8 us
    dot_general x1, local copies, waits for them, and re-layouts, shards(): jnp.einsum('bij,bh->hij', (buckets[None, :, :] == kinds[:, None, None]).a...  17.9 us
  transfers between devices with their start and end apart: 10, of which 4 were waited for; matrix products, arithmetic and copies ran while one was open for 26% of the time, Pallas kernels for 0%

commit v1 on v0

v1 whole, which is shorter than its diff:
```python
import functools
import jax
import jax.numpy as jnp
from jax import lax
from jax.experimental import pallas as pl
from jax.experimental.pallas import tpu as pltpu
from jax.sharding import PartitionSpec as P

MESH = pl.DeviceIdType.MESH
F32, BF16 = jnp.float32, jnp.bfloat16
NT = (((1,), (1,)), ((), ()))


def dot(a, b, dims=(((1,), (0,)), ((), ()))):
    return lax.dot_general(a, b, dims, preferred_element_type=F32)


def flipped(index, bits, count):
    result, bit = 0, 1
    while bit < count:
        result = result + bit * (((index // bit) % 2 + (bits // bit) % 2) % 2)
        bit *= 2
    return result


def gelu_parts(hidden):
    c0, c1 = 0.7978845608028654, 0.044715
    square = hidden * hidden
    bend = jnp.tanh(hidden * (c0 + (c0 * c1) * square))
    half = 0.5 + 0.5 * bend
    slope = half + (0.5 * hidden) * (1.0 - bend * bend) * (c0 + (3.0 * c0 * c1) * square)
    return hidden * half, slope


def moe_kernel(
    n, cap, pad, experts,
    rows_ref, cots_ref, router_ref, win_hbm, wout_hbm,
    back_ret, prod_ret, gin_ref, gout_ref,
    win, wout, xin, cin, xt, rt, act, hgr, backs, prods, acc1, acc2,
    sib_send, sib_recv, stage,
    wsem, send_sem, recv_sem, ret_send, ret_recv, own_sem, sib_ss, sib_rs, out_sem,
):
    dp, me = lax.axis_index("dp"), lax.axis_index("expert")
    width, ff = win.shape
    per = 256 // cap
    groups = n // per
    rows = per * cap
    chunk = 512
    load_in = pltpu.make_async_copy(win_hbm, win, wsem.at[0])
    load_out = pltpu.make_async_copy(wout_hbm, wout, wsem.at[1])
    load_in.start()
    load_out.start()
    barrier = pltpu.get_barrier_semaphore()

    def greet(p, _):
        pl.semaphore_signal(barrier, inc=1, device_id=(dp, flipped(me, p, n)), device_id_type=MESH)
        return 0

    lax.fori_loop(1, n, greet, 0)
    pl.semaphore_signal(barrier, inc=1, device_id=(1 - dp, me), device_id_type=MESH)
    pl.semaphore_wait(barrier, n)

    def send(kind, p):
        src, dst = ((rows_ref, xin), (cots_ref, cin))[kind]
        return pltpu.make_async_remote_copy(
            src_ref=src.at[p], dst_ref=dst.at[p],
            send_sem=send_sem.at[kind, p], recv_sem=recv_sem.at[kind, p],
            device_id=(dp, flipped(me, p, n)), device_id_type=MESH,
        )

    def give(kind, p):
        src, dst = ((backs, back_ret), (prods, prod_ret))[kind]
        return pltpu.make_async_remote_copy(
            src_ref=src.at[p], dst_ref=dst.at[p],
            send_sem=ret_send.at[kind, p], recv_sem=ret_recv.at[kind, p],
            device_id=(dp, flipped(me, p, n)), device_id_type=MESH,
        )

    for kind in (0, 1):
        def start(i, _):
            send(kind, n - i).start()
            return 0
        lax.fori_loop(1, n, start, 0)
    xin[0] = rows_ref[0]
    cin[0] = cots_ref[0]
    load_in.wait()
    load_out.wait()

    def packed_rows(ref, g):
        block = ref[pl.ds(g * per, per)].reshape(per * pad, width)
        if pad == cap:
            return block
        r = lax.broadcasted_iota(jnp.int32, (rows, per * pad), 0)
        c = lax.broadcasted_iota(jnp.int32, (rows, per * pad), 1)
        return dot(((r // cap) * pad + r % cap == c).astype(BF16), block).astype(BF16)

    def spread_rows(block):
        if pad == cap:
            return block
        r = lax.broadcasted_iota(jnp.int32, (per * pad, rows), 0)
        c = lax.broadcasted_iota(jnp.int32, (per * pad, rows), 1)
        pick = (r // pad == c // cap) & (r % pad == c % cap)
        return dot(pick.astype(BF16), block).astype(BF16)

    def group(g, _):
        for kind in (0, 1):
            def arrive(j, _):
                p = g * per + j
                @pl.when(p != 0)
                def _():
                    send(kind, p).wait_recv()
                return 0
            lax.fori_loop(0, per, arrive, 0)
        here = pl.ds(pl.multiple_of(g * rows, rows), rows)
        x = packed_rows(xin, g)
        logits = dot(x, router_ref[...])
        lane = lax.broadcasted_iota(jnp.int32, logits.shape, 1)
        logits = jnp.where(lane < experts, logits, -1e30)
        chance = jnp.exp(logits - jnp.max(logits, axis=1, keepdims=True))
        gate = jnp.sum(jnp.where(lane == me, chance, 0.0), axis=1, keepdims=True) / jnp.sum(
            chance, axis=1, keepdims=True)
        r = (gate * packed_rows(cin, g).astype(F32)).astype(BF16)
        xt[:, here] = x.T
        rt[:, here] = r.T
        acc1[...] = jnp.zeros_like(acc1)
        acc2[...] = jnp.zeros_like(acc2)

        def hidden_chunk(k, _):
            cols = pl.ds(pl.multiple_of(k * chunk, chunk), chunk)
            hidden = dot(x, win[:, cols])
            value, slope = gelu_parts(hidden)
            value = value.astype(BF16)
            act[here, cols] = value
            hg = (dot(r, wout[:, cols]) * slope).astype(BF16)
            hgr[here, cols] = hg
            acc1[...] += dot(hg, win[:, cols], NT)
            acc2[...] += dot(value, wout[:, cols], NT)
            return 0

        lax.fori_loop(0, ff // chunk, hidden_chunk, 0)
        backs[pl.ds(g * per, per)] = spread_rows(acc1[...].astype(BF16)).reshape(per, pad, width)
        prods[pl.ds(g * per, per)] = spread_rows(acc2[...].astype(BF16)).reshape(per, pad, width)
        for kind in (0, 1):
            def leave(j, _):
                p = g * per + j
                @pl.when(p != 0)
                def _():
                    give(kind, p).start()
                return 0
            lax.fori_loop(0, per, leave, 0)
        return 0

    lax.fori_loop(0, groups, group, 0)
    own_back = pltpu.make_async_copy(backs.at[0], back_ret.at[0], own_sem.at[0])
    own_prod = pltpu.make_async_copy(prods.at[0], prod_ret.at[0], own_sem.at[1])
    own_back.start()
    own_prod.start()

    half = ff // 2
    part = sib_send.shape[3]
    steps = half // part

    def sibling(kind, k):
        return pltpu.make_async_remote_copy(
            src_ref=sib_send.at[kind, k], dst_ref=sib_recv.at[kind, k],
            send_sem=sib_ss.at[kind, k], recv_sem=sib_rs.at[kind, k],
            device_id=(1 - dp, me), device_id_type=MESH,
        )

    def partial(kind, owner, k):
        cols = pl.ds(pl.multiple_of(owner * half + k * part, 128), part)
        return dot(xt[...], hgr[:, cols]) if kind == 0 else dot(rt[...], act[:, cols])

    def theirs(k, _):
        for kind in (0, 1):
            sib_send[kind, k] = partial(kind, 1 - dp, k).astype(BF16)
            sibling(kind, k).start()
        return 0

    lax.fori_loop(0, steps, theirs, 0)

    def out_copy(kind, k):
        cols = pl.ds(pl.multiple_of(k * part, 128), part)
        return pltpu.make_async_copy(
            stage.at[kind, k % 2], (gin_ref, gout_ref)[kind].at[:, cols], out_sem.at[kind, k % 2])

    def ours(k, _):
        for kind in (0, 1):
            value = partial(kind, dp, k)
            sibling(kind, k).wait_recv()
            @pl.when(k >= 2)
            def _():
                out_copy(kind, k - 2).wait()
            stage[kind, k % 2] = value + sib_recv[kind, k].astype(F32)
            out_copy(kind, k).start()
        return 0

    lax.fori_loop(0, steps, ours, 0)
    for kind in (0, 1):
        for k in (steps - 2, steps - 1):
            out_copy(kind, k).wait()

    def settle(p, _):
        for kind in (0, 1):
            give(kind, p).wait_recv()
            send(kind, p).wait_send()
            give(kind, p).wait_send()
        return 0

    lax.fori_loop(1, n, settle, 0)

    def settle_sibling(k, _):
        for kind in (0, 1):
            sibling(kind, k).wait_send()
        return 0

    lax.fori_loop(0, steps, settle_sibling, 0)
    own_back.wait()
    own_prod.wait()


def moe(n, cap, pad, experts, rows, cots, router, win, wout):
    width, ff = win.shape
    total = n * cap
    part = 256
    steps = ff // 2 // part
    any_ = pl.BlockSpec(memory_space=pl.ANY)
    vmem = pl.BlockSpec(memory_space=pltpu.VMEM)
    dma = pltpu.SemaphoreType.DMA
    per = 256 // cap
    return pl.pallas_call(
        functools.partial(moe_kernel, n, cap, pad, experts),
        out_shape=(
            jax.ShapeDtypeStruct((n, pad, width), BF16),
            jax.ShapeDtypeStruct((n, pad, width), BF16),
            jax.ShapeDtypeStruct((width, ff // 2), F32),
            jax.ShapeDtypeStruct((width, ff // 2), F32),
        ),
        in_specs=[vmem, vmem, vmem, any_, any_],
        out_specs=(any_, any_, any_, any_),
        scratch_shapes=[
            pltpu.VMEM((width, ff), BF16),
            pltpu.VMEM((width, ff), BF16),
            pltpu.VMEM((n, pad, width), BF16),
            pltpu.VMEM((n, pad, width), BF16),
            pltpu.VMEM((width, total), BF16),
            pltpu.VMEM((width, total), BF16),
            pltpu.VMEM((total, ff), BF16),
            pltpu.VMEM((total, ff), BF16),
            pltpu.VMEM((n, pad, width), BF16),
            pltpu.VMEM((n, pad, width), BF16),
            pltpu.VMEM((per * cap, width), F32),
            pltpu.VMEM((per * cap, width), F32),
            pltpu.VMEM((2, steps, width, part), BF16),
            pltpu.VMEM((2, steps, width, part), BF16),
            pltpu.VMEM((2, 2, width, part), F32),
            dma((2,)), dma((2, n)), dma((2, n)), dma((2, n)), dma((2, n)), dma((2,)),
            dma((2, steps)), dma((2, steps)), dma((2, 2)),
        ],
        compiler_params=pltpu.CompilerParams(
            collective_id=2, has_side_effects=True, vmem_limit_bytes=60 * 1024 * 1024),
        cost_estimate=pl.CostEstimate(
            flops=12 * total * width * ff, bytes_accessed=8 * width * ff, transcendentals=total * ff),
        name="experts",
    )(rows, cots, router, win, wout)


EPSILON = 1e-06
PRECISE = lax.Precision.HIGHEST


def rms_scale(values, gains):
    return values * lax.rsqrt(jnp.mean(values * values, axis=-1, keepdims=True) + EPSILON) * gains


def split_heads(packed, width, heads):
    rows_here = packed.shape[0]
    head_dim = width // heads
    return (
        packed[:, :width].reshape(rows_here, heads, head_dim),
        packed[:, width : 2 * width].reshape(rows_here, heads, head_dim),
        packed[:, 2 * width :].reshape(rows_here, heads, head_dim),
    )


def shards(
    n, tokens, cotangent, routes, buckets, gain_attn, w_qkv, w_att, rel_bias, gain_moe, w_router, w_in, w_out,
):
    axes = ("dp", "expert")
    tok_count, width = tokens.shape
    experts = w_router.shape[1]
    bundle = jnp.concatenate([w_qkv, w_att, w_router, gain_attn[:, None], gain_moe[:, None]], axis=1)
    bundle = lax.all_gather(bundle, axes, axis=0, tiled=True)
    full_qkv = bundle[:, : 3 * width]
    full_att = bundle[:, 3 * width : 4 * width]
    full_router = bundle[:, 4 * width : 4 * width + experts]
    full_gain_attn = bundle[:, 4 * width + experts]
    full_gain_moe = bundle[:, 4 * width + experts + 1]
    seq_len = buckets.shape[0]
    heads = rel_bias.shape[1]
    score_scale = (width // heads) ** (-0.5)
    cap = max(2, 2 * tok_count // experts)
    pad = max(16, cap)
    kinds = jnp.arange(rel_bias.shape[0], dtype=jnp.int32)
    bucket_hits = (buckets[None, :, :] == kinds[:, None, None]).astype(jnp.bfloat16)
    bias_table = jnp.einsum(
        "bij,bh->hij", (buckets[None, :, :] == kinds[:, None, None]).astype(jnp.float32), rel_bias,
        precision=PRECISE,
    )
    inputs = tokens.astype(jnp.float32)
    normed_f, attn_norm_pull = jax.vjp(rms_scale, inputs, full_gain_attn.astype(jnp.float32))
    normed = normed_f.astype(jnp.bfloat16)
    packed = jnp.dot(normed, full_qkv, preferred_element_type=jnp.float32).astype(jnp.bfloat16)

    query_rows, key_rows, value_rows = split_heads(packed, width, heads)
    scores = jnp.einsum("qhd,khd->hqk", query_rows, key_rows, preferred_element_type=jnp.float32) * score_scale + bias_table
    log_total = jax.nn.logsumexp(scores, axis=-1, keepdims=True)
    weights = jnp.exp(scores - log_total).astype(jnp.bfloat16)
    attended = jnp.einsum("hqk,khd->qhd", weights, value_rows, preferred_element_type=jnp.float32).reshape(seq_len, width).astype(jnp.bfloat16)

    middle = inputs + jnp.dot(attended, full_att, preferred_element_type=jnp.float32)
    moe_f, moe_norm_pull = jax.vjp(rms_scale, middle, full_gain_moe.astype(jnp.float32))
    moe_in = moe_f.astype(jnp.bfloat16)
    logits = jnp.dot(moe_in, full_router, preferred_element_type=jnp.float32)
    router_prob = jax.nn.softmax(logits, axis=-1)
    chosen = routes[:, 0]
    me = lax.axis_index("expert")
    picked = (chosen[:, None] == jnp.arange(experts, dtype=jnp.int32)[None, :]).astype(jnp.int32)
    gate_value = jnp.sum(router_prob * picked, axis=-1)
    ranks = jnp.sum((jnp.cumsum(picked, axis=0, dtype=jnp.int32) - 1) * picked, axis=1, dtype=jnp.int32)
    slot = jnp.bitwise_xor(chosen, me) * pad + ranks
    hits = (slot[None, :] == jnp.arange(n * pad, dtype=jnp.int32)[:, None]).astype(jnp.bfloat16)

    def to_slots(rows):
        return jnp.dot(hits, rows, preferred_element_type=jnp.float32).astype(jnp.bfloat16).reshape(n, pad, width)

    def from_slots(rows):
        return jnp.dot(hits.T, rows.reshape(n * pad, width), preferred_element_type=jnp.float32)

    upstream = cotangent.astype(jnp.float32)
    router_wide = jnp.pad(full_router, ((0, 0), (0, -experts % 128)))
    came_back, returned, grad_in, grad_out = moe(
        n, cap, pad, experts, to_slots(moe_in), to_slots(cotangent), router_wide, w_in[0], w_out[0])
    expert_back = from_slots(returned)
    mixed = (middle + gate_value[:, None] * expert_back).astype(jnp.bfloat16)
    gate_grad = jnp.sum(upstream * expert_back, axis=-1)
    logit_grad = ((gate_value * gate_grad)[:, None] * (picked - router_prob)).astype(jnp.bfloat16)
    router_grad = jnp.einsum("td,te->de", moe_in, logit_grad, preferred_element_type=jnp.float32)
    moe_in_grad = from_slots(came_back)
    moe_in_grad = moe_in_grad + jnp.einsum("te,de->td", logit_grad, full_router, preferred_element_type=jnp.float32)
    middle_norm_grad, gain_moe_grad = moe_norm_pull(moe_in_grad)
    middle_grad = upstream + middle_norm_grad
    attn_grad = middle_grad.astype(jnp.bfloat16)
    att_weight_grad = jnp.einsum("td,te->de", attended, attn_grad, preferred_element_type=jnp.float32)
    attended_grad = jnp.einsum("te,de->td", attn_grad, full_att, preferred_element_type=jnp.float32).astype(jnp.bfloat16)

    grad_heads = attended_grad.reshape(seq_len, heads, width // heads)
    chance = jnp.exp(scores - log_total)
    weight_grad = jnp.einsum("qhd,khd->hqk", grad_heads, value_rows, preferred_element_type=jnp.float32)
    score_grad = (chance * (weight_grad - jnp.sum(chance * weight_grad, axis=-1, keepdims=True))).astype(jnp.bfloat16)
    query_grad = jnp.einsum("hqk,khd->qhd", score_grad, key_rows, preferred_element_type=jnp.float32) * score_scale
    key_grad = jnp.einsum("hqk,qhd->khd", score_grad, query_rows, preferred_element_type=jnp.float32) * score_scale
    value_grad = jnp.einsum("hqk,qhd->khd", weights, grad_heads, preferred_element_type=jnp.float32)
    packed_grad = jnp.concatenate(
        [g.reshape(seq_len, width) for g in (query_grad, key_grad, value_grad)], axis=1).astype(jnp.bfloat16)
    bias_grad = jnp.einsum("hij,bij->bh", score_grad, bucket_hits, preferred_element_type=jnp.float32)
    qkv_weight_grad = jnp.einsum("td,te->de", normed, packed_grad, preferred_element_type=jnp.float32)
    normed_grad = jnp.einsum("te,de->td", packed_grad, full_qkv, preferred_element_type=jnp.float32)
    input_norm_grad, gain_attn_grad = attn_norm_pull(normed_grad)
    grad_tokens = middle_grad + input_norm_grad
    wide = jnp.concatenate(
        [qkv_weight_grad, att_weight_grad, router_grad, gain_attn_grad[:, None], gain_moe_grad[:, None]], axis=1)
    wide = lax.psum_scatter(wide, axes, scatter_dimension=0, tiled=True)
    grad_bias = lax.psum(bias_grad, axes)
    return (
        mixed, grad_tokens, wide[:, 4 * width + experts], wide[:, : 3 * width], wide[:, 3 * width : 4 * width],
        grad_bias, wide[:, 4 * width + experts + 1], wide[:, 4 * width : 4 * width + experts],
        grad_in[None], grad_out[None],
    )


def solution(mesh):
    both = P(("dp", "expert"))
    return jax.shard_map(
        functools.partial(shards, mesh.shape["expert"]),
        mesh=mesh,
        in_specs=(both, both, both, P(), both, both, both, P(), both, both, P("expert"), P("expert")),
        out_specs=(both, both, both, both, both, P(), both, both, P("expert", None, "dp"), P("expert", None, "dp")),
        check_vma=False,
    )
```

time: 697 us -> 541 us (0.78)
  blocking collectives: 217 us -> 54.9 us
  Pallas kernels: 0 us -> 133 us
  matrix products: 130 us -> 81.1 us
  waiting for transfers between devices: 198 us -> 161 us
  starting transfers between devices: 22.5 us -> 0.08 us
  other arithmetic: 34.6 us -> 18.3 us
    pallas_call x0 -> x1, Pallas kernels: none -> 133 us  [moe(): pl.pallas_call(functools.partial(moe_kernel, n, cap, pad, experts), out_s...]
    unnamed x6 -> x3, waiting for transfers between devices: 1.44 us -> 129 us
    reduce_scatter x4 -> x0, waiting for transfers between devices: 111 us -> none  [the longest x1 111 us: shards(): lax.psum_scatter(qkv_weight_grad, ('dp', 'expert'), scatter_dimension=0,...]
    all_gather x1 -> x0, blocking collectives: 87.9 us -> none  [shards(): lax.all_gather(w_router, ('dp', 'expert'), axis=0, tiled=True)]
    unnamed x2 -> x0, blocking collectives: 86.1 us -> none
    all_to_all x4 -> x0, waiting for transfers between devices: 66.5 us -> none  [the longest x1 33.4 us: shards(): lax.all_to_all(row_back, 'expert', split_axis=0, concat_axis=0, tiled=True)]
    psum x0 -> x1, blocking collectives: none -> 54.9 us  [shards(): grad_bias = lax.psum(bias_grad, axes)]
    dot_general x15 -> x13, matrix products: 101 us -> 52.1 us  [the longest x1 8.87 us: shards(): jnp.einsum('qhd,khd->hqk', grad_heads, value_rows, preferred_element_type...]
  transfers between devices with their start and end apart: 10 -> 2, of which waited for: 4 -> 2; matrix products, arithmetic and copies ran while one was open for 26% -> 11% of each run, Pallas kernels for 0% -> 0%
where the time goes in v1:
time: 541 us; the launch traced here: 532 us
  waiting for transfers between devices  161 us (30%)
  Pallas kernels  133 us (25%)
  matrix products  81.1 us (15%)
  local copies, waits for them, and re-layouts  68.3 us (13%)
  blocking collectives  54.9 us (10%)
  other arithmetic  18.3 us (3%)
  between operations  14.9 us (3%)
    pallas_call x1, Pallas kernels, moe(): pl.pallas_call(functools.partial(moe_kernel, n, cap, pad, experts), out_s...  133 us
    unnamed x3, waiting for transfers between devices  129 us
    psum x1, blocking collectives, shards(): grad_bias = lax.psum(bias_grad, axes)  54.9 us
    all_gather x1, waiting for transfers between devices, shards(): bundle = lax.all_gather(bundle, axes, axis=0, tiled=True)  31.3 us
    dot_general x1, local copies, waits for them, and re-layouts, shards(): jnp.einsum('bij,bh->hij', (buckets[None, :, :] == kinds[:, None, None]).a...  17.3 us
    dot_general x1, matrix products, shards(): jnp.einsum('bij,bh->hij', (buckets[None, :, :] == kinds[:, None, None]).a...  14.8 us
    convert_element_type x1, local copies, waits for them, and re-layouts, shards(): (chance * (weight_grad - jnp.sum(chance * weight_grad, axis=-1, keepdims=...  14.4 us
    unnamed x60, local copies, waits for them, and re-layouts  12 us
  transfers between devices with their start and end apart: 2, of which 2 were waited for; matrix products, arithmetic and copies ran while one was open for 11% of the time, Pallas kernels for 0%

profile of v1, /device:TPU:0, one launch (start us, length us, event | category | flops | bytes accessed | tf_op | source)
XLA Modules:
  0.0 531.8 jit_solution(829459612820724802)
XLA Ops:
  7.2 0.0 copy-start
  7.2 0.0 all-gather.2.cloned.1.call-start
  7.2 0.8 copy.62
  8.0 0.7 copy.63
  8.8 0.7 copy.64
  9.5 1.6 concatenate.10
  11.1 0.0 all-gather.2.cloned.1.call-update
  11.2 0.0 all-reduce.4.cloned.1.call-start
  11.2 14.8 %fusion.1 = f32[512,512,12]{1,2,0:T(8,128)} fusion(s32[512,512]{1,0:T(8,128)} %param.15, f32[32,12]{0,1:T(8,128)S(1)} %copy-done), kind=kOutput, calls=%fused_computation.2 | convolution fusion | flops 1216348160 | bytes 13633024 | tf_op jit(solution)/shard_map/bij,bh->hij/dot_general | solution.py:306
  26.1 17.3 %copy.68 = f32[512,512,12]{0,1,2:T(8,128)} copy(f32[512,512,12]{1,2,0:T(8,128)} %fusion.1) | data formatting | bytes 25165824 | tf_op jit(solution)/shard_map/bij,bh->hij/dot_general | solution.py:306
  43.4 1.2 reduce-window.6
  44.5 0.2 slice_reduce_fusion
  44.8 0.1 fusion.47
  44.9 0.2 fusion.24
  45.1 2.2 fusion.15
  47.3 31.3 %all-gather.2.cloned.1.call-done = bf16[768,3090]{1,0:T(8,128)(2,1)} async-done(((bf16[24,3090]{1,0:T(8,128)(2,1)}), bf16[768,3090]{1,0:T(8,128)(2,1)}) %all-gather.2.cloned.1.call-update) | async-done | bytes 4746256 | tf_op jit(solution)/shard_map/all_gather | solution.py:293
  78.6 1.3 convert_reduce_fusion
  79.9 4.1 convolution_convert_fusion
  84.0 0.2 fusion.61
  84.2 0.3 copy.65
  84.5 0.3 copy.66
  84.8 0.3 copy.67
  85.0 6.0 %fusion.62 = (f32[12,512]{1,0:T(8,128)S(1)}, f32[12,512,512]{1,2,0:T(8,128)S(1)}) fusion(f32[512,512,12]{0,1,2:T(8,128)} %copy.68, bf16[512,12,64]{0,2,1:T(8,128)(2,1)S(1)} %bitcast.77, bf16[512,12,64]{0,2,1:T(8,128)(2,1)S(1)} %bitcast.71), kind=kOutput, calls=%fused_computation.100 | convolution fusion | flops 412084224 | bytes 26763264 | tf_op jit(solution)/shard_map/qhd,khd->hqk/dot_general | solution.py:316
  91.1 1.9 exponential_reduce_fusion
  93.0 2.7 copy-done.2
  95.7 2.1 fusion.27
  97.8 2.5 multiply_reduce_fusion.3
  100.3 0.2 multiply_convert_fusion.3
  100.5 2.2 fusion.14
  102.7 1.3 fusion.63
  104.0 0.7 pad.4.router_ref
  104.7 133.4 %experts.1 = (bf16[16,64,768]{2,1,0:T(8,128)(2,1)}, bf16[16,64,768]{2,1,0:T(8,128)(2,1)}, f32[768,1536]{1,0:T(8,128)}, f32[768,1536]{1,0:T(8,128)}) custom-call(bf16[16,64,768]{2,1,0:T(8,128)(2,1)} %bitcast.107, bf16[16,64,768]{2,1,0:T(8,128)(2,1)} %bitcast.105, bf16[768,128]{1,0:T(8,128)(2,1)} %pad.4.router_ref, bf16[768,3072]{1,0:T(8,128)(2,1)} %bitcast.103, ...), custom_call_target="tpu_custom_call" | custom-call | flops 28991029248 | bytes 18874368 | tf_op jit(solution)/shard_map/experts/pallas_call | solution.py:231
  238.2 3.0 fusion.22
  241.2 1.4 fusion.57
  242.6 1.6 multiply_reduce_fusion.1
  244.2 3.0 convert_add_fusion.1
  247.2 1.7 convolution_convert_fusion.1
  248.9 2.3 copy.71
  251.2 7.0 %fusion.30 = bf16[12,64,512]{2,1,0:T(8,128)(2,1)S(1)} fusion(bf16[512,12,64]{0,2,1:T(8,128)(2,1)} %bitcast.75, f32[12,512,512]{1,2,0:T(8,128)} %copy-done.2, f32[12,512]{1,0:T(8,128)S(1)} %log_add_fusion), kind=kOutput, calls=%fused_computation.52 | convolution fusion | flops 409337856 | bytes 14180352 | tf_op jit(solution)/shard_map/hqk,qhd->khd/dot_general | solution.py:363
  258.2 8.9 %multiply_reduce_fusion = (f32[12,512]{1,0:T(8,128)S(1)}, f32[12,512,512]{1,2,0:T(8,128)}) fusion(f32[12,512,512]{1,2,0:T(8,128)} %copy-done.2, f32[12,512]{1,0:T(8,128)S(1)} %log_add_fusion, bf16[512,12,64]{0,2,1:T(8,128)(2,1)S(1)} %bitcast.76, bf16[512,12,64]{0,2,1:T(8,128)(2,1)S(1)} %bitcast.74), kind=kOutput, calls=%fused_computation.7 | convolution fusion | flops 412084224 | bytes 26787840 | tf_op jit(solution)/shard_map/qhd,khd->hqk/dot_general | solution.py:359
  267.1 7.2 %multiply_convert_fusion = bf16[12,512,512]{1,2,0:T(8,128)(2,1)S(1)} fusion(f32[12,512,512]{1,2,0:T(8,128)} %get-tuple-element.71, f32[12,512,512]{1,2,0:T(8,128)S(1)} %bitcast.70, f32[12,512]{1,0:T(8,128)S(1)} %get-tuple-element.70, f32[12,512]{1,0:T(8,128)S(1)} %log_add_fusion), kind=kLoop, calls=%fused_computation.6 | loop fusion | flops 12582912 | bytes 31506432 | tf_op jit(solution)/shard_map/convert_element_type | solution.py:360
  274.4 2.0 multiply_convert_fusion.1
  276.4 0.6 copy-done.3
  277.0 1.1 multiply_convert_fusion.2
  278.1 2.2 fusion.41
  280.3 1.2 fusion.56
  281.5 5.1 fusion.40
  286.6 3.5 fusion.21
  290.0 0.2 broadcast_in_dim.54
  290.2 0.2 broadcast_in_dim.55
  290.4 11.4 %concatenate.12 = f32[768,3090]{1,0:T(8,128)} concatenate(f32[768,2304]{1,0:T(8,128)} %fusion.40, f32[768,768]{1,0:T(8,128)} %fusion.41, f32[768,16]{1,0:T(8,128)} %fusion.56, f32[768,1]{1,0:T(8,128)S(1)} %broadcast_in_dim.54, f32[768,1]{1,0:T(8,128)S(1)} %broadcast_in_dim.55), dimensions={1} | concatenate | bytes 18984960 | tf_op jit(solution)/shard_map/concatenate | solution.py:371
  301.8 0.0 all-reduce.4.cloned.1.call-update
  301.8 14.4 %copy.79 = bf16[12,512,512]{2,0,1:T(8,128)(2,1)} copy(bf16[12,512,512]{1,2,0:T(8,128)(2,1)} %copy-done.3) | data formatting | bytes 12582912 | tf_op jit(solution)/shard_map/convert_element_type | solution.py:360
  316.3 7.5 %fusion.33 = f32[32,12]{0,1:T(8,128)S(1)} fusion(bf16[12,512,512]{2,0,1:T(8,128)(2,1)} %copy.79, s32[512,512]{1,0:T(8,128)} %param.15), kind=kOutput, calls=%fused_computation.53 | convolution fusion | flops 209715200 | bytes 7341568 | tf_op jit(solution)/shard_map/hij,bij->bh/dot_general | solution.py:366
  323.7 54.9 %psum.7 = f32[32,12]{0,1:T(8,128)} all-reduce(f32[32,12]{0,1:T(8,128)S(1)} %fusion.33), channel_id=1, replica_groups=mesh['dp'=2,'expert'=16] {'dp','expert'}, use_global_device_ids=true, to_apply=%region_17.18 | all-reduce | flops 384 | bytes 3072 | tf_op jit(solution)/shard_map/psum | solution.py:374
  378.7 3.1 fusion.23
  381.7 129.4 %all-reduce.4.cloned.1.call-done = f32[768,3090]{1,0:T(8,128)} async-done(((f32[768,3090]{1,0:T(8,128)}), f32[768,3090]{1,0:T(8,128)}) %all-reduce.4.cloned.1.call-update) | async-done | bytes 9492496
  511.1 0.8 dynamic-slice.5
  511.9 0.7 copy.80
  512.6 1.6 constant_dynamic-slice_fusion
  514.2 1.6 dynamic-slice.3
  515.8 1.5 dynamic-slice_reduce_fusion
  517.3 5.0 copy.92
  522.3 2.2 copy.93
  (72 shorter events, 0.3 us)
Async XLA Ops:
  7.2 4.1 copy-start
  7.2 71.4 %all-gather.2.cloned.1.call-start = ((), (), s32[]{:S(2)}) async-start(), calls=%async_computation | async-start | bytes 5068800 | tf_op jit(solution)/shard_map/all_gather | solution.py:293
  11.2 499.9 %all-reduce.4.cloned.1.call-start = ((), (), s32[]{:S(2)}) async-start(), calls=%async_computation.1 | async-start | bytes 19660800
  26.1 17.3 %copy-start.17 = (s32[512,1]{0,1:T(1,128)S(1)}, s32[512,1]{0,1:T(1,128)}, u32[]{:S(2)}) copy-start(s32[512,1]{0,1:T(1,128)} %param.14) | copy-start | bytes 6148
  26.1 18.8 %copy-start.12 = (bf16[512,768]{1,0:T(8,128)(2,1)S(1)}, bf16[512,768]{1,0:T(8,128)(2,1)}, u32[]{:S(2)}) copy-start(bf16[512,768]{1,0:T(8,128)(2,1)} %param.12) | copy-start | bytes 2359300
  26.1 19.0 %copy-start.15 = (bf16[512,768]{1,0:T(8,128)(2,1)S(1)}, bf16[512,768]{1,0:T(8,128)(2,1)}, u32[]{:S(2)}) copy-start(bf16[512,768]{1,0:T(8,128)(2,1)} %param.13) | copy-start | bytes 2359300
  84.8 6.3 %copy-start.5 = (bf16[512,768]{0,1:T(8,128)(2,1)}, bf16[512,768]{0,1:T(8,128)(2,1)S(1)}, u32[]{:S(2)}) copy-start(bf16[512,768]{0,1:T(8,128)(2,1)S(1)} %copy.66) | copy-start | bytes 2359300
  91.1 4.6 copy-start.2
  95.7 2.1 copy-start.13
  97.7 2.5 copy-start.10
  100.2 142.3 %copy-start.9 = (f32[512,768]{1,0:T(8,128)}, f32[512,768]{1,0:T(8,128)S(1)}, u32[]{:S(2)}) copy-start(f32[512,768]{1,0:T(8,128)S(1)} %get-tuple-element.64) | copy-start | bytes 4718596
  100.5 3.5 copy-start.7
  100.5 3.5 slice-start.9
  238.2 4.4 copy-start.18
  242.5 1.6 copy-start.16
  242.5 4.6 slice-start.5
  244.2 3.0 slice-start.6
  251.1 7.0 %copy-start.4 = (bf16[512,768]{0,1:T(8,128)(2,1)S(1)}, bf16[512,768]{0,1:T(8,128)(2,1)}, u32[]{:S(2)}) copy-start(bf16[512,768]{0,1:T(8,128)(2,1)} %copy.71) | copy-start | bytes 2359300
  251.1 15.9 %slice-start = ((s8[12582912]{0:T(1024)(128)(4,1)}), s8[4194304]{0:T(1024)(128)(4,1)S(1)}, s32[]{:S(2)}) async-start(s8[12582912]{0:T(1024)(128)(4,1)} %bitcast.69), calls=%async_computation.2 | async-start | bytes 8388608
  251.2 15.9 %slice-start.1 = ((s8[12582912]{0:T(1024)(128)(4,1)}), s8[4194304]{0:T(1024)(128)(4,1)S(1)}, s32[]{:S(2)}) async-start(s8[12582912]{0:T(1024)(128)(4,1)} %bitcast.69), calls=%async_computation.3 | async-start | bytes 8388608
  258.2 8.9 %slice-start.2 = ((s8[12582912]{0:T(1024)(128)(4,1)}), s8[4194304]{0:T(1024)(128)(4,1)S(1)}, s32[]{:S(2)}) async-start(s8[12582912]{0:T(1024)(128)(4,1)} %bitcast.69), calls=%async_computation.4 | async-start | bytes 8388608
  267.1 7.3 %copy-start.6 = (bf16[512,768]{0,1:T(8,128)(2,1)S(1)}, bf16[512,768]{0,1:T(8,128)(2,1)}, u32[]{:S(2)}) copy-start(bf16[512,768]{0,1:T(8,128)(2,1)} %copy-done.5) | copy-start | bytes 2359300
  274.4 2.6 copy-start.3
  277.0 1.1 copy-start.11
  278.1 2.2 copy-start.8
  278.1 3.4 copy-start.14
  278.1 8.5 %slice-start.7 = ((s8[4915200]{0:T(1024)(128)(4,1)}), s8[4194304]{0:T(1024)(128)(4,1)S(1)}, s32[]{:S(2)}) async-start(s8[4915200]{0:T(1024)(128)(4,1)} %bitcast.91), calls=%async_computation.9 | async-start | bytes 8388608
  281.5 5.1 slice-start.8
  378.6 143.6 %slice-start.3 = ((s8[4718592]{0:T(1024)(128)(4,1)}), s8[524288]{0:T(1024)(128)(4,1)S(1)}, s32[]{:S(2)}) async-start(s8[4718592]{0:T(1024)(128)(4,1)} %bitcast.79), calls=%async_computation.5 | async-start | bytes 1048576
  517.3 5.0 slice-start.4
  522.3 2.2 copy-start.1
Sparse Core Ops, SparseCore 0:
  11.4 67.0 all-gather.1
  301.9 209.1 all-reduce.3

commit v2 on v1

v2 whole, which is shorter than its diff:
```python
import functools
import jax
import jax.numpy as jnp
from jax import lax
from jax.experimental import pallas as pl
from jax.experimental.pallas import tpu as pltpu
from jax.sharding import PartitionSpec as P

MESH = pl.DeviceIdType.MESH
F32, BF16 = jnp.float32, jnp.bfloat16
NT = (((1,), (1,)), ((), ()))
EPSILON = 1e-06


def dot(a, b, dims=(((1,), (0,)), ((), ()))):
    return lax.dot_general(a, b, dims, preferred_element_type=F32)


def flipped(index, bits, count):
    result, bit = 0, 1
    while bit < count:
        result = result + bit * (((index // bit) % 2 + (bits // bit) % 2) % 2)
        bit *= 2
    return result


def gelu_parts(hidden):
    c0, c1 = 0.7978845608028654, 0.044715
    square = hidden * hidden
    bend = jnp.tanh(hidden * (c0 + (c0 * c1) * square))
    half = 0.5 + 0.5 * bend
    slope = half + (0.5 * hidden) * (1.0 - bend * bend) * (c0 + (3.0 * c0 * c1) * square)
    return hidden * half, slope


def slots_by_row(routes, me, pad, experts):
    count = routes.shape[1]
    picked = routes == lax.broadcasted_iota(jnp.int32, (experts, count), 0)
    first = lax.broadcasted_iota(jnp.int32, (count, count), 0)
    second = lax.broadcasted_iota(jnp.int32, (count, count), 1)
    before = dot(picked.astype(BF16), (first < second).astype(BF16))
    rank = jnp.sum(jnp.where(picked, before, 0.0), axis=0, keepdims=True).astype(jnp.int32)
    return jnp.bitwise_xor(routes, me) * pad + rank


def greet_all(dp, me, n):
    barrier = pltpu.get_barrier_semaphore()

    def greet(p, _):
        pl.semaphore_signal(barrier, inc=1, device_id=(dp, flipped(me, p, n)), device_id_type=MESH)
        return 0

    lax.fori_loop(1, n, greet, 0)
    pl.semaphore_signal(barrier, inc=1, device_id=(1 - dp, me), device_id_type=MESH)
    pl.semaphore_wait(barrier, n)


def grow_strip(strip, w8):
    strip[0:8] = w8
    have = 8
    while have < strip.shape[0]:
        strip[have : 2 * have] = pltpu.roll(strip[0:have], have, 1)
        have *= 2


def forward_kernel(
    n, pad, experts, heads, gathers, *refs,
):
    (tokens_ref, cot_ref, weights_ref, routes_ref, bias_ref,
     rows_hbm, cots_hbm, probs_hbm, packed_hbm, normed_hbm, attended_hbm, middle_hbm, moe_hbm, chance_hbm, w_hbm, gains_ref,
     w, packed, normed, attended, middle, moe_in, chance, rows, cots, probs, strip,
     shard, blocks, put_sem, cot_send, cot_recv, tree_send, tree_recv, sib_send, sib_recv, pair_sem) = refs
    dp, me = lax.axis_index("dp"), lax.axis_index("expert")
    count, width = tokens_ref.shape
    total = n * pad
    puts = []

    def put(src, dst):
        copy = pltpu.make_async_copy(src, dst, put_sem.at[len(puts)])
        copy.start()
        puts.append(copy)

    greet_all(dp, me, n)
    if gathers:
        own = weights_ref.shape[0]
        block = 2 * own
        half = weights_ref.shape[1] // 2
        pair = pltpu.make_async_remote_copy(
            src_ref=weights_ref, dst_ref=shard, send_sem=pair_sem.at[0], recv_sem=pair_sem.at[1],
            device_id=(1 - dp, me), device_id_type=MESH)
        pair.start()
    else:
        load = pltpu.make_async_copy(weights_ref, w, pair_sem.at[0])
        load.start()
    hits = (slots_by_row(routes_ref[...], me, pad, experts)
            == lax.broadcasted_iota(jnp.int32, (total, count), 0)).astype(BF16)
    cots[...] = dot(hits, cot_ref[...]).astype(BF16).reshape(n, pad, width)
    cots_own = pltpu.make_async_copy(cots.at[0], cots_hbm.at[0], pair_sem.at[2])
    cots_own.start()
    x = tokens_ref[...].astype(F32)
    unit = x * lax.rsqrt(jnp.mean(x * x, axis=1, keepdims=True) + EPSILON)

    def cot_copy(p):
        return pltpu.make_async_remote_copy(
            src_ref=cots.at[p], dst_ref=cots_hbm.at[p], send_sem=cot_send.at[p], recv_sem=cot_recv.at[p],
            device_id=(dp, flipped(me, p, n)), device_id_type=MESH)

    def start_cots(i, _):
        cot_copy(n - i).start()
        return 0

    if gathers:
        pair.wait()
        mine, other = weights_ref[...], shard[...]
        blocks[pl.ds(pl.multiple_of(me * block, 16), block)] = jnp.concatenate(
            [jnp.where(dp == 0, mine, other), jnp.where(dp == 0, other, mine)], axis=0).astype(BF16)
        cols = pl.ds(pl.multiple_of(dp * half, 128), half)
        second, third = 2 - dp, 1 + dp

        def at(r):
            return blocks.at[pl.ds(pl.multiple_of(flipped(me, r, n) * block, 16), block), cols]

        def hop(r, step):
            return pltpu.make_async_remote_copy(
                src_ref=at(r), dst_ref=at(r), send_sem=tree_send.at[r + step], recv_sem=tree_recv.at[r + step],
                device_id=(dp, flipped(me, step, n)), device_id_type=MESH)

        def direct(r):
            return pltpu.make_async_remote_copy(
                src_ref=at(0), dst_ref=at(0), send_sem=tree_send.at[r], recv_sem=tree_recv.at[r],
                device_id=(dp, flipped(me, r, n)), device_id_type=MESH)

        def arrived(r):
            pltpu.make_async_remote_copy(
                src_ref=at(r), dst_ref=at(r), send_sem=tree_send.at[r], recv_sem=tree_recv.at[r],
                device_id=(dp, me), device_id_type=MESH).wait_recv()

        def to_sibling(r):
            return pltpu.make_async_remote_copy(
                src_ref=at(r), dst_ref=at(r), send_sem=sib_send.at[r], recv_sem=sib_recv.at[r],
                device_id=(1 - dp, me), device_id_type=MESH)

        far = list(range(4, n, 4))
        for r in far:
            direct(r).start()
        hop(0, third).start()
        hop(0, second).start()
        for r in far:
            arrived(r)
            hop(r, second).start()
            hop(r, third).start()
            to_sibling(r).start()
        for r in [0] + far:
            arrived(r + second)
            hop(r + second, third).start()
            to_sibling(r + second).start()
        lax.fori_loop(1, n, start_cots, 0)
        for r in [0] + far:
            arrived(r + third)
            to_sibling(r + third).start()
            arrived(r + 3)
            to_sibling(r + 3).start()

        def settle_sibling(r, _):
            other_cols = pl.ds(pl.multiple_of((1 - dp) * half, 128), half)
            there = blocks.at[pl.ds(pl.multiple_of(flipped(me, r, n) * block, 16), block), other_cols]
            pltpu.make_async_remote_copy(
                src_ref=there, dst_ref=there, send_sem=sib_send.at[r], recv_sem=sib_recv.at[r],
                device_id=(1 - dp, me), device_id_type=MESH).wait_recv()
            return 0

        lax.fori_loop(1, n, settle_sibling, 0)
        for core in (0, 1):
            for q in range(n // 2):
                low = blocks[(2 * q) * block + core * own : (2 * q) * block + core * own + own].astype(F32)
                high = blocks[(2 * q + 1) * block + core * own : (2 * q + 1) * block + core * own + own].astype(F32)
                place = core * own * n + q * block
                w[place : place + block] = jnp.concatenate([low, high], axis=0).astype(BF16)
    else:
        lax.fori_loop(1, n, start_cots, 0)
        load.wait()
    put(w, w_hbm)
    extras = w[:, 4 * width :].astype(F32)
    gains = extras[:, 128:256].T
    gains_ref[...] = gains[0:8]
    normed[...] = (unit * gains[0:1]).astype(BF16)
    put(normed, normed_hbm)
    for c in range(3):
        cols_c = slice(c * width, (c + 1) * width)
        packed[:, cols_c] = dot(normed[...], w[:, cols_c]).astype(BF16)
    put(packed, packed_hbm)
    scale = (width // heads) ** -0.5
    lane = lax.broadcasted_iota(jnp.int32, (count, 128), 1)

    def attend(k, _):
        def part(c):
            return packed[:, pl.ds(pl.multiple_of(c * width + k * 128, 128), 128)]

        queries = (part(0).astype(F32) * scale).astype(BF16)
        keys = part(1)
        values = part(2).astype(F32).T.astype(BF16)
        outs = []
        for h in (0, 1):
            grow_strip(strip, bias_ref[2 * k + h])
            own_keys = jnp.where((lane < 64) == (h == 0), keys, jnp.zeros_like(keys))
            scores = dot(own_keys, queries, NT)
            scores = jnp.concatenate(
                [scores[128 * b : 128 * b + 128] + strip[:, 384 - 128 * b : 896 - 128 * b] for b in range(4)], axis=0)
            powers = jnp.exp(scores - jnp.max(scores, axis=0, keepdims=True))
            weights = (powers * (1.0 / jnp.sum(powers, axis=0, keepdims=True))).astype(BF16)
            probs[2 * k + h] = weights
            outs.append(dot(values[64 * h : 64 * h + 64], weights))
        attended[:, pl.ds(pl.multiple_of(k * 128, 128), 128)] = jnp.concatenate(outs, axis=0).T.astype(BF16)
        return 0

    lax.fori_loop(0, heads // 2, attend, 0)
    put(probs, probs_hbm)
    put(attended, attended_hbm)
    mid = tokens_ref[...].astype(F32) + dot(attended[...], w[:, 3 * width : 4 * width])
    middle[...] = mid
    put(middle, middle_hbm)
    moe = (mid * lax.rsqrt(jnp.mean(mid * mid, axis=1, keepdims=True) + EPSILON) * gains[1:2]).astype(BF16)
    moe_in[...] = moe
    put(moe_in, moe_hbm)
    hits = (slots_by_row(routes_ref[...], me, pad, experts)
            == lax.broadcasted_iota(jnp.int32, (total, count), 0)).astype(BF16)
    rows[...] = dot(hits, moe).astype(BF16).reshape(n, pad, width)
    put(rows, rows_hbm)
    logits = dot(moe, w[:, 4 * width : 4 * width + 128])
    logits = jnp.where(lane < experts, logits, -1e30)
    powers = jnp.exp(logits - jnp.max(logits, axis=1, keepdims=True))
    chance[...] = powers / jnp.sum(powers, axis=1, keepdims=True)
    put(chance, chance_hbm)
    if gathers:
        for r in far:
            direct(r).wait_send()
        for r in [0] + far:
            hop(r, second).wait_send()
            hop(r, third).wait_send()
            hop(r + second, third).wait_send()

        def settle_sends(r, _):
            to_sibling(r).wait_send()
            return 0

        lax.fori_loop(1, n, settle_sends, 0)

    def settle_cots(p, _):
        cot_copy(p).wait_send()
        cot_copy(p).wait_recv()
        return 0

    lax.fori_loop(1, n, settle_cots, 0)
    cots_own.wait()
    for copy in puts:
        copy.wait()


def forward(n, pad, experts, heads, gathers, tokens, cotangent, weights, routes, bias):
    count, width = tokens.shape
    wide = weights.shape[1]
    any_ = pl.BlockSpec(memory_space=pl.ANY)
    vmem = pl.BlockSpec(memory_space=pltpu.VMEM)
    dma = pltpu.SemaphoreType.DMA
    own = weights.shape[0]
    shapes = [
        ((n, pad, width), BF16), ((n, pad, width), BF16), ((heads, count, count), BF16), ((count, 3 * width), BF16),
        ((count, width), BF16), ((count, width), BF16), ((count, width), F32), ((count, width), BF16),
        ((count, 128), F32), ((width, wide), BF16), ((8, width), F32),
    ]
    return pl.pallas_call(
        functools.partial(forward_kernel, n, pad, experts, heads, gathers),
        out_shape=tuple(jax.ShapeDtypeStruct(*s) for s in shapes),
        in_specs=[vmem, vmem, vmem if gathers else any_, vmem, vmem],
        out_specs=tuple([any_] * 10 + [vmem]),
        scratch_shapes=[
            pltpu.VMEM((width, wide), BF16),
            pltpu.VMEM((count, 3 * width), BF16),
            pltpu.VMEM((count, width), BF16),
            pltpu.VMEM((count, width), BF16),
            pltpu.VMEM((count, width), F32),
            pltpu.VMEM((count, width), BF16),
            pltpu.VMEM((count, 128), F32),
            pltpu.VMEM((n, pad, width), BF16),
            pltpu.VMEM((n, pad, width), BF16),
            pltpu.VMEM((heads, count, count), BF16),
            pltpu.VMEM((128, 1024), F32),
            pltpu.VMEM((own, wide) if gathers else (8, 128), F32),
            pltpu.VMEM((width, wide) if gathers else (16, 128), BF16),
            dma((10,)), dma((n,)), dma((n,)), dma((n,)), dma((n,)), dma((n,)), dma((n,)), dma((3,)),
        ],
        compiler_params=pltpu.CompilerParams(
            collective_id=1, has_side_effects=True, vmem_limit_bytes=60 * 1024 * 1024),
        name="forward",
    )(tokens, cotangent, weights, routes, bias)


def moe_kernel(
    n, cap, pad, experts,
    rows_ref, cin, w_hbm, win_hbm, wout_hbm,
    back_ret, tie_ret, prod_out, gin_ref, gout_ref,
    win, wout, router, xin, xt, rt, act, hgr, backs, ties, prods, acc1, acc2,
    sib_send, sib_recv, stage,
    wsem, send_sem, recv_sem, ret_send, ret_recv, own_sem, sib_ss, sib_rs, out_sem,
):
    dp, me = lax.axis_index("dp"), lax.axis_index("expert")
    width, ff = win.shape
    per = 256 // cap
    groups = n // per
    rows = per * cap
    chunk = 512
    load_in = pltpu.make_async_copy(win_hbm, win, wsem.at[0])
    load_out = pltpu.make_async_copy(wout_hbm, wout, wsem.at[1])
    load_router = pltpu.make_async_copy(w_hbm.at[:, pl.ds(4 * width, 128)], router, wsem.at[2])
    load_router.start()
    load_in.start()
    load_out.start()
    greet_all(dp, me, n)

    def send(p):
        return pltpu.make_async_remote_copy(
            src_ref=rows_ref.at[p], dst_ref=xin.at[p], send_sem=send_sem.at[p], recv_sem=recv_sem.at[p],
            device_id=(dp, flipped(me, p, n)), device_id_type=MESH,
        )

    def give(kind, p):
        src, dst = ((backs, back_ret), (ties, tie_ret))[kind]
        return pltpu.make_async_remote_copy(
            src_ref=src.at[p], dst_ref=dst.at[p],
            send_sem=ret_send.at[kind, p], recv_sem=ret_recv.at[kind, p],
            device_id=(dp, flipped(me, p, n)), device_id_type=MESH,
        )

    def start(i, _):
        send(n - i).start()
        return 0

    lax.fori_loop(1, n, start, 0)
    xin[0] = rows_ref[0]
    load_router.wait()
    load_in.wait()
    load_out.wait()

    def packed_rows(ref, g):
        block = ref[pl.ds(g * per, per)].reshape(per * pad, width)
        if pad == cap:
            return block
        r = lax.broadcasted_iota(jnp.int32, (rows, per * pad), 0)
        c = lax.broadcasted_iota(jnp.int32, (rows, per * pad), 1)
        return dot(((r // cap) * pad + r % cap == c).astype(BF16), block).astype(BF16)

    def spread_rows(block):
        if pad == cap:
            return block
        r = lax.broadcasted_iota(jnp.int32, (per * pad, rows), 0)
        c = lax.broadcasted_iota(jnp.int32, (per * pad, rows), 1)
        pick = (r // pad == c // cap) & (r % pad == c % cap)
        return dot(pick.astype(BF16), block).astype(BF16)

    def group(g, _):
        def arrive(j, _):
            p = g * per + j

            @pl.when(p != 0)
            def _():
                send(p).wait_recv()
            return 0

        lax.fori_loop(0, per, arrive, 0)
        here = pl.ds(pl.multiple_of(g * rows, rows), rows)
        x = packed_rows(xin, g)
        logits = dot(x, router[...])
        lane = lax.broadcasted_iota(jnp.int32, logits.shape, 1)
        logits = jnp.where(lane < experts, logits, -1e30)
        chance = jnp.exp(logits - jnp.max(logits, axis=1, keepdims=True))
        gate = jnp.sum(jnp.where(lane == me, chance, 0.0), axis=1, keepdims=True) / jnp.sum(
            chance, axis=1, keepdims=True)
        r = (gate * packed_rows(cin, g).astype(F32)).astype(BF16)
        xt[:, here] = x.T
        rt[:, here] = r.T
        acc1[...] = jnp.zeros_like(acc1)
        acc2[...] = jnp.zeros_like(acc2)

        def hidden_chunk(k, _):
            cols = pl.ds(pl.multiple_of(k * chunk, chunk), chunk)
            hidden = dot(x, win[:, cols])
            value, slope = gelu_parts(hidden)
            value = value.astype(BF16)
            act[here, cols] = value
            hg = (dot(r, wout[:, cols]) * slope).astype(BF16)
            hgr[here, cols] = hg
            acc1[...] += dot(hg, win[:, cols], NT)
            acc2[...] += dot(value, wout[:, cols], NT)
            return 0

        lax.fori_loop(0, ff // chunk, hidden_chunk, 0)
        backs[pl.ds(g * per, per)] = spread_rows(acc1[...].astype(BF16)).reshape(per, pad, width)
        produced = acc2[...].astype(BF16)
        prods[pl.ds(g * per, per)] = spread_rows(produced).reshape(per, pad, width)
        tie = jnp.sum(r.astype(F32) * produced.astype(F32), axis=1, keepdims=True)
        for j in range(per):
            row = jnp.broadcast_to(tie[j * cap : (j + 1) * cap], (cap, 128)).T[0:8]
            ties[g * per + j] = jnp.concatenate([row, jnp.zeros((8, 128 - cap), F32)], axis=1)

        def leave(j, _):
            p = g * per + j

            @pl.when(p != 0)
            def _():
                for kind in (0, 1):
                    give(kind, p).start()
            return 0

        lax.fori_loop(0, per, leave, 0)
        return 0

    lax.fori_loop(0, groups, group, 0)
    own_back = pltpu.make_async_copy(backs.at[0], back_ret.at[0], own_sem.at[0])
    own_tie = pltpu.make_async_copy(ties.at[0], tie_ret.at[0], own_sem.at[1])
    out_prod = pltpu.make_async_copy(prods, prod_out, own_sem.at[2])
    own_back.start()
    own_tie.start()
    out_prod.start()

    half = ff // 2
    part = sib_send.shape[3]
    steps = half // part

    def sibling(kind, k):
        return pltpu.make_async_remote_copy(
            src_ref=sib_send.at[kind, k], dst_ref=sib_recv.at[kind, k],
            send_sem=sib_ss.at[kind, k], recv_sem=sib_rs.at[kind, k],
            device_id=(1 - dp, me), device_id_type=MESH,
        )

    def partial(kind, owner, k):
        cols = pl.ds(pl.multiple_of(owner * half + k * part, 128), part)
        return dot(xt[...], hgr[:, cols]) if kind == 0 else dot(rt[...], act[:, cols])

    def theirs(k, _):
        for kind in (0, 1):
            sib_send[kind, k] = partial(kind, 1 - dp, k).astype(BF16)
            sibling(kind, k).start()
        return 0

    lax.fori_loop(0, steps, theirs, 0)

    def out_copy(kind, k):
        cols = pl.ds(pl.multiple_of(k * part, 128), part)
        return pltpu.make_async_copy(
            stage.at[kind, k % 2], (gin_ref, gout_ref)[kind].at[:, cols], out_sem.at[kind, k % 2])

    def ours(k, _):
        for kind in (0, 1):
            value = partial(kind, dp, k)
            sibling(kind, k).wait_recv()
            @pl.when(k >= 2)
            def _():
                out_copy(kind, k - 2).wait()
            stage[kind, k % 2] = value + sib_recv[kind, k].astype(F32)
            out_copy(kind, k).start()
        return 0

    lax.fori_loop(0, steps, ours, 0)
    for kind in (0, 1):
        for k in (steps - 2, steps - 1):
            out_copy(kind, k).wait()

    def settle(p, _):
        send(p).wait_send()
        for kind in (0, 1):
            give(kind, p).wait_recv()
            give(kind, p).wait_send()
        return 0

    lax.fori_loop(1, n, settle, 0)

    def settle_sibling(k, _):
        for kind in (0, 1):
            sibling(kind, k).wait_send()
        return 0

    lax.fori_loop(0, steps, settle_sibling, 0)
    own_back.wait()
    own_tie.wait()
    out_prod.wait()


def moe(n, cap, pad, experts, rows, cots, w, win, wout):
    width, ff = win.shape
    total = n * cap
    part = 256
    steps = ff // 2 // part
    any_ = pl.BlockSpec(memory_space=pl.ANY)
    vmem = pl.BlockSpec(memory_space=pltpu.VMEM)
    dma = pltpu.SemaphoreType.DMA
    per = 256 // cap
    return pl.pallas_call(
        functools.partial(moe_kernel, n, cap, pad, experts),
        out_shape=(
            jax.ShapeDtypeStruct((n, pad, width), BF16),
            jax.ShapeDtypeStruct((n, 8, 128), F32),
            jax.ShapeDtypeStruct((n, pad, width), BF16),
            jax.ShapeDtypeStruct((width, ff // 2), F32),
            jax.ShapeDtypeStruct((width, ff // 2), F32),
        ),
        in_specs=[vmem, vmem, any_, any_, any_],
        out_specs=(any_, any_, any_, any_, any_),
        scratch_shapes=[
            pltpu.VMEM((width, ff), BF16),
            pltpu.VMEM((width, ff), BF16),
            pltpu.VMEM((width, 128), BF16),
            pltpu.VMEM((n, pad, width), BF16),
            pltpu.VMEM((width, total), BF16),
            pltpu.VMEM((width, total), BF16),
            pltpu.VMEM((total, ff), BF16),
            pltpu.VMEM((total, ff), BF16),
            pltpu.VMEM((n, pad, width), BF16),
            pltpu.VMEM((n, 8, 128), F32),
            pltpu.VMEM((n, pad, width), BF16),
            pltpu.VMEM((per * cap, width), F32),
            pltpu.VMEM((per * cap, width), F32),
            pltpu.VMEM((2, steps, width, part), BF16),
            pltpu.VMEM((2, steps, width, part), BF16),
            pltpu.VMEM((2, 2, width, part), F32),
            dma((3,)), dma((n,)), dma((n,)), dma((2, n)), dma((2, n)), dma((3,)),
            dma((2, steps)), dma((2, steps)), dma((2, 2)),
        ],
        compiler_params=pltpu.CompilerParams(
            collective_id=2, has_side_effects=True, vmem_limit_bytes=60 * 1024 * 1024),
        cost_estimate=pl.CostEstimate(
            flops=12 * total * width * ff, bytes_accessed=8 * width * ff, transcendentals=total * ff),
        name="experts",
    )(rows, cots, w, win, wout)


def backward_kernel(n, pad, experts, heads, scatters, *refs):
    (back_ref, tie_ref, prods_ref, routes_ref, cot_ref, tokens_ref, middle_ref, moe_ref, chance_ref, attended_ref,
     normed_ref, packed_ref, gains_ref, hot_ref, own_ref, gain_ref, probs_hbm, w_hbm,
     *rest) = refs
    (mixed_ref, tokens_grad_ref, qkv_grad_ref, att_grad_ref, extra_grad_ref, gain_grad_ref, bias_grad_ref,
     w, prob, returned, mid_grad, att_cot, packed_grad, normed_t, chunk, strip, bias_rows,
     sib_out, sib_in, mine, out1, in1, keep, out2, in2, out3, in3, in4, bias_out, bias_in,
     load_sem, prob_sem, prod_send, prod_recv, sib_s, sib_r, s1, r1, s2, r2, s3, r3, s4, r4, bias_s, bias_r, own_sem) = rest
    dp, me = lax.axis_index("dp"), lax.axis_index("expert")
    count, width = tokens_ref.shape
    total = n * pad
    part = 3 * 128
    lead = (width + 256 + part - 1) // part
    chunks = lead + heads // 2
    load = pltpu.make_async_copy(w_hbm, w, load_sem.at[0])
    load.start()

    def fetch(k):
        return pltpu.make_async_copy(probs_hbm.at[pl.ds(2 * k, 2)], prob.at[k % 2], prob_sem.at[k % 2])

    fetch(0).start()
    greet_all(dp, me, n)

    def give(p):
        return pltpu.make_async_remote_copy(
            src_ref=prods_ref.at[p], dst_ref=returned.at[p], send_sem=prod_send.at[p], recv_sem=prod_recv.at[p],
            device_id=(dp, flipped(me, p, n)), device_id_type=MESH)

    def start_prods(i, _):
        give(n - i).start()
        return 0

    lax.fori_loop(1, n, start_prods, 0)
    own_prod = pltpu.make_async_copy(prods_ref.at[0], returned.at[0], own_sem.at[0])
    own_prod.start()

    if scatters:
        own = own_ref.shape[0]
        half = own * n
        second, third = 2 - dp, 1 + dp

        def remote(src, dst, send, recv, k, device):
            return pltpu.make_async_remote_copy(
                src_ref=src, dst_ref=dst, send_sem=send.at[k], recv_sem=recv.at[k], device_id=device, device_id_type=MESH)

        def hop(stage, k):
            if stage == 0:
                return remote(sib_out.at[k], sib_in.at[k], sib_s, sib_r, k, (1 - dp, me))
            if stage == 1:
                return remote(out1.at[k], in1.at[k], s1, r1, k, (dp, flipped(me, third, n)))
            if stage == 2:
                return remote(out2.at[k], in2.at[k], s2, r2, k, (dp, flipped(me, second, n)))
            if stage == 3:
                return remote(out3.at[k], in3.at[k], s3, r3, k, (dp, flipped(me, 8, n)))
            return remote(keep.at[k, own : 2 * own], in4.at[k], s4, r4, k, (dp, flipped(me, 4, n)))

        def unit(k, u):
            r = third * (u // 4) + second * ((u // 2) % 2) + 8 * (u % 2)
            places = [pl.multiple_of(flipped(me, r + z, n) * own, 8) for z in (0, 4)]
            return jnp.concatenate([mine[k, pl.ds(place, own)] for place in places], axis=0)

        def stage(s, k):
            if s == 0:
                there = pl.ds(pl.multiple_of((1 - dp) * half, 8), half)
                here = pl.ds(pl.multiple_of(dp * half, 8), half)
                sib_out[k] = chunk[there].astype(BF16)
                hop(0, k).start()
                mine[k] = chunk[here]
            elif s == 1:
                hop(0, k).wait_recv()
                mine[k] = mine[k] + sib_in[k].astype(F32)
                for u in range(4):
                    out1[k, 2 * own * u : 2 * own * (u + 1)] = unit(k, u + 4).astype(BF16)
                hop(1, k).start()
                for u in range(4):
                    keep[k, 2 * own * u : 2 * own * (u + 1)] = unit(k, u)
            elif s == 2:
                hop(1, k).wait_recv()
                keep[k] = keep[k] + in1[k].astype(F32)
                out2[k] = keep[k, 4 * own :].astype(BF16)
                hop(2, k).start()
            elif s == 3:
                hop(2, k).wait_recv()
                keep[k, : 4 * own] = keep[k, : 4 * own] + in2[k].astype(F32)
                out3[k] = keep[k, 2 * own : 4 * own].astype(BF16)
                hop(3, k).start()
            elif s == 4:
                hop(3, k).wait_recv()
                keep[k, : 2 * own] = keep[k, : 2 * own] + in3[k].astype(F32)
                hop(4, k).start()
            else:
                hop(4, k).wait_recv()
                keep[k, :own] = keep[k, :own] + in4[k]

        def advance(k, newest):
            for s in (5, 4, 3, 2, 1):
                @pl.when((k - s >= 0) & (k - s < chunks))
                def _():
                    stage(s, k - s)
            if newest:
                stage(0, k)
    else:
        def advance(k, newest):
            if newest:
                copy = pltpu.make_async_copy(chunk, qkv_grad_ref.at[k], own_sem.at[1])
                copy.start()
                copy.wait()

    expert_of = routes_ref[...]
    lane = lax.broadcasted_iota(jnp.int32, (count, 128), 1)
    picked = expert_of == lane
    first = lax.broadcasted_iota(jnp.int32, (count, count), 0)
    other = lax.broadcasted_iota(jnp.int32, (count, count), 1)
    before = dot((other < first).astype(BF16), picked.astype(BF16))
    rank = jnp.sum(jnp.where(picked, before, 0.0), axis=1, keepdims=True).astype(jnp.int32)
    block = jnp.bitwise_xor(expert_of, me)
    hits = (block * pad + rank == lax.broadcasted_iota(jnp.int32, (count, total), 1)).astype(BF16)
    ties = lax.dot_general((block == lax.broadcasted_iota(jnp.int32, (count, n), 1)).astype(F32), tie_ref[...],
                           (((1,), (0,)), ((), ())), preferred_element_type=F32, precision=lax.Precision.HIGHEST)
    tie = jnp.sum(jnp.where(lane == rank, ties, 0.0), axis=1, keepdims=True)
    chance = chance_ref[...]
    logit_grad = (tie * (picked.astype(F32) - chance)).astype(BF16)
    grad = dot(hits, back_ref[...].reshape(total, width))
    load.wait()
    grad = grad + dot(logit_grad, w[:, 4 * width : 4 * width + 128], NT)
    mid = middle_ref[...]
    root = lax.rsqrt(jnp.mean(mid * mid, axis=1, keepdims=True) + EPSILON)
    unit_mid = mid * root
    gain_rows = jnp.sum(grad * unit_mid, axis=0, keepdims=True)
    scaled = grad * gains_ref[1:2]
    mid_g = cot_ref[...].astype(F32) + root * (scaled - unit_mid * jnp.mean(scaled * unit_mid, axis=1, keepdims=True))
    mid_grad[...] = mid_g
    attn_grad = mid_g.astype(BF16)
    att_cot[...] = dot(attn_grad, w[:, 3 * width : 4 * width], NT).astype(BF16)
    attended_t = attended_ref[...].T
    for k in range(lead):
        if (k + 1) * part <= width:
            chunk[...] = dot(attended_t, attn_grad[:, k * part : (k + 1) * part])
        else:
            chunk[:, 0:128] = dot(moe_ref[...].T, logit_grad)
            chunk[:, 128:256] = jnp.broadcast_to(gain_rows, (128, width)).T
            chunk[:, 256:] = jnp.zeros((width, part - 256), F32)
        advance(k, True)
    normed_t[...] = normed_ref[...].T

    scale = (width // heads) ** -0.5

    def attend_back(k, _):
        fetch(k).wait()

        @pl.when(k + 1 < heads // 2)
        def _():
            fetch(k + 1).start()

        def piece(c):
            return packed_ref[:, pl.ds(pl.multiple_of(c * width + k * 128, 128), 128)]

        queries, keys, values = piece(0), piece(1), piece(2)
        keys_t = (keys.astype(F32) * scale).T.astype(BF16)
        cot = att_cot[:, pl.ds(pl.multiple_of(k * 128, 128), 128)]
        query_t, key_g, value_g = [], None, None
        for h in (0, 1):
            mask = (lane < 64) == (h == 0)
            own_cot = jnp.where(mask, cot, jnp.zeros_like(cot))
            own_queries = jnp.where(mask, queries, jnp.zeros_like(queries))
            weights = prob[k % 2, h]
            chances = weights.astype(F32)
            weight_grad = dot(values, own_cot, NT)
            product = chances * weight_grad
            score_grad = product - chances * jnp.sum(product, axis=0, keepdims=True)
            score_grad = score_grad.astype(BF16)
            wide = score_grad.astype(F32)
            for b in range(4):
                rows = wide[128 * b : 128 * b + 128]
                cols = slice(384 - 128 * b, 896 - 128 * b)
                if b == 0:
                    strip[:, cols] = rows
                    strip[:, 0:384] = jnp.zeros((128, 384), F32)
                    strip[:, 896:1024] = jnp.zeros((128, 128), F32)
                else:
                    strip[:, cols] += rows
            have = 64
            folded = strip[...]
            while have >= 8:
                folded = folded[:have] + pltpu.roll(folded[have:], 1024 - have, 1)
                have //= 2
            for s in range(1, 8):
                folded = jnp.where(lax.broadcasted_iota(jnp.int32, folded.shape, 0) == s, pltpu.roll(folded, 1024 - s, 1), folded)
            bias_rows[2 * k + h] = folded
            v = dot(weights, own_cot)
            q = dot(score_grad, own_queries)
            value_g = v if h == 0 else value_g + v
            key_g = q if h == 0 else key_g + q
            query_t.append(dot(keys_t[64 * h : 64 * h + 64], score_grad))
        query_g = jnp.concatenate(query_t, axis=0).T.astype(BF16)
        grads = jnp.concatenate([query_g, (key_g * scale).astype(BF16), value_g.astype(BF16)], axis=1)
        for c in range(3):
            packed_grad[:, pl.ds(pl.multiple_of(c * width + k * 128, 128), 128)] = grads[:, c * 128 : (c + 1) * 128]
        chunk[...] = dot(normed_t[...], grads)
        advance(k + lead, True)
        return 0

    lax.fori_loop(0, heads // 2, attend_back, 0)
    sums = jnp.concatenate([jnp.sum(bias_rows[h], axis=0, keepdims=True) for h in range(heads)]
                           + [jnp.zeros((16 - heads, 1024), F32)], axis=0)
    bias_sum = lax.dot_general(sums, hot_ref[...], (((1,), (0,)), ((), ())), preferred_element_type=F32,
                               precision=lax.Precision.HIGHEST)
    if scatters:
        bias_out[0] = bias_sum

        def bias_hop(s):
            device = (1 - dp, me) if s == 0 else (dp, flipped(me, 1 << (s - 1), n))
            return remote(bias_out.at[s], bias_in.at[s], bias_s, bias_r, s, device)

        steps = n.bit_length()
        bias_hop(0).start()

    def settle(s):
        if scatters:
            advance(chunks + s, False)
            if s < steps:
                bias_hop(s).wait_recv()
                total_bias = bias_out[s] + bias_in[s]
                if s + 1 < steps:
                    bias_out[s + 1] = total_bias
                    bias_hop(s + 1).start()
                else:
                    bias_grad_ref[...] = total_bias

    settle(0)
    normed_grad = dot(packed_grad[...], w[:, : 3 * width], NT)
    settle(1)
    x = tokens_ref[...].astype(F32)
    root = lax.rsqrt(jnp.mean(x * x, axis=1, keepdims=True) + EPSILON)
    unit_x = x * root
    scaled = normed_grad * gains_ref[0:1]
    tokens_grad_ref[...] = mid_grad[...] + root * (
        scaled - unit_x * jnp.mean(scaled * unit_x, axis=1, keepdims=True))
    settle(2)

    def settle_prods(p, _):
        give(p).wait_recv()
        return 0

    own_prod.wait()
    lax.fori_loop(1, n, settle_prods, 0)
    gate = jnp.sum(jnp.where(picked, chance, 0.0), axis=1, keepdims=True)
    mixed_ref[...] = (middle_ref[...] + gate * dot(hits, returned[...].reshape(total, width))).astype(BF16)
    settle(3)
    settle(4)
    if scatters:
        for k in range(chunks):
            done = keep[k, :own]
            if k < lead:
                if (k + 1) * part <= width:
                    att_grad_ref[:, k * part : (k + 1) * part] = done
                else:
                    extra_grad_ref[...] = done[:, :256]
            else:
                for c in range(3):
                    start = c * width + (k - lead) * 128
                    qkv_grad_ref[:, start : start + 128] = done[:, c * 128 : (c + 1) * 128]
        total_gain = jnp.sum(qkv_grad_ref[...] * own_ref[...][:, : 3 * width], axis=1, keepdims=True)
        gain_grad_ref[...] = jnp.broadcast_to(total_gain / gain_ref[...], gain_grad_ref.shape)

        def settle_sends(k, _):
            for s in range(5):
                hop(s, k).wait_send()
            return 0

        lax.fori_loop(0, chunks, settle_sends, 0)
        for s in range(steps):
            bias_hop(s).wait_send()
    else:
        bias_grad_ref[...] = bias_sum

    def settle_sent(p, _):
        give(p).wait_send()
        return 0

    lax.fori_loop(1, n, settle_sent, 0)


def backward(n, pad, experts, heads, scatters, back, ties, prods, routes, cot, tokens, middle, moe_in, chance, attended,
             normed, packed, gains, hot, own, gain, probs, w):
    count, width = tokens.shape
    wide = w.shape[1]
    rows = own.shape[0]
    half = rows * n
    part = 3 * 128
    chunks = (width + 256 + part - 1) // part + heads // 2
    any_ = pl.BlockSpec(memory_space=pl.ANY)
    vmem = pl.BlockSpec(memory_space=pltpu.VMEM)
    dma = pltpu.SemaphoreType.DMA
    small = (1, 8, 128)

    def buffer(shape, kind):
        return pltpu.VMEM(shape if scatters else small, kind)

    return pl.pallas_call(
        functools.partial(backward_kernel, n, pad, experts, heads, scatters),
        out_shape=(
            jax.ShapeDtypeStruct((count, width), BF16),
            jax.ShapeDtypeStruct((count, width), F32),
            jax.ShapeDtypeStruct((rows, 3 * width) if scatters else (chunks, width, part), F32),
            jax.ShapeDtypeStruct((rows, width), F32),
            jax.ShapeDtypeStruct((rows, 256), F32),
            jax.ShapeDtypeStruct((rows, 128), F32),
            jax.ShapeDtypeStruct((16, 128), F32),
        ),
        in_specs=[vmem] * 16 + [any_, any_],
        out_specs=(vmem, vmem, vmem if scatters else any_, vmem, vmem, vmem, vmem),
        scratch_shapes=[
            pltpu.VMEM((width, wide), BF16),
            pltpu.VMEM((2, 2, count, count), BF16),
            pltpu.VMEM((n, pad, width), BF16),
            pltpu.VMEM((count, width), F32),
            pltpu.VMEM((count, width), BF16),
            pltpu.VMEM((count, 3 * width), BF16),
            pltpu.VMEM((width, count), BF16),
            pltpu.VMEM((width, part), F32),
            pltpu.VMEM((128, 1024), F32),
            pltpu.VMEM((heads, 8, 1024), F32),
            buffer((chunks, half, part), BF16),
            buffer((chunks, half, part), BF16),
            buffer((chunks, half, part), F32),
            buffer((chunks, half // 2, part), BF16),
            buffer((chunks, half // 2, part), BF16),
            buffer((chunks, half // 2, part), F32),
            buffer((chunks, half // 4, part), BF16),
            buffer((chunks, half // 4, part), BF16),
            buffer((chunks, half // 8, part), BF16),
            buffer((chunks, half // 8, part), BF16),
            buffer((chunks, rows, part), F32),
            pltpu.VMEM((5, 16, 128), F32),
            pltpu.VMEM((5, 16, 128), F32),
            dma((1,)), dma((2,)), dma((n,)), dma((n,)),
            *[dma((chunks,)) for _ in range(10)],
            dma((5,)), dma((5,)), dma((2,)),
        ],
        compiler_params=pltpu.CompilerParams(
            collective_id=3, has_side_effects=True, vmem_limit_bytes=62 * 1024 * 1024),
        name="backward",
    )(back, ties, prods, routes, cot, tokens, middle, moe_in, chance, attended, normed, packed, gains, hot, own, gain,
      probs, w)


def shards(
    n, tokens, cotangent, routes, buckets, gain_attn, w_qkv, w_att, rel_bias, gain_moe, w_router, w_in, w_out,
):
    axes = ("dp", "expert")
    count, width = tokens.shape
    experts = w_router.shape[1]
    heads = rel_bias.shape[1]
    own = w_qkv.shape[0]
    cap = max(2, 2 * count // experts)
    pad = max(16, cap)
    direct = n == 16 and own % 8 == 0
    blank = jnp.zeros((own, 128 - experts), w_qkv.dtype), jnp.zeros((own, 126), w_qkv.dtype)
    bundle = jnp.concatenate([w_qkv, w_att, w_router, blank[0], gain_attn[:, None], gain_moe[:, None], blank[1]], axis=1)
    weights = bundle.astype(F32) if direct else lax.all_gather(bundle, axes, axis=0, tiled=True)
    line = jnp.concatenate([buckets[0, :385][::-1], buckets[1:, 0], buckets[0, -1:], buckets[0, 385:][::-1]])
    hot = (line[:, None] == jnp.arange(128, dtype=jnp.int32)[None, :]).astype(F32)
    bias = jnp.dot(rel_bias.T, hot[:, : rel_bias.shape[0]].T, precision=lax.Precision.HIGHEST)
    bias = jnp.stack([jnp.roll(bias, s, axis=1) for s in range(8)], axis=1)
    rows, cots, probs, packed, normed, attended, middle, moe_in, chance, w, gains = forward(
        n, pad, experts, heads, direct, tokens, cotangent, weights, routes.reshape(1, count), bias)
    back, ties, prods, grad_in, grad_out = moe(n, cap, pad, experts, rows, cots, w, w_in[0], w_out[0])
    gain_column = gain_attn.astype(F32)[:, None]
    mixed, grad_tokens, grad_qkv, grad_att, grad_extra, grad_gain, grad_bias = backward(
        n, pad, experts, heads, direct, back, ties[:, 0], prods, routes, cotangent, tokens, middle, moe_in, chance,
        attended, normed, packed, gains, hot, bundle.astype(F32), gain_column, probs, w)
    if not direct:
        lead = grad_qkv.shape[0] - heads // 2
        early = jnp.concatenate([grad_qkv[k] for k in range(lead)], axis=1)
        late = [grad_qkv[lead:, :, c * 128 : (c + 1) * 128].transpose(1, 0, 2).reshape(width, width) for c in range(3)]
        both = lax.psum_scatter(jnp.concatenate([early, *late], axis=1), axes, scatter_dimension=0, tiled=True)
        grad_att, grad_extra = both[:, :width], both[:, width : width + 256]
        grad_qkv = both[:, early.shape[1] :]
        grad_gain = jnp.sum(grad_qkv * w_qkv.astype(F32), axis=1, keepdims=True) / gain_column
        grad_bias = lax.psum(grad_bias, axes)
    return (
        mixed, grad_tokens, grad_gain[:, 0], grad_qkv, grad_att, grad_bias[:heads, : rel_bias.shape[0]].T,
        grad_extra[:, 128], grad_extra[:, :experts], grad_in[None], grad_out[None],
    )


def solution(mesh):
    both = P(("dp", "expert"))
    return jax.shard_map(
        functools.partial(shards, mesh.shape["expert"]),
        mesh=mesh,
        in_specs=(both, both, both, P(), both, both, both, P(), both, both, P("expert"), P("expert")),
        out_specs=(both, both, both, both, both, P(), both, both, P("expert", None, "dp"), P("expert", None, "dp")),
        check_vma=False,
    )
```

time: 541 us -> 275 us (0.51); the launches traced: 532 us -> 275 us
  waiting for transfers between devices: 161 us -> 0 us
  Pallas kernels: 133 us -> 241 us
  matrix products: 81.1 us -> 0.31 us
  blocking collectives: 54.9 us -> 0 us
  local copies, waits for them, and re-layouts: 68.3 us -> 29.8 us
  other arithmetic: 18.3 us -> 3.05 us
  between operations: 14.9 us -> 0.81 us
    pallas_call x0 -> x2, Pallas kernels: none -> 157 us  [the longest x1 89 us: backward(): pl.pallas_call(functools.partial(backward_kernel, n, pad, experts, heads,...]
    unnamed x3 -> x0, waiting for transfers between devices: 129 us -> none
    dot_general x21 -> x1, matrix products: 81.1 us -> 0.31 us  [shards(): jnp.dot(rel_bias.T, hot[:, :rel_bias.shape[0]].T, precision=lax.Precision...]
    psum x1 -> x0, blocking collectives: 54.9 us -> none  [shards(): grad_bias = lax.psum(bias_grad, axes)]
    pallas_call x1, Pallas kernels: 133 us -> 83.3 us  [moe(): pl.pallas_call(functools.partial(moe_kernel, n, cap, pad, experts), out_s...]
    all_gather x1 -> x0, waiting for transfers between devices: 31.3 us -> none  [shards(): bundle = lax.all_gather(bundle, axes, axis=0, tiled=True)]
    dot_general x1 -> x0, local copies, waits for them, and re-layouts: 17.3 us -> none  [shards(): jnp.einsum('bij,bh->hij', (buckets[None, :, :] == kinds[:, None, None]).a...]
    convert_element_type x2 -> x0, local copies, waits for them, and re-layouts: 16.7 us -> none  [the longest x1 14.4 us: shards(): (chance * (weight_grad - jnp.sum(chance * weight_grad, axis=-1, keepdims=...]
  transfers between devices with their start and end apart: 2 -> 0, of which waited for: 2 -> 0; matrix products, arithmetic and copies ran while one was open for 11% -> 0% of each run, Pallas kernels for 0% -> 0%
where the time goes in v2:
time: 275 us
  Pallas kernels  241 us (88%)
  local copies, waits for them, and re-layouts  29.8 us (11%)
  other arithmetic  3.05 us (1%)
    pallas_call x1, Pallas kernels, backward(): pl.pallas_call(functools.partial(backward_kernel, n, pad, experts, heads,...  89 us
    pallas_call x1, Pallas kernels, moe(): pl.pallas_call(functools.partial(moe_kernel, n, cap, pad, experts), out_s...  83.3 us
    pallas_call x1, Pallas kernels, forward(): pl.pallas_call(functools.partial(forward_kernel, n, pad, experts, heads,...  68.4 us
    unnamed x25, local copies, waits for them, and re-layouts  15.6 us

profile of v2, /device:TPU:0, one launch (start us, length us, event | category | flops | bytes accessed | tf_op | source)
XLA Modules:
  0.0 274.8 jit_solution(3661201038043472015)
XLA Ops:
  0.6 0.0 copy-start
  0.7 0.7 slice.86
  1.4 0.1 reverse
  1.5 0.1 slice.134
  1.6 1.1 slice_reduce_fusion
  2.6 0.8 slice_bitcast_fusion.2
  3.4 0.1 rev.7
  3.5 1.3 slice.88
  4.8 0.7 pad_add_fusion
  5.5 1.0 fusion.2
  6.5 0.0 copy-done
  6.5 0.3 fusion
  6.8 0.1 slice.115
  6.9 0.1 maximum_bitcast_fusion.2
  7.0 0.1 copy.56
  7.1 0.1 slice.117
  7.1 0.1 maximum_bitcast_fusion.3
  7.2 0.1 copy.57
  7.3 0.1 slice.119
  7.4 0.1 maximum_bitcast_fusion.4
  7.4 0.1 copy.58
  7.5 0.1 slice.121
  7.6 0.1 maximum_bitcast_fusion.5
  7.7 0.1 copy.59
  7.7 0.1 slice.123
  7.8 0.1 pad_maximum_fusion
  7.9 0.1 slice.113
  8.0 0.1 maximum_bitcast_fusion.1
  8.1 0.1 copy.55
  8.1 0.1 slice.111
  8.2 0.1 maximum_bitcast_fusion
  8.3 0.1 copy.54
  8.4 0.1 copy.53
  8.4 1.3 stack.35.refs_4_
  9.7 0.8 copy.50
  10.5 0.7 copy.51
  11.2 0.7 copy.52
  12.0 1.0 concatenate.34
  13.0 0.7 convert_element_type.8.refs_2_.refs_14_
  13.7 68.4 %forward.1 = (bf16[16,64,768]{2,1,0:T(8,128)(2,1)}, bf16[16,64,768]{2,1,0:T(8,128)(2,1)}, bf16[12,512,512]{2,1,0:T(8,128)(2,1)}, bf16[512,2304]{1,0:T(8,128)(2,1...) custom-call(bf16[512,768]{1,0:T(8,128)(2,1)} %refs_5_.1, ...), custom_call_target="tpu_custom_call" | custom-call | tf_op jit(solution)/shard_map/forward/pallas_call | solution.py:271
  82.1 0.0 copy-start.3
  82.1 0.0 copy-start.4
  82.1 83.3 %experts.1 = (bf16[16,64,768]{2,1,0:T(8,128)(2,1)}, f32[16,8,128]{2,1,0:T(8,128)}, bf16[16,64,768]{2,1,0:T(8,128)(2,1)}, f32[768,1536]{1,0:T(8,128)}, f32[768,1536]{1,0:T(8,128)}) custom-call(bf16[16,64,768]{2,1,0:T(8,128)(2,1)} %get-tuple-element.33.rows_ref, bf16[16,64,768]{2,1,0:T(8,128)(2,1)} %get-tuple-element.34.cin, ...), custom_call_target="tpu_custom_call" | custom-call | flops 28991029248 | bytes 18874368 | tf_op jit(solution)/shard_map/experts/pallas_call | solution.py:498
  165.5 0.9 copy.60
  166.3 0.6 slice_bitcast_fusion.refs_1_
  166.9 0.0 copy-done.3
  166.9 0.9 copy.61.refs_3_
  167.8 0.0 copy-done.4
  167.8 0.7 copy.62.refs_15_
  168.5 89.0 %backward.1 = (bf16[512,768]{1,0:T(8,128)(2,1)}, f32[512,768]{1,0:T(8,128)}, f32[24,2304]{1,0:T(8,128)}, f32[24,768]{1,0:T(8,128)}, f32[24,256]{1,0:T(8,128)}, /*index=5*/f32[24,128]{1,0:T(8,128)}, f32[16,128]{1,0:T(8,128)}) custom-call(bf16[16,64,768]{2,1,0:T(8,128)(2,1)} %get-tuple-element.36.refs_0_, f32[16,128]{1,0:T(8,128)} %slice_bitcast_fusion.refs_1_, ...), custom_call_target="tpu_custom_call" | custom-call | tf_op jit(solution)/shard_map/backward/pallas_call | solution.py:836
  257.5 0.0 copy-start.1
  257.5 0.0 copy-start.2
  257.6 1.4 slice_reduce_fusion.1
  258.9 0.7 slice.109
  259.7 0.7 copy.63
  260.3 1.3 slice_bitcast_fusion.1
  261.6 2.1 copy.71
  263.7 2.7 copy.72
  266.3 0.0 copy-done.1
  266.3 0.7 copy.73
  267.0 0.0 copy-done.2
  267.0 0.6 copy.74
  267.7 4.9 %copy.75 = f32[1,768,1536]{2,1,0:T(8,128)} copy(f32[1,768,1536]{2,1,0:T(8,128)} %bitcast.58) | data formatting | bytes 9437184
  272.6 2.2 copy.76
  (9 shorter events, 0.1 us)
Async XLA Ops:
  0.6 5.9 %copy-start = (f32[32,12]{0,1:T(8,128)S(1)}, f32[32,12]{0,1:T(8,128)}, u32[]{:S(2)}) copy-start(f32[32,12]{0,1:T(8,128)} %param.19) | copy-start | bytes 4612
  82.1 84.8 %copy-start.3 = (s32[512,1]{0,1:T(1,128)S(1)}, s32[512,1]{0,1:T(1,128)}, u32[]{:S(2)}) copy-start(s32[512,1]{0,1:T(1,128)} %param.14) | copy-start | bytes 6148
  82.1 85.7 %copy-start.4 = (bf16[24]{0:T(256)(128)(2,1)S(1)}, bf16[24]{0:T(256)(128)(2,1)}, u32[]{:S(2)}) copy-start(bf16[24]{0:T(256)(128)(2,1)} %param.16) | copy-start | bytes 148
  257.5 8.8 %copy-start.1 = (f32[24,2304]{1,0:T(8,128)S(1)}, f32[24,2304]{1,0:T(8,128)}, u32[]{:S(2)}) copy-start(f32[24,2304]{1,0:T(8,128)} %get-tuple-element.103) | copy-start | bytes 663556
  257.5 9.5 %copy-start.2 = (f32[24,768]{1,0:T(8,128)S(1)}, f32[24,768]{1,0:T(8,128)}, u32[]{:S(2)}) copy-start(f32[24,768]{1,0:T(8,128)} %get-tuple-element.104) | copy-start | bytes 221188
  266.3 6.2 %slice-start = ((s8[4718592]{0:T(1024)(128)(4,1)}), s8[4194304]{0:T(1024)(128)(4,1)S(1)}, s32[]{:S(2)}) async-start(s8[4718592]{0:T(1024)(128)(4,1)} %bitcast.55), calls=%async_computation | async-start | bytes 8388608
  267.7 4.9 %slice-start.1 = ((s8[4718592]{0:T(1024)(128)(4,1)}), s8[524288]{0:T(1024)(128)(4,1)S(1)}, s32[]{:S(2)}) async-start(s8[4718592]{0:T(1024)(128)(4,1)} %bitcast.55), calls=%async_computation.1 | async-start | bytes 1048576

commit v3 on v2

v3 whole, which is shorter than its diff:
```python
import functools
import jax
import jax.numpy as jnp
from jax import lax
from jax.experimental import pallas as pl
from jax.experimental.pallas import tpu as pltpu
from jax.sharding import PartitionSpec as P

MESH = pl.DeviceIdType.MESH
F32, BF16 = jnp.float32, jnp.bfloat16
NT = (((1,), (1,)), ((), ()))
EPSILON = 1e-06


def dot(a, b, dims=(((1,), (0,)), ((), ()))):
    return lax.dot_general(a, b, dims, preferred_element_type=F32)


def flipped(index, bits, count):
    result, bit = 0, 1
    while bit < count:
        result = result + bit * (((index // bit) % 2 + (bits // bit) % 2) % 2)
        bit *= 2
    return result


def gelu_parts(hidden):
    c0, c1 = 0.7978845608028654, 0.044715
    square = hidden * hidden
    bend = jnp.tanh(hidden * (c0 + (c0 * c1) * square))
    half = 0.5 + 0.5 * bend
    slope = half + (0.5 * hidden) * (1.0 - bend * bend) * (c0 + (3.0 * c0 * c1) * square)
    return hidden * half, slope


def slots_by_row(routes, me, pad, experts):
    count = routes.shape[1]
    picked = routes == lax.broadcasted_iota(jnp.int32, (experts, count), 0)
    first = lax.broadcasted_iota(jnp.int32, (count, count), 0)
    second = lax.broadcasted_iota(jnp.int32, (count, count), 1)
    before = dot(picked.astype(BF16), (first < second).astype(BF16))
    rank = jnp.sum(jnp.where(picked, before, 0.0), axis=0, keepdims=True).astype(jnp.int32)
    return jnp.bitwise_xor(routes, me) * pad + rank


def greet_all(dp, me, n):
    barrier = pltpu.get_barrier_semaphore()

    def greet(p, _):
        pl.semaphore_signal(barrier, inc=1, device_id=(dp, flipped(me, p, n)), device_id_type=MESH)
        return 0

    lax.fori_loop(1, n, greet, 0)
    pl.semaphore_signal(barrier, inc=1, device_id=(1 - dp, me), device_id_type=MESH)
    pl.semaphore_wait(barrier, n)


def grow_strip(strip, w8):
    strip[0:8] = w8
    have = 8
    while have < strip.shape[0]:
        strip[have : 2 * have] = pltpu.roll(strip[0:have], have, 1)
        have *= 2


def forward_kernel(
    n, pad, experts, heads, gathers, *refs,
):
    (tokens_ref, cot_ref, qkv_ref, att_ref, extra_ref, full_hbm, routes_ref, table_ref, buckets_hbm,
     rows_hbm, cots_hbm, probs_hbm, packed_hbm, normed_hbm, attended_hbm, middle_hbm, moe_hbm, chance_hbm, w_hbm, gains_ref, hot_ref,
     w, packed, normed, attended, middle, moe_in, chance, rows, cots, probs, strip,
     bias, ends, weights_ref, shard, blocks, put_sem, cot_send, cot_recv, tree_send, tree_recv, sib_send, sib_recv, pair_sem) = refs
    dp, me = lax.axis_index("dp"), lax.axis_index("expert")
    count, width = tokens_ref.shape
    total = n * pad
    puts = []

    def put(src, dst):
        copy = pltpu.make_async_copy(src, dst, put_sem.at[len(puts)])
        copy.start()
        puts.append(copy)

    offsets = [pltpu.make_async_copy(buckets_hbm.at[:, pl.ds(c, 128)], ends.at[i], put_sem.at[9 + i])
               for i, c in enumerate((0, count - 128))]
    for copy in offsets:
        copy.start()
    if gathers:
        weights_ref[:, : 3 * width] = qkv_ref[...].astype(F32)
        weights_ref[:, 3 * width : 3 * width + 256] = extra_ref[...].T[: weights_ref.shape[0]]
        weights_ref[:, 3 * width + 256 :] = att_ref[...].astype(F32)
    greet_all(dp, me, n)
    if gathers:
        own = weights_ref.shape[0]
        block = 2 * own
        early = 3 * width + 256
        pair = pltpu.make_async_remote_copy(
            src_ref=weights_ref, dst_ref=shard, send_sem=pair_sem.at[0], recv_sem=pair_sem.at[1],
            device_id=(1 - dp, me), device_id_type=MESH)
        pair.start()
    else:
        load = pltpu.make_async_copy(full_hbm, w, pair_sem.at[0])
        load.start()
    slots = slots_by_row(routes_ref[...], me, pad, experts)
    hits = (slots == lax.broadcasted_iota(jnp.int32, (total, count), 0)).astype(BF16)
    cots[...] = dot(hits, cot_ref[...]).astype(BF16).reshape(n, pad, width)
    cots_own = pltpu.make_async_copy(cots.at[0], cots_hbm.at[0], pair_sem.at[2])
    cots_own.start()
    for copy in offsets:
        copy.wait()
    last, first = ends[1].astype(F32).T[127:128], ends[0].astype(F32).T[0:1]
    line = jnp.concatenate([last, pltpu.roll(first, count - 1, 1)], axis=1)
    line = pltpu.roll(jnp.broadcast_to(line, (8, 2 * count)), 2 * count - 127, 1)[0:1]
    kinds = table_ref.shape[1]
    hot = (line.astype(jnp.int32) == lax.broadcasted_iota(jnp.int32, (kinds, 2 * count), 0)).astype(F32)
    hot_ref[...] = hot
    table = lax.dot_general(table_ref[...], hot, (((1,), (0,)), ((), ())), preferred_element_type=F32,
                            precision=lax.Precision.HIGHEST)
    for h in range(heads):
        row = jnp.broadcast_to(table[h : h + 1], (8, 2 * count))
        place = lax.broadcasted_iota(jnp.int32, row.shape, 0)
        shifted = row
        for r in range(1, 8):
            shifted = jnp.where(place == r, pltpu.roll(row, r, 1), shifted)
        bias[h] = shifted
    x = tokens_ref[...].astype(F32)
    unit = x * lax.rsqrt(jnp.mean(x * x, axis=1, keepdims=True) + EPSILON)

    def cot_copy(p):
        return pltpu.make_async_remote_copy(
            src_ref=cots.at[p], dst_ref=cots_hbm.at[p], send_sem=cot_send.at[p], recv_sem=cot_recv.at[p],
            device_id=(dp, flipped(me, p, n)), device_id_type=MESH)

    def start_cots(early):
        def one(p, _):
            @pl.when((p % 4 == 0) == early)
            def _():
                cot_copy(p).start()
            return 0

        lax.fori_loop(1, n, one, 0)

    if gathers:
        pair.wait()
        mine, other = weights_ref[...], shard[...]
        blocks[pl.ds(pl.multiple_of(me * block, 16), block)] = jnp.concatenate(
            [jnp.where(dp == 0, mine, other), jnp.where(dp == 0, other, mine)], axis=0).astype(BF16)
        second, third = 2 - dp, 1 + dp
        far = list(range(4, n, 4))
        near = [0] + far

        def at(t, r, core):
            start, size = ((0, early // 2), (early, width // 2))[t]
            return blocks.at[pl.ds(pl.multiple_of(flipped(me, r, n) * block, 16), block),
                             pl.ds(pl.multiple_of(start + core * size, 128), size)]

        def hop(t, r, step):
            return pltpu.make_async_remote_copy(
                src_ref=at(t, r, dp), dst_ref=at(t, r, dp),
                send_sem=tree_send.at[t, r + step], recv_sem=tree_recv.at[t, r + step],
                device_id=(dp, flipped(me, step, n)), device_id_type=MESH)

        def arrived(t, r):
            pltpu.make_async_remote_copy(
                src_ref=at(t, r, dp), dst_ref=at(t, r, dp), send_sem=tree_send.at[t, r], recv_sem=tree_recv.at[t, r],
                device_id=(dp, flipped(me, r, n)), device_id_type=MESH).wait_recv()

        def to_sibling(t, r):
            return pltpu.make_async_remote_copy(
                src_ref=at(t, r, dp), dst_ref=at(t, r, dp), send_sem=sib_send.at[t, r], recv_sem=sib_recv.at[t, r],
                device_id=(1 - dp, me), device_id_type=MESH)

        def from_sibling(t, r):
            return pltpu.make_async_remote_copy(
                src_ref=at(t, r, 1 - dp), dst_ref=at(t, r, 1 - dp), send_sem=sib_send.at[t, r], recv_sem=sib_recv.at[t, r],
                device_id=(1 - dp, me), device_id_type=MESH)

        def turn(t, step):
            if step == 0:
                for r in far:
                    hop(t, 0, r).start()
                hop(t, 0, third).start()
                hop(t, 0, second).start()
            elif step == 1:
                for r in far:
                    arrived(t, r)
                    hop(t, r, third).start()
                    hop(t, r, second).start()
                    to_sibling(t, r).start()
            elif step == 2:
                for r in near:
                    arrived(t, r + second)
                    hop(t, r + second, third).start()
                    to_sibling(t, r + second).start()
            elif step == 3:
                for r in near:
                    arrived(t, r + third)
                    to_sibling(t, r + third).start()
                    arrived(t, r + 3)
                    to_sibling(t, r + 3).start()
            else:
                def settle(r, _):
                    from_sibling(t, r).wait_recv()
                    return 0

                lax.fori_loop(1, n, settle, 0)
                place = (slice(0, early), slice(early, w.shape[1]))[t]
                for core in (0, 1):
                    for q in range(n // 2):
                        low = 2 * q * block + core * own
                        pair_rows = [blocks[p : p + own, place].astype(F32) for p in (low, low + block)]
                        w[core * own * n + q * block : core * own * n + (q + 1) * block, place] = jnp.concatenate(
                            pair_rows, axis=0).astype(BF16)

        turn(0, 0)
        turn(0, 1)
        turn(1, 0)
        turn(0, 2)
        start_cots(True)
        turn(1, 1)
        turn(0, 3)
        turn(1, 2)
        start_cots(False)
        turn(0, 4)
    else:
        start_cots(True)
        start_cots(False)
        load.wait()
    gains_ref[...] = w[:, 3 * width + 128 : 3 * width + 256].astype(F32).T[0:8]
    normed[...] = (unit * gains_ref[0:1]).astype(BF16)
    put(normed, normed_hbm)
    for c in range(3):
        cols_c = slice(c * width, (c + 1) * width)
        packed[:, cols_c] = dot(normed[...], w[:, cols_c]).astype(BF16)
    put(packed, packed_hbm)
    scale = (width // heads) ** -0.5
    lane = lax.broadcasted_iota(jnp.int32, (count, 128), 1)

    def attend(k, _):
        def part(c):
            return packed[:, pl.ds(pl.multiple_of(c * width + k * 128, 128), 128)]

        queries = (part(0).astype(F32) * scale).astype(BF16)
        keys = part(1)
        values = part(2).astype(F32).T.astype(BF16)
        outs = []
        for h in (0, 1):
            grow_strip(strip, bias[2 * k + h])
            own_keys = jnp.where((lane < 64) == (h == 0), keys, jnp.zeros_like(keys))
            scores = dot(own_keys, queries, NT)
            scores = jnp.concatenate(
                [scores[128 * b : 128 * b + 128] + strip[:, 384 - 128 * b : 896 - 128 * b] for b in range(4)], axis=0)
            powers = jnp.exp(scores - jnp.max(scores, axis=0, keepdims=True))
            weights = (powers * (1.0 / jnp.sum(powers, axis=0, keepdims=True))).astype(BF16)
            probs[2 * k + h] = weights
            outs.append(dot(values[64 * h : 64 * h + 64], weights))
        attended[:, pl.ds(pl.multiple_of(k * 128, 128), 128)] = jnp.concatenate(outs, axis=0).T.astype(BF16)
        if gathers:
            for step in (3, 4):
                @pl.when(k == step - 2)
                def _():
                    turn(1, step)
        return 0

    lax.fori_loop(0, heads // 2, attend, 0)
    put(w, w_hbm)
    put(probs, probs_hbm)
    put(attended, attended_hbm)
    mid = tokens_ref[...].astype(F32) + dot(attended[...], w[:, 3 * width + 256 :])
    middle[...] = mid
    put(middle, middle_hbm)
    moe = (mid * lax.rsqrt(jnp.mean(mid * mid, axis=1, keepdims=True) + EPSILON) * gains_ref[1:2]).astype(BF16)
    moe_in[...] = moe
    put(moe_in, moe_hbm)
    hits = (slots == lax.broadcasted_iota(jnp.int32, (total, count), 0)).astype(BF16)
    rows[...] = dot(hits, moe).astype(BF16).reshape(n, pad, width)
    put(rows, rows_hbm)
    logits = dot(moe, w[:, 3 * width : 3 * width + 128])
    logits = jnp.where(lane < experts, logits, -1e30)
    powers = jnp.exp(logits - jnp.max(logits, axis=1, keepdims=True))
    chance[...] = powers / jnp.sum(powers, axis=1, keepdims=True)
    put(chance, chance_hbm)
    if gathers:
        for t in (0, 1):
            for r in far:
                hop(t, 0, r).wait_send()
            for r in near:
                hop(t, r, second).wait_send()
                hop(t, r, third).wait_send()
                hop(t, r + second, third).wait_send()

            def settle_sends(r, _):
                to_sibling(t, r).wait_send()
                return 0

            lax.fori_loop(1, n, settle_sends, 0)

    def settle_cots(p, _):
        cot_copy(p).wait_send()
        cot_copy(p).wait_recv()
        return 0

    lax.fori_loop(1, n, settle_cots, 0)
    cots_own.wait()
    for copy in puts:
        copy.wait()


def forward(n, pad, experts, heads, gathers, tokens, cotangent, qkv, att, extra, full, routes, table, buckets):
    count, width = tokens.shape
    wide = 4 * width + 256
    any_ = pl.BlockSpec(memory_space=pl.ANY)
    vmem = pl.BlockSpec(memory_space=pltpu.VMEM)
    dma = pltpu.SemaphoreType.DMA
    own = qkv.shape[0]
    shapes = [
        ((n, pad, width), BF16), ((n, pad, width), BF16), ((heads, count, count), BF16), ((count, 3 * width), BF16),
        ((count, width), BF16), ((count, width), BF16), ((count, width), F32), ((count, width), BF16),
        ((count, 128), F32), ((width, wide), BF16), ((8, width), F32), ((table.shape[1], 2 * count), F32),
    ]
    return pl.pallas_call(
        functools.partial(forward_kernel, n, pad, experts, heads, gathers),
        out_shape=tuple(jax.ShapeDtypeStruct(*s) for s in shapes),
        in_specs=[vmem] * 5 + [any_, vmem, vmem, any_],
        out_specs=tuple([any_] * 10 + [vmem] * 2),
        scratch_shapes=[
            pltpu.VMEM((width, wide), BF16),
            pltpu.VMEM((count, 3 * width), BF16),
            pltpu.VMEM((count, width), BF16),
            pltpu.VMEM((count, width), BF16),
            pltpu.VMEM((count, width), F32),
            pltpu.VMEM((count, width), BF16),
            pltpu.VMEM((count, 128), F32),
            pltpu.VMEM((n, pad, width), BF16),
            pltpu.VMEM((n, pad, width), BF16),
            pltpu.VMEM((heads, count, count), BF16),
            pltpu.VMEM((128, 1024), F32),
            pltpu.VMEM((heads, 8, 2 * count), F32),
            pltpu.VMEM((2, count, 128), jnp.int32),
            pltpu.VMEM((own, wide) if gathers else (8, 128), F32),
            pltpu.VMEM((own, wide) if gathers else (8, 128), F32),
            pltpu.VMEM((width, wide) if gathers else (16, 128), BF16),
            dma((11,)), dma((n,)), dma((n,)), dma((2, n)), dma((2, n)), dma((2, n)), dma((2, n)), dma((3,)),
        ],
        compiler_params=pltpu.CompilerParams(
            collective_id=1, has_side_effects=True, vmem_limit_bytes=60 * 1024 * 1024),
        name="forward",
    )(tokens, cotangent, qkv, att, extra, full, routes, table, buckets)


def moe_kernel(
    n, cap, pad, experts,
    rows_ref, cin, w_hbm, win_hbm, wout_hbm,
    back_ret, tie_ret, prod_out, gin_ref, gout_ref,
    win, wout, router, xin, xt, rt, act, hgr, backs, ties, prods,
    sib_send, sib_recv, stage,
    wsem, send_sem, recv_sem, ret_send, ret_recv, own_sem, sib_ss, sib_rs, out_sem,
):
    dp, me = lax.axis_index("dp"), lax.axis_index("expert")
    width, ff = win.shape
    per = 256 // cap
    groups = n // per
    rows = per * cap
    chunk = 1024
    load_in = pltpu.make_async_copy(win_hbm, win, wsem.at[0])
    load_out = pltpu.make_async_copy(wout_hbm, wout, wsem.at[1])
    load_router = pltpu.make_async_copy(w_hbm.at[:, pl.ds(3 * width, 128)], router, wsem.at[2])
    load_router.start()
    load_in.start()
    load_out.start()
    greet_all(dp, me, n)

    def send(p):
        return pltpu.make_async_remote_copy(
            src_ref=rows_ref.at[p], dst_ref=xin.at[p], send_sem=send_sem.at[p], recv_sem=recv_sem.at[p],
            device_id=(dp, flipped(me, p, n)), device_id_type=MESH,
        )

    def give(kind, p):
        src, dst = ((backs, back_ret), (ties, tie_ret))[kind]
        return pltpu.make_async_remote_copy(
            src_ref=src.at[p], dst_ref=dst.at[p],
            send_sem=ret_send.at[kind, p], recv_sem=ret_recv.at[kind, p],
            device_id=(dp, flipped(me, p, n)), device_id_type=MESH,
        )

    def start(early):
        def one(p, _):
            @pl.when(((p < 4) | (p % 4 == 0)) == early)
            def _():
                send(p).start()
            return 0

        lax.fori_loop(1, n, one, 0)

    start(True)
    xin[0] = rows_ref[0]
    load_router.wait()
    load_in.wait()
    load_out.wait()

    def packed_rows(ref, g):
        block = ref[pl.ds(g * per, per)].reshape(per * pad, width)
        if pad == cap:
            return block
        r = lax.broadcasted_iota(jnp.int32, (rows, per * pad), 0)
        c = lax.broadcasted_iota(jnp.int32, (rows, per * pad), 1)
        return dot(((r // cap) * pad + r % cap == c).astype(BF16), block).astype(BF16)

    def spread_rows(block):
        if pad == cap:
            return block
        r = lax.broadcasted_iota(jnp.int32, (per * pad, rows), 0)
        c = lax.broadcasted_iota(jnp.int32, (per * pad, rows), 1)
        pick = (r // pad == c // cap) & (r % pad == c % cap)
        return dot(pick.astype(BF16), block).astype(BF16)

    def group(g, _):
        def arrive(j, _):
            send(g * per + j).wait_recv()
            return 0

        @pl.when(g == 0)
        def _():
            lax.fori_loop(1, 4, arrive, 0)
            start(False)
            lax.fori_loop(4, per, arrive, 0)

        @pl.when(g != 0)
        def _():
            lax.fori_loop(0, per, arrive, 0)

        here = pl.ds(pl.multiple_of(g * rows, rows), rows)
        x = packed_rows(xin, g)
        logits = dot(x, router[...])
        lane = lax.broadcasted_iota(jnp.int32, logits.shape, 1)
        logits = jnp.where(lane < experts, logits, -1e30)
        chance = jnp.exp(logits - jnp.max(logits, axis=1, keepdims=True))
        gate = jnp.sum(jnp.where(lane == me, chance, 0.0), axis=1, keepdims=True) / jnp.sum(
            chance, axis=1, keepdims=True)
        r = (gate * packed_rows(cin, g).astype(F32)).astype(BF16)
        xt[:, here] = x.T
        rt[:, here] = r.T

        def hidden_chunk(k, _):
            cols = pl.ds(pl.multiple_of(k * chunk, chunk), chunk)
            hidden = dot(x, win[:, cols])
            value, slope = gelu_parts(hidden)
            value = value.astype(BF16)
            act[here, cols] = value
            hg = (dot(r, wout[:, cols]) * slope).astype(BF16)
            hgr[here, cols] = hg
            return 0

        lax.fori_loop(0, ff // chunk, hidden_chunk, 0)
        backs[pl.ds(g * per, per)] = spread_rows(dot(hgr[here], win[...], NT).astype(BF16)).reshape(per, pad, width)

        def leave(kind):
            def one(j, _):
                p = g * per + j

                @pl.when(p != 0)
                def _():
                    give(kind, p).start()
                return 0

            lax.fori_loop(0, per, one, 0)

        leave(0)
        produced = dot(act[here], wout[...], NT).astype(BF16)
        prods[pl.ds(g * per, per)] = spread_rows(produced).reshape(per, pad, width)
        tie = jnp.sum(r.astype(F32) * produced.astype(F32), axis=1, keepdims=True)
        for j in range(per):
            row = jnp.broadcast_to(tie[j * cap : (j + 1) * cap], (cap, 128)).T[0:8]
            ties[g * per + j] = jnp.concatenate([row, jnp.zeros((8, 128 - cap), F32)], axis=1)
        leave(1)
        return 0

    lax.fori_loop(0, groups, group, 0)
    own_back = pltpu.make_async_copy(backs.at[0], back_ret.at[0], own_sem.at[0])
    own_tie = pltpu.make_async_copy(ties.at[0], tie_ret.at[0], own_sem.at[1])
    out_prod = pltpu.make_async_copy(prods, prod_out, own_sem.at[2])
    own_back.start()
    own_tie.start()
    out_prod.start()

    half = ff // 2
    part = sib_send.shape[3]
    steps = half // part

    def sibling(kind, k):
        return pltpu.make_async_remote_copy(
            src_ref=sib_send.at[kind, k], dst_ref=sib_recv.at[kind, k],
            send_sem=sib_ss.at[kind, k], recv_sem=sib_rs.at[kind, k],
            device_id=(1 - dp, me), device_id_type=MESH,
        )

    def partial(kind, owner, k):
        cols = pl.ds(pl.multiple_of(owner * half + k * part, 128), part)
        return dot(xt[...], hgr[:, cols]) if kind == 0 else dot(rt[...], act[:, cols])

    def theirs(k, _):
        for kind in (0, 1):
            sib_send[kind, k] = partial(kind, 1 - dp, k).astype(BF16)
            sibling(kind, k).start()
        return 0

    lax.fori_loop(0, steps, theirs, 0)

    def out_copy(kind, k):
        cols = pl.ds(pl.multiple_of(k * part, 128), part)
        return pltpu.make_async_copy(
            stage.at[kind, k % 2], (gin_ref, gout_ref)[kind].at[:, cols], out_sem.at[kind, k % 2])

    def ours(k, _):
        for kind in (0, 1):
            value = partial(kind, dp, k)
            sibling(kind, k).wait_recv()
            @pl.when(k >= 2)
            def _():
                out_copy(kind, k - 2).wait()
            stage[kind, k % 2] = (value + sib_recv[kind, k].astype(F32)).astype(BF16)
            out_copy(kind, k).start()
        return 0

    lax.fori_loop(0, steps, ours, 0)
    for kind in (0, 1):
        for k in (steps - 2, steps - 1):
            out_copy(kind, k).wait()

    def settle(p, _):
        send(p).wait_send()
        for kind in (0, 1):
            give(kind, p).wait_recv()
            give(kind, p).wait_send()
        return 0

    lax.fori_loop(1, n, settle, 0)

    def settle_sibling(k, _):
        for kind in (0, 1):
            sibling(kind, k).wait_send()
        return 0

    lax.fori_loop(0, steps, settle_sibling, 0)
    own_back.wait()
    own_tie.wait()
    out_prod.wait()


def moe(n, cap, pad, experts, rows, cots, w, win, wout):
    width, ff = win.shape
    total = n * cap
    part = 768
    steps = ff // 2 // part
    any_ = pl.BlockSpec(memory_space=pl.ANY)
    vmem = pl.BlockSpec(memory_space=pltpu.VMEM)
    dma = pltpu.SemaphoreType.DMA
    return pl.pallas_call(
        functools.partial(moe_kernel, n, cap, pad, experts),
        out_shape=(
            jax.ShapeDtypeStruct((n, pad, width), BF16),
            jax.ShapeDtypeStruct((n, 8, 128), F32),
            jax.ShapeDtypeStruct((n, pad, width), BF16),
            jax.ShapeDtypeStruct((width, ff // 2), BF16),
            jax.ShapeDtypeStruct((width, ff // 2), BF16),
        ),
        in_specs=[vmem, vmem, any_, any_, any_],
        out_specs=(any_, any_, any_, any_, any_),
        scratch_shapes=[
            pltpu.VMEM((width, ff), BF16),
            pltpu.VMEM((width, ff), BF16),
            pltpu.VMEM((width, 128), BF16),
            pltpu.VMEM((n, pad, width), BF16),
            pltpu.VMEM((width, total), BF16),
            pltpu.VMEM((width, total), BF16),
            pltpu.VMEM((total, ff), BF16),
            pltpu.VMEM((total, ff), BF16),
            pltpu.VMEM((n, pad, width), BF16),
            pltpu.VMEM((n, 8, 128), F32),
            pltpu.VMEM((n, pad, width), BF16),
            pltpu.VMEM((2, steps, width, part), BF16),
            pltpu.VMEM((2, steps, width, part), BF16),
            pltpu.VMEM((2, 2, width, part), BF16),
            dma((3,)), dma((n,)), dma((n,)), dma((2, n)), dma((2, n)), dma((3,)),
            dma((2, steps)), dma((2, steps)), dma((2, 2)),
        ],
        compiler_params=pltpu.CompilerParams(
            collective_id=2, has_side_effects=True, vmem_limit_bytes=60 * 1024 * 1024),
        cost_estimate=pl.CostEstimate(
            flops=12 * total * width * ff, bytes_accessed=8 * width * ff, transcendentals=total * ff),
        name="experts",
    )(rows, cots, w, win, wout)


LOADS = 11
LAG = (0, 1, 7, 9)


def backward_kernel(n, pad, experts, heads, scatters, *refs):
    (routes_ref, gains_ref, hot_ref, own_ref, gain_ref, probs_hbm, prods_hbm, *rest) = refs
    sources, rest = rest[:LOADS], rest[LOADS:]
    (mixed_ref, tokens_grad_ref, qkv_grad_ref, att_grad_ref, extra_grad_ref, gain_grad_ref, bias_grad_ref, *rest) = rest
    loaded, rest = rest[:LOADS], rest[LOADS:]
    (prob, returned, mid_grad, att_cot, packed_grad, normed_t, chunk, strip, bias_rows,
     sib_out, sib_in, mine, out1, in1, keep, out2, in2, bias_out, bias_in, bias_pair,
     load_sem, prob_sem, prod_send, prod_recv, sib_s, sib_r, s1, r1, s2, r2, bias_s, bias_r, own_sem) = rest
    (back_ref, tie_ref, chance_ref, middle_ref, w, cot_ref, attended_ref, moe_ref, normed_ref, packed_ref, tokens_ref) = loaded
    loads = [pltpu.make_async_copy(sources[i], loaded[i], load_sem.at[i]) for i in range(LOADS)]
    for load in loads:
        load.start()
    dp, me = lax.axis_index("dp"), lax.axis_index("expert")
    count, width = tokens_ref.shape
    total = n * pad
    part = 3 * 128
    lead = (width + 256 + part - 1) // part
    chunks = lead + heads // 2

    def fetch(k):
        return pltpu.make_async_copy(probs_hbm.at[pl.ds(2 * k, 2)], prob.at[k % 2], prob_sem.at[k % 2])

    fetch(0).start()
    greet_all(dp, me, n)

    def give(p):
        return pltpu.make_async_remote_copy(
            src_ref=prods_hbm.at[p], dst_ref=returned.at[p], send_sem=prod_send.at[p], recv_sem=prod_recv.at[p],
            device_id=(dp, flipped(me, p, n)), device_id_type=MESH)

    def start_prods(i, _):
        give(n - i).start()
        return 0

    lax.fori_loop(1, n, start_prods, 0)
    own_prod = pltpu.make_async_copy(prods_hbm.at[0], returned.at[0], own_sem.at[0])
    own_prod.start()

    if scatters:
        own = own_ref.shape[0]
        half = own * n

        def remote(src, dst, send, recv, device):
            return pltpu.make_async_remote_copy(
                src_ref=src, dst_ref=dst, send_sem=send, recv_sem=recv, device_id=device, device_id_type=MESH)

        def hop(stage, k, d):
            if stage == 0:
                return remote(sib_out.at[k], sib_in.at[k], sib_s.at[k], sib_r.at[k], (1 - dp, me))
            if stage == 1:
                return remote(out1.at[k, d - 1], in1.at[k, d - 1], s1.at[k, d - 1], r1.at[k, d - 1],
                              (dp, flipped(me, d, n)))
            return remote(out2.at[k, d - 1], in2.at[k, d - 1], s2.at[k, d - 1], r2.at[k, d - 1],
                          (dp, flipped(me, 4 * d, n)))

        def owners(k, d):
            places = [pl.multiple_of(flipped(me, d + 4 * z, n) * own, 8) for z in range(4)]
            return jnp.concatenate([mine[k, pl.ds(place, own)] for place in places], axis=0)

        def stage(s, k):
            if s == 0:
                there = pl.ds(pl.multiple_of((1 - dp) * half, 8), half)
                here = pl.ds(pl.multiple_of(dp * half, 8), half)
                sib_out[k] = chunk[there].astype(BF16)
                hop(0, k, 0).start()
                mine[k] = chunk[here]
            elif s == 1:
                hop(0, k, 0).wait_recv()
                mine[k] = mine[k] + sib_in[k].astype(F32)
                for d in (3, 1, 2):
                    out1[k, d - 1] = owners(k, d).astype(BF16)
                    hop(1, k, d).start()
                keep[k] = owners(k, 0)
            elif s == 2:
                for d in (1, 2, 3):
                    hop(1, k, d).wait_recv()
                total_rows = keep[k] + (in1[k, 0].astype(F32) + in1[k, 1].astype(F32)) + in1[k, 2].astype(F32)
                for z in (3, 2, 1):
                    block = total_rows[own * z : own * (z + 1)]
                    out2[k, z - 1] = jnp.concatenate(
                        [block[:, 128 * c : 128 * (c + 1)] for c in range(3)]
                        + [jnp.zeros((out2.shape[2] - 3 * own, 128), F32)], axis=0).astype(BF16)
                    hop(2, k, z).start()
                keep[k, :own] = total_rows[:own]
            else:
                for z in (1, 2, 3):
                    hop(2, k, z).wait_recv()
                far = (in2[k, 0].astype(F32) + in2[k, 1].astype(F32)) + in2[k, 2].astype(F32)
                keep[k, :own] = keep[k, :own] + jnp.concatenate(
                    [far[own * c : own * (c + 1)] for c in range(3)], axis=1)

        def advance(k):
            stage(0, k)
            for s in range(1, 4):
                @pl.when((k - LAG[s] >= 0) & (k - LAG[s] < chunks))
                def _():
                    stage(s, k - LAG[s])

        at = {k: max(s for s in range(4) if LAG[s] <= chunks - 1 - k) for k in range(chunks)}

        def drain():
            for k in sorted((k for k in range(chunks) if at[k] < 3), key=lambda k: (at[k] > 0, k)):
                at[k] += 1
                stage(at[k], k)
    else:
        def advance(k):
            copy = pltpu.make_async_copy(chunk, qkv_grad_ref.at[k], own_sem.at[1])
            copy.start()
            copy.wait()

    expert_of = jnp.broadcast_to(routes_ref[...].astype(F32), (128, count)).T[:, 0:1].astype(jnp.int32)
    lane = lax.broadcasted_iota(jnp.int32, (count, 128), 1)
    picked = expert_of == lane
    first = lax.broadcasted_iota(jnp.int32, (count, count), 0)
    other = lax.broadcasted_iota(jnp.int32, (count, count), 1)
    before = dot((other < first).astype(BF16), picked.astype(BF16))
    rank = jnp.sum(jnp.where(picked, before, 0.0), axis=1, keepdims=True).astype(jnp.int32)
    block = jnp.bitwise_xor(expert_of, me)
    for load in loads[:3]:
        load.wait()
    hits = (block * pad + rank == lax.broadcasted_iota(jnp.int32, (count, total), 1)).astype(BF16)
    ties = lax.dot_general((block == lax.broadcasted_iota(jnp.int32, (count, n), 1)).astype(F32), jnp.max(tie_ref[...], axis=1),
                           (((1,), (0,)), ((), ())), preferred_element_type=F32, precision=lax.Precision.HIGHEST)
    tie = jnp.sum(jnp.where(lane == rank, ties, 0.0), axis=1, keepdims=True)
    chance = chance_ref[...]
    logit_grad = (tie * (picked.astype(F32) - chance)).astype(BF16)
    grad = dot(hits, back_ref[...].reshape(total, width))
    for load in loads[3:]:
        load.wait()
    grad = grad + dot(logit_grad, w[:, 3 * width : 3 * width + 128], NT)
    mid = middle_ref[...]
    root = lax.rsqrt(jnp.mean(mid * mid, axis=1, keepdims=True) + EPSILON)
    unit_mid = mid * root
    gain_rows = jnp.sum(grad * unit_mid, axis=0, keepdims=True)
    scaled = grad * gains_ref[1:2]
    mid_g = cot_ref[...].astype(F32) + root * (scaled - unit_mid * jnp.mean(scaled * unit_mid, axis=1, keepdims=True))
    mid_grad[...] = mid_g
    attn_grad = mid_g.astype(BF16)
    att_cot[...] = dot(attn_grad, w[:, 3 * width + 256 :], NT).astype(BF16)
    attended_t = attended_ref[...].T
    for k in range(lead):
        if (k + 1) * part <= width:
            chunk[...] = dot(attended_t, attn_grad[:, k * part : (k + 1) * part])
        else:
            chunk[:, 0:128] = dot(moe_ref[...].T, logit_grad)
            chunk[:, 128:256] = jnp.broadcast_to(gain_rows, (128, width)).T
            chunk[:, 256:] = jnp.zeros((width, part - 256), F32)
        advance(k)
    normed_t[...] = normed_ref[...].T

    scale = (width // heads) ** -0.5

    def attend_back(k, _):
        fetch(k).wait()

        @pl.when(k + 1 < heads // 2)
        def _():
            fetch(k + 1).start()

        def piece(c):
            return packed_ref[:, pl.ds(pl.multiple_of(c * width + k * 128, 128), 128)]

        queries, keys, values = piece(0), piece(1), piece(2)
        keys_t = (keys.astype(F32) * scale).T.astype(BF16)
        cot = att_cot[:, pl.ds(pl.multiple_of(k * 128, 128), 128)]
        query_t, key_g, value_g = [], None, None
        for h in (0, 1):
            mask = (lane < 64) == (h == 0)
            own_cot = jnp.where(mask, cot, jnp.zeros_like(cot))
            own_queries = jnp.where(mask, queries, jnp.zeros_like(queries))
            weights = prob[k % 2, h]
            chances = weights.astype(F32)
            weight_grad = dot(values, own_cot, NT)
            product = chances * weight_grad
            score_grad = product - chances * jnp.sum(product, axis=0, keepdims=True)
            score_grad = score_grad.astype(BF16)
            wide = score_grad.astype(F32)
            for b in range(4):
                rows = wide[128 * b : 128 * b + 128]
                cols = slice(384 - 128 * b, 896 - 128 * b)
                if b == 0:
                    strip[:, cols] = rows
                    strip[:, 0:384] = jnp.zeros((128, 384), F32)
                    strip[:, 896:1024] = jnp.zeros((128, 128), F32)
                else:
                    strip[:, cols] += rows
            have = 64
            folded = strip[...]
            while have >= 8:
                folded = folded[:have] + pltpu.roll(folded[have:], 1024 - have, 1)
                have //= 2
            for s in range(1, 8):
                folded = jnp.where(lax.broadcasted_iota(jnp.int32, folded.shape, 0) == s, pltpu.roll(folded, 1024 - s, 1), folded)
            bias_rows[2 * k + h] = folded
            v = dot(weights, own_cot)
            q = dot(score_grad, own_queries)
            value_g = v if h == 0 else value_g + v
            key_g = q if h == 0 else key_g + q
            query_t.append(dot(keys_t[64 * h : 64 * h + 64], score_grad))
        query_g = jnp.concatenate(query_t, axis=0).T.astype(BF16)
        grads = jnp.concatenate([query_g, (key_g * scale).astype(BF16), value_g.astype(BF16)], axis=1)
        for c in range(3):
            packed_grad[:, pl.ds(pl.multiple_of(c * width + k * 128, 128), 128)] = grads[:, c * 128 : (c + 1) * 128]
        chunk[...] = dot(normed_t[...], grads)
        advance(k + lead)
        return 0

    lax.fori_loop(0, heads // 2, attend_back, 0)
    if scatters:
        drain()
    sums = jnp.concatenate([jnp.sum(bias_rows[h], axis=0, keepdims=True) for h in range(heads)], axis=0)
    bias_sum = lax.dot_general(sums, hot_ref[...], NT, preferred_element_type=F32, precision=lax.Precision.HIGHEST)
    if scatters:
        bias_out[...] = bias_sum
        pair_hop = remote(bias_out, bias_pair, own_sem.at[1], own_sem.at[2], (1 - dp, me))
        pair_hop.start()

        def bias_hop(p):
            return remote(bias_in.at[me], bias_in.at[me], bias_s.at[p], bias_r.at[p], (dp, flipped(me, p, n)))

        def bias_arrived(p):
            there = flipped(me, p, n)
            return remote(bias_in.at[there], bias_in.at[there], bias_s.at[p], bias_r.at[p], (dp, there))

    normed_grad = dot(packed_grad[...], w[:, : 3 * width], NT)
    if scatters:
        drain()
        pair_hop.wait()
        bias_in[me] = bias_out[...] + bias_pair[...]

        def start_bias(p, _):
            bias_hop(p).start()
            return 0

        lax.fori_loop(1, n, start_bias, 0)
    x = tokens_ref[...].astype(F32)
    root = lax.rsqrt(jnp.mean(x * x, axis=1, keepdims=True) + EPSILON)
    unit_x = x * root
    scaled = normed_grad * gains_ref[0:1]
    tokens_grad_ref[...] = mid_grad[...] + root * (
        scaled - unit_x * jnp.mean(scaled * unit_x, axis=1, keepdims=True))
    if scatters:
        drain()

    def settle_prods(p, _):
        give(p).wait_recv()
        return 0

    own_prod.wait()
    lax.fori_loop(1, n, settle_prods, 0)
    gate = jnp.sum(jnp.where(picked, chance, 0.0), axis=1, keepdims=True)
    mixed_ref[...] = (middle_ref[...] + gate * dot(hits, returned[...].reshape(total, width))).astype(BF16)
    if scatters:
        drain()

        def settle_bias(p, _):
            bias_arrived(p).wait_recv()
            return 0

        lax.fori_loop(1, n, settle_bias, 0)
        total_bias = bias_in[0]
        for p in range(1, n):
            total_bias = total_bias + bias_in[p]
        bias_grad_ref[...] = total_bias
        for k in range(chunks):
            done = keep[k, :own]
            if k < lead:
                if (k + 1) * part <= width:
                    att_grad_ref[:, k * part : (k + 1) * part] = done
                else:
                    extra_grad_ref[...] = done[:, :256]
            else:
                for c in range(3):
                    start = c * width + (k - lead) * 128
                    qkv_grad_ref[:, start : start + 128] = done[:, c * 128 : (c + 1) * 128]
        total_gain = jnp.sum(qkv_grad_ref[...] * own_ref[...].astype(F32), axis=1, keepdims=True)
        gain_grad_ref[...] = jnp.broadcast_to(total_gain / gain_ref[128:256].T[:own, 0:1], gain_grad_ref.shape)

        def settle_sends(k, _):
            hop(0, k, 0).wait_send()
            for d in (1, 2, 3):
                hop(1, k, d).wait_send()
                hop(2, k, d).wait_send()
            return 0

        lax.fori_loop(0, chunks, settle_sends, 0)

        def settle_bias_sends(p, _):
            bias_hop(p).wait_send()
            return 0

        lax.fori_loop(1, n, settle_bias_sends, 0)
    else:
        bias_grad_ref[...] = bias_sum

    def settle_sent(p, _):
        give(p).wait_send()
        return 0

    lax.fori_loop(1, n, settle_sent, 0)


def backward(n, pad, experts, heads, scatters, routes, gains, hot, own, gain, probs, prods, *sources):
    count, width = routes.shape[1], gains.shape[1]
    buckets = hot.shape[0]
    rows = own.shape[0]
    half = rows * n
    part = 3 * 128
    chunks = (width + 256 + part - 1) // part + heads // 2
    any_ = pl.BlockSpec(memory_space=pl.ANY)
    vmem = pl.BlockSpec(memory_space=pltpu.VMEM)
    dma = pltpu.SemaphoreType.DMA
    small = (1, 8, 128)

    def buffer(shape, kind):
        return pltpu.VMEM(shape if scatters else small, kind)

    return pl.pallas_call(
        functools.partial(backward_kernel, n, pad, experts, heads, scatters),
        out_shape=(
            jax.ShapeDtypeStruct((count, width), BF16),
            jax.ShapeDtypeStruct((count, width), F32),
            jax.ShapeDtypeStruct((rows, 3 * width) if scatters else (chunks, width, part), F32),
            jax.ShapeDtypeStruct((rows, width), F32),
            jax.ShapeDtypeStruct((rows, 256), F32),
            jax.ShapeDtypeStruct((rows, 128), F32),
            jax.ShapeDtypeStruct((heads, buckets), F32),
        ),
        in_specs=[vmem] * 5 + [any_] * (2 + LOADS),
        out_specs=(vmem, vmem, vmem if scatters else any_, vmem, vmem, vmem, vmem),
        scratch_shapes=[
            *[pltpu.VMEM(source.shape, source.dtype) for source in sources],
            pltpu.VMEM((2, 2, count, count), BF16),
            pltpu.VMEM((n, pad, width), BF16),
            pltpu.VMEM((count, width), F32),
            pltpu.VMEM((count, width), BF16),
            pltpu.VMEM((count, 3 * width), BF16),
            pltpu.VMEM((width, count), BF16),
            pltpu.VMEM((width, part), F32),
            pltpu.VMEM((128, 1024), F32),
            pltpu.VMEM((heads, 8, 1024), F32),
            buffer((chunks, half, part), BF16),
            buffer((chunks, half, part), BF16),
            buffer((chunks, half, part), F32),
            buffer((chunks, 3, 4 * rows, part), BF16),
            buffer((chunks, 3, 4 * rows, part), BF16),
            buffer((chunks, 4 * rows, part), F32),
            buffer((chunks, 3, -(-3 * rows // 16) * 16, 128), BF16),
            buffer((chunks, 3, -(-3 * rows // 16) * 16, 128), BF16),
            pltpu.VMEM((heads, buckets), F32),
            pltpu.VMEM((n, heads, buckets), F32),
            pltpu.VMEM((heads, buckets), F32),
            dma((LOADS,)), dma((2,)), dma((n,)), dma((n,)), dma((chunks,)), dma((chunks,)),
            *[dma((chunks, 3)) for _ in range(4)],
            dma((n,)), dma((n,)), dma((3,)),
        ],
        compiler_params=pltpu.CompilerParams(
            collective_id=3, has_side_effects=True, vmem_limit_bytes=62 * 1024 * 1024),
        name="backward",
    )(routes, gains, hot, own, gain, probs, prods, *sources)


def finish_kernel(
    mixed_in, tokens_in, in_hbm, out_hbm, qkv_in, att_in, extra_in, gain_in, bias_in,
    mixed_out, tokens_out, in_out, out_out, qkv_out, att_out, router_out, gain_out, gain_moe_out, bias_out,
    mixed, tokens, narrow, wide, sem, load_sem, store_sem,
):
    ins = [pltpu.make_async_copy(mixed_in, mixed, sem.at[0]), pltpu.make_async_copy(tokens_in, tokens, sem.at[1])]
    outs = [pltpu.make_async_copy(mixed, mixed_out, sem.at[2]), pltpu.make_async_copy(tokens, tokens_out, sem.at[3])]
    parts, rows = narrow.shape[1], narrow.shape[2]

    def load(kind, k):
        return pltpu.make_async_copy(
            (in_hbm, out_hbm)[kind].at[pl.ds(k * rows, rows)], narrow.at[kind, k], load_sem.at[kind, k])

    def store(kind, k):
        return pltpu.make_async_copy(
            wide.at[kind, k], (in_out, out_out)[kind].at[0, pl.ds(k * rows, rows)], store_sem.at[kind, k])

    for k in range(parts):
        for kind in (0, 1):
            load(kind, k).start()
    for copy in ins:
        copy.start()
    qkv_out[...] = qkv_in[...]
    att_out[...] = att_in[...]
    router_out[...] = extra_in[:, :128].T[: router_out.shape[0]]
    gain_out[...] = gain_in[...].T[0:1]
    gain_moe_out[...] = extra_in[:, 128:].T[0:1]
    bias_out[...] = bias_in[...]
    for k in range(parts):
        for kind in (0, 1):
            load(kind, k).wait()
            wide[kind, k] = narrow[kind, k].astype(F32)
            store(kind, k).start()
    for copy_in, copy_out in zip(ins, outs):
        copy_in.wait()
        copy_out.start()
    for k in range(parts):
        for kind in (0, 1):
            store(kind, k).wait()
    for copy in outs:
        copy.wait()


def finish(experts, mixed, tokens_grad, grad_in, grad_out, qkv, att, extra, gain, bias):
    any_ = pl.BlockSpec(memory_space=pl.ANY)
    vmem = pl.BlockSpec(memory_space=pltpu.VMEM)
    dma = pltpu.SemaphoreType.DMA
    parts = 8
    rows = grad_in.shape[0] // parts
    own = qkv.shape[0]
    shape = jax.ShapeDtypeStruct
    return pl.pallas_call(
        finish_kernel,
        out_shape=(
            shape(mixed.shape, BF16), shape(tokens_grad.shape, F32), shape((1, *grad_in.shape), F32),
            shape((1, *grad_out.shape), F32), shape(qkv.shape, F32), shape(att.shape, F32), shape((experts, own), F32),
            shape((1, own), F32), shape((1, own), F32), shape(bias.shape, F32),
        ),
        in_specs=[any_] * 4 + [vmem] * 5,
        out_specs=tuple([any_] * 4 + [vmem] * 6),
        scratch_shapes=[
            pltpu.VMEM(mixed.shape, BF16),
            pltpu.VMEM(tokens_grad.shape, F32),
            pltpu.VMEM((2, parts, rows, grad_in.shape[1]), BF16),
            pltpu.VMEM((2, parts, rows, grad_in.shape[1]), F32),
            dma((4,)), dma((2, parts)), dma((2, parts)),
        ],
        compiler_params=pltpu.CompilerParams(vmem_limit_bytes=60 * 1024 * 1024),
        name="finish",
    )(mixed, tokens_grad, grad_in, grad_out, qkv, att, extra, gain, bias)


def shards(
    n, tokens, cotangent, routes, buckets, gain_attn, w_qkv, w_att, rel_bias, gain_moe, w_router, w_in, w_out,
):
    axes = ("dp", "expert")
    count, width = tokens.shape
    experts = w_router.shape[1]
    heads = rel_bias.shape[1]
    own = w_qkv.shape[0]
    cap = max(2, 2 * count // experts)
    pad = max(16, cap)
    direct = n == 16 and own % 8 == 0
    extra = sum(jnp.pad(part.astype(F32), ((low, 256 - low - part.shape[0]), (0, 128 - own)))
                for low, part in ((0, w_router.T), (128, gain_attn[None]), (129, gain_moe[None])))
    full = w_att if direct else lax.all_gather(
        jnp.concatenate([w_qkv, extra[:, :own].T.astype(BF16), w_att], axis=1), axes, axis=0, tiled=True)
    rows, cots, probs, packed, normed, attended, middle, moe_in, chance, w, gains, hot = forward(
        n, pad, experts, heads, direct, tokens, cotangent, w_qkv, w_att, extra, full, routes.T, rel_bias.T, buckets)
    back, ties, prods, grad_in, grad_out = moe(n, cap, pad, experts, rows, cots, w, w_in[0], w_out[0])
    mixed, grad_tokens, grad_qkv, grad_att, grad_extra, grad_gain, grad_bias = backward(
        n, pad, experts, heads, direct, routes.T, gains, hot, w_qkv, extra, probs, prods,
        back, ties, chance, middle, w, cotangent, attended, moe_in, normed, packed, tokens)
    if not direct:
        lead = grad_qkv.shape[0] - heads // 2
        early = jnp.concatenate([grad_qkv[k] for k in range(lead)], axis=1)
        late = [grad_qkv[lead:, :, c * 128 : (c + 1) * 128].transpose(1, 0, 2).reshape(width, width) for c in range(3)]
        both = lax.psum_scatter(jnp.concatenate([early, *late], axis=1), axes, scatter_dimension=0, tiled=True)
        grad_att, grad_extra = both[:, :width], both[:, width : width + 256]
        grad_qkv = both[:, early.shape[1] :]
        grad_gain = jnp.sum(grad_qkv * w_qkv.astype(F32), axis=1, keepdims=True) / gain_attn.astype(F32)[:, None]
        grad_gain = jnp.broadcast_to(grad_gain, (own, 128))
        grad_bias = lax.psum(grad_bias, axes)
    mixed, grad_tokens, grad_in, grad_out, grad_qkv, grad_att, grad_router, grad_gain, grad_gain_moe, grad_bias = finish(
        experts, mixed, grad_tokens, grad_in, grad_out, grad_qkv, grad_att, grad_extra, grad_gain, grad_bias)
    return (
        mixed, grad_tokens, grad_gain.reshape(own), grad_qkv, grad_att, grad_bias.T, grad_gain_moe.reshape(own), grad_router.T,
        grad_in, grad_out,
    )


def solution(mesh):
    both = P(("dp", "expert"))
    return jax.shard_map(
        functools.partial(shards, mesh.shape["expert"]),
        mesh=mesh,
        in_specs=(both, both, both, P(), both, both, both, P(), both, both, P("expert"), P("expert")),
        out_specs=(both, both, both, both, both, P(), both, both, P("expert", None, "dp"), P("expert", None, "dp")),
        check_vma=False,
    )
```

time: 275 us -> 225 us (0.82)
  local copies, waits for them, and re-layouts: 29.8 us -> 0 us
  Pallas kernels: 241 us -> 223 us
    unnamed x25 -> x0, local copies, waits for them, and re-layouts: 15.6 us -> none
    pallas_call x1, Pallas kernels: 89 us -> 78.4 us  [backward(): pl.pallas_call(functools.partial(backward_kernel, n, pad, experts, heads,...]
    pallas_call x1, Pallas kernels: 83.3 us -> 73.6 us  [moe(): pl.pallas_call(functools.partial(moe_kernel, n, cap, pad, experts), out_s...]
    pallas_call x0 -> x1, Pallas kernels: none -> 8.9 us  [finish(): pl.pallas_call(finish_kernel, out_shape=(shape(mixed.shape, BF16), shape(...]
    pallas_call x1, Pallas kernels: 68.4 us -> 61.6 us  [forward(): pl.pallas_call(functools.partial(forward_kernel, n, pad, experts, heads,...]
    slice x12 -> x0, local copies, waits for them, and re-layouts: 5.7 us -> none  [the longest x1 1.4 us: shards(): grad_extra[:, 128]]
where the time goes in v3:
time: 225 us
  Pallas kernels  223 us (99%)
    pallas_call x1, Pallas kernels, backward(): pl.pallas_call(functools.partial(backward_kernel, n, pad, experts, heads,...  78.4 us
    pallas_call x1, Pallas kernels, moe(): pl.pallas_call(functools.partial(moe_kernel, n, cap, pad, experts), out_s...  73.6 us
    pallas_call x1, Pallas kernels, forward(): pl.pallas_call(functools.partial(forward_kernel, n, pad, experts, heads,...  61.6 us
    pallas_call x1, Pallas kernels, finish(): pl.pallas_call(finish_kernel, out_shape=(shape(mixed.shape, BF16), shape(...  8.9 us

profile of v3, /device:TPU:0, one launch (start us, length us, event | category | flops | bytes accessed | tf_op | source)
XLA Modules:
  0.0 224.8 jit_solution(3480714536159417692)
XLA Ops:
  0.6 1.4 convert_add_fusion.refs_4_
  2.0 61.6 %forward.1 = (bf16[16,64,768]{2,1,0:T(8,128)(2,1)}, bf16[16,64,768]{2,1,0:T(8,128)(2,1)}, bf16[12,512,512]{2,1,0:T(8,128)(2,1)}, bf16[512,2304]{1,0:T(8,128)(2,1...) custom-call(bf16[512,768]{1,0:T(8,128)(2,1)} %refs_17_.1, ...), custom_call_target="tpu_custom_call" | custom-call | tf_op jit(solution)/shard_map/forward/pallas_call | solution.py:320
  63.7 73.6 %experts.1 = (bf16[16,64,768]{2,1,0:T(8,128)(2,1)}, f32[16,8,128]{2,1,0:T(8,128)}, bf16[16,64,768]{2,1,0:T(8,128)(2,1)}, bf16[768,1536]{1,0:T(8,128)(2,1)}, bf16[768,1536]{1,0:T(8,128)(2,1)}) custom-call(bf16[16,64,768]{2,1,0:T(8,128)(2,1)} %get-tuple-element.47.rows_ref, bf16[16,64,768]{2,1,0:T(8,128)(2,1)} %get-tuple-element.48.cin, ...), custom_call_target="tpu_custom_call" | custom-call | flops 28991029248 | bytes 18874368 | tf_op jit(solution)/shard_map/experts/pallas_call | solution.py:558
  137.3 78.4 %backward.1 = (bf16[512,768]{1,0:T(8,128)(2,1)}, f32[512,768]{1,0:T(8,128)}, f32[24,2304]{1,0:T(8,128)}, f32[24,768]{1,0:T(8,128)}, f32[24,256]{1,0:T(8,128)}, /*index=5*/f32[24,128]{1,0:T(8,128)}, f32[12,32]{1,0:T(8,128)}) custom-call(s32[1,512]{1,0:T(1,128)} %bitcast.13, f32[8,768]{1,0:T(8,128)} %get-tuple-element.44.refs_1_, ...), custom_call_target="tpu_custom_call" | custom-call | tf_op jit(solution)/shard_map/backward/pallas_call | solution.py:916
  215.7 8.9 %finish.1 = (bf16[512,768]{1,0:T(8,128)(2,1)}, f32[512,768]{1,0:T(8,128)}, f32[1,768,1536]{2,1,0:T(8,128)}, f32[1,768,1536]{2,1,0:T(8,128)}, f32[24,2304]{1,0:T(...) custom-call(bf16[512,768]{1,0:T(8,128)(2,1)} %get-tuple-element.59.m, ...), custom_call_target="tpu_custom_call" | custom-call | tf_op jit(solution)/shard_map/finish/pallas_call | solution.py:1012

commit v4 on v0

v4 whole, which is shorter than its diff:
```python
import functools
import jax
import jax.numpy as jnp
from jax import lax
from jax.experimental import pallas as pl
from jax.experimental.pallas import tpu as pltpu
from jax.sharding import PartitionSpec as P

MESH = pl.DeviceIdType.MESH
F32, BF16 = jnp.float32, jnp.bfloat16
NT = (((1,), (1,)), ((), ()))
EPSILON = 1e-06
PART = 384
WIDE = 768
LAG = (0, 1, 4, 99)


def dot(a, b, dims=(((1,), (0,)), ((), ()))):
    return lax.dot_general(a, b, dims, preferred_element_type=F32)


def exact(a, b, dims=(((1,), (0,)), ((), ()))):
    return lax.dot_general(a, b, dims, preferred_element_type=F32, precision=lax.Precision.HIGHEST)


def flipped(index, bits, count):
    result, bit = 0, 1
    while bit < count:
        result = result + bit * (((index // bit) % 2 + (bits // bit) % 2) % 2)
        bit *= 2
    return result


def gelu_parts(hidden):
    c0, c1 = 0.7978845608028654, 0.044715
    square = hidden * hidden
    bend = jnp.tanh(hidden * (c0 + (c0 * c1) * square))
    half = 0.5 + 0.5 * bend
    slope = half + (0.5 * hidden) * (1.0 - bend * bend) * (c0 + (3.0 * c0 * c1) * square)
    return hidden * half, slope


def slots_by_row(routes, me, pad, experts):
    count = routes.shape[1]
    picked = routes == lax.broadcasted_iota(jnp.int32, (experts, count), 0)
    first = lax.broadcasted_iota(jnp.int32, (count, count), 0)
    second = lax.broadcasted_iota(jnp.int32, (count, count), 1)
    before = dot(picked.astype(BF16), (first < second).astype(BF16))
    rank = jnp.sum(jnp.where(picked, before, 0.0), axis=0, keepdims=True).astype(jnp.int32)
    return jnp.bitwise_xor(routes, me) * pad + rank


def grow_strip(strip, w8):
    strip[0:8] = w8
    have = 8
    while have < strip.shape[0]:
        strip[have : 2 * have] = pltpu.roll(strip[0:have], have, 1)
        have *= 2


SPILLS = 7


def layer_kernel(n, cap, pad, experts, heads, direct, *refs):
    (tokens_ref, cot_ref, qkv_ref, att_ref, extra_ref, full_hbm, routes_ref, table_ref, buckets_hbm, win_hbm, wout_hbm,
     mixed_hbm, tokens_grad_hbm, qkv_grad_ref, att_grad_ref, extra_grad_ref, gain_grad_ref, bias_grad_ref,
     gin_hbm, gout_hbm, probs_hbm, *rest) = refs
    spilled, rest = rest[:SPILLS], rest[SPILLS:]
    (blocks, shard, gains, hot, router, rows, cots, ties, xin, cin, back_in, returned, tie_in, sib_recv,
     sib_in, in1, in2, bias_out, bias_in, bias_pair,
     put_sem, prob_sem, load_sem, pair_sem, swap_send, swap_recv, tree_send, tree_recv, turn_send, turn_recv,
     piece_send, piece_recv, piece_out, sib_s, sib_r, s1, r1, s2, r2, bias_s, bias_r, end_sem) = rest
    dp, me = lax.axis_index("dp"), lax.axis_index("expert")
    count, width = tokens_ref.shape
    total = n * pad
    early = 3 * width + 256
    sibling = (1 - dp, me)
    lane = lax.broadcasted_iota(jnp.int32, (count, 128), 1)

    def peer(p):
        return dp, flipped(me, p, n)

    def remote(src, dst, send, recv, device):
        return pltpu.make_async_remote_copy(
            src_ref=src, dst_ref=dst, send_sem=send, recv_sem=recv, device_id=device, device_id_type=MESH)

    def swap(kind, p):
        src, dst = ((rows, xin), (cots, cin), (rows, back_in), (cots, returned), (ties, tie_in))[kind]
        return remote(src.at[p], dst.at[p], swap_send.at[kind, p], swap_recv.at[kind, p], peer(p))

    def start_swaps(kind, wanted):
        def one(p, _):
            @pl.when(wanted(p))
            def _():
                swap(kind, p).start()
            return 0

        lax.fori_loop(1, n, one, 0)

    def greet_all():
        barrier = pltpu.get_barrier_semaphore()

        def greet(p, _):
            pl.semaphore_signal(barrier, inc=1, device_id=peer(p), device_id_type=MESH)
            return 0

        lax.fori_loop(1, n, greet, 0)
        pl.semaphore_signal(barrier, inc=1, device_id=sibling, device_id_type=MESH)
        pl.semaphore_wait(barrier, n)

    half = win_hbm.shape[1] // 2
    steps = half // WIDE
    pieces = [(kind, k) for k in range(steps) for kind in (0, 1)]

    def piece(kind, k):
        place = pl.ds((kind * steps + k) * WIDE, WIDE)
        return remote(blocks.at[:, place], sib_recv.at[kind, k], piece_send.at[kind, k], piece_recv.at[kind, k], sibling)

    def out_piece(kind, k):
        return pltpu.make_async_copy(
            sib_recv.at[kind, k], (gin_hbm, gout_hbm)[kind].at[:, pl.ds(k * WIDE, WIDE)], piece_out.at[kind, k])

    def forward(w, packed, normed, attended, middle, moe_in, chance, probs, strip, bias, ends, weights):
        puts = []

        def put(index, src):
            copy = pltpu.make_async_copy(src, spilled[index], put_sem.at[index])
            copy.start()
            puts.append(copy)

        offsets = [pltpu.make_async_copy(buckets_hbm.at[:, pl.ds(c, 128)], ends.at[i], load_sem.at[i])
                   for i, c in enumerate((0, count - 128))]
        for copy in offsets:
            copy.start()
        if direct:
            weights[:, : 3 * width] = qkv_ref[...].astype(F32)
            weights[:, 3 * width : early] = extra_ref[...].T[: weights.shape[0]]
            weights[:, early:] = att_ref[...].astype(F32)
        greet_all()
        if direct:
            own = weights.shape[0]
            block = 2 * own
            pair = remote(weights, shard, pair_sem.at[0], pair_sem.at[1], sibling)
            pair.start()
        else:
            load = pltpu.make_async_copy(full_hbm, w, pair_sem.at[0])
            load.start()
        slots = slots_by_row(routes_ref[...], me, pad, experts)

        def to_slots(values):
            hits = (slots == lax.broadcasted_iota(jnp.int32, (total, count), 0)).astype(BF16)
            return dot(hits, values).astype(BF16).reshape(n, pad, width)

        def make_cots():
            cots[...] = to_slots(cot_ref[...])
            cin[0] = cots[0]

        def make_bias():
            for copy in offsets:
                copy.wait()
            last, first = ends[1].astype(F32).T[127:128], ends[0].astype(F32).T[0:1]
            line = jnp.concatenate([last, pltpu.roll(first, count - 1, 1)], axis=1)
            line = pltpu.roll(jnp.broadcast_to(line, (8, 2 * count)), 2 * count - 127, 1)[0:1]
            hot[...] = (line.astype(jnp.int32) == lax.broadcasted_iota(jnp.int32, hot.shape, 0)).astype(F32)
            table = exact(table_ref[...], hot[...])
            for h in range(heads):
                row = jnp.broadcast_to(table[h : h + 1], (8, 2 * count))
                place = lax.broadcasted_iota(jnp.int32, row.shape, 0)
                shifted = row
                for r in range(1, 8):
                    shifted = jnp.where(place == r, pltpu.roll(row, r, 1), shifted)
                bias[h] = shifted

        if direct:
            pair.wait()
            mine, other = weights[...], shard[...]
            blocks[pl.ds(pl.multiple_of(me * block, 16), block), : w.shape[1]] = jnp.concatenate(
                [jnp.where(dp == 0, mine, other), jnp.where(dp == 0, other, mine)], axis=0).astype(BF16)
            second, third = 2 - dp, 1 + dp
            far = list(range(4, n, 4))
            near = [0] + far

            def at(t, r, core):
                start, size = ((0, early // 2), (early, width // 2))[t]
                return blocks.at[pl.ds(pl.multiple_of(flipped(me, r, n) * block, 16), block),
                                 pl.ds(pl.multiple_of(start + core * size, 128), size)]

            def hop(t, r, step):
                return remote(at(t, r, dp), at(t, r, dp), tree_send.at[t, r + step], tree_recv.at[t, r + step], peer(step))

            def arrived(t, r):
                remote(at(t, r, dp), at(t, r, dp), tree_send.at[t, r], tree_recv.at[t, r], peer(r)).wait_recv()

            def to_sibling(t, r, core):
                return remote(at(t, r, core), at(t, r, core), turn_send.at[t, r], turn_recv.at[t, r], sibling)

            def turn(t, step):
                if step == 0:
                    for r in far:
                        hop(t, 0, r).start()
                    hop(t, 0, third).start()
                    hop(t, 0, second).start()
                elif step == 1:
                    for r in far:
                        arrived(t, r)
                        hop(t, r, third).start()
                        hop(t, r, second).start()
                        to_sibling(t, r, dp).start()
                elif step == 2:
                    for r in near:
                        arrived(t, r + second)
                        hop(t, r + second, third).start()
                        to_sibling(t, r + second, dp).start()
                elif step == 3:
                    for r in near:
                        arrived(t, r + third)
                        to_sibling(t, r + third, dp).start()
                        arrived(t, r + 3)
                        to_sibling(t, r + 3, dp).start()
                else:
                    def settle(r, _):
                        to_sibling(t, r, 1 - dp).wait_recv()
                        return 0

                    lax.fori_loop(1, n, settle, 0)
                    place = (slice(0, early), slice(early, w.shape[1]))[t]
                    for core in (0, 1):
                        for q in range(n // 2):
                            low = 2 * q * block + core * own
                            pair_rows = [blocks[p : p + own, place].astype(F32) for p in (low, low + block)]
                            w[core * own * n + q * block : core * own * n + (q + 1) * block, place] = jnp.concatenate(
                                pair_rows, axis=0).astype(BF16)

            turn(0, 0)
            make_bias()
            make_cots()
            turn(0, 1)
            turn(1, 0)
            start_swaps(1, lambda p: p % 4 == 0)
            turn(0, 2)
            turn(1, 1)
            turn(0, 3)
            turn(1, 2)
            start_swaps(1, lambda p: p % 4 != 0)
            turn(0, 4)
        else:
            make_bias()
            make_cots()
            start_swaps(1, lambda p: p > 0)
            load.wait()
        gains[...] = w[:, 3 * width + 128 : early].astype(F32).T[0:8]
        router[...] = w[:, 3 * width : 3 * width + 128]
        x = tokens_ref[...].astype(F32)
        normed[...] = (x * lax.rsqrt(jnp.mean(x * x, axis=1, keepdims=True) + EPSILON) * gains[0:1]).astype(BF16)
        put(0, normed)
        for c in range(3):
            cols_c = slice(c * width, (c + 1) * width)
            packed[:, cols_c] = dot(normed[...], w[:, cols_c]).astype(BF16)
        put(1, packed)
        scale = (width // heads) ** -0.5

        def put_probs(k):
            return pltpu.make_async_copy(probs.at[pl.ds(2 * k, 2)], probs_hbm.at[pl.ds(2 * k, 2)], prob_sem.at[k])

        def attend(k, _):
            def part(c):
                return packed[:, pl.ds(pl.multiple_of(c * width + k * 128, 128), 128)]

            queries = (part(0).astype(F32) * scale).astype(BF16)
            keys = part(1)
            values = part(2).astype(F32).T.astype(BF16)
            outs = []
            for h in (0, 1):
                grow_strip(strip, bias[2 * k + h])
                own_keys = jnp.where((lane < 64) == (h == 0), keys, jnp.zeros_like(keys))
                scores = dot(own_keys, queries, NT)
                scores = jnp.concatenate(
                    [scores[128 * b : 128 * b + 128] + strip[:, 384 - 128 * b : 896 - 128 * b] for b in range(4)], axis=0)
                powers = jnp.exp(scores - jnp.max(scores, axis=0, keepdims=True))
                part_weights = (powers * (1.0 / jnp.sum(powers, axis=0, keepdims=True))).astype(BF16)
                probs[2 * k + h] = part_weights
                outs.append(dot(values[64 * h : 64 * h + 64], part_weights))
            put_probs(k).start()
            attended[:, pl.ds(pl.multiple_of(k * 128, 128), 128)] = jnp.concatenate(outs, axis=0).T.astype(BF16)
            if direct:
                for step in (3, 4):
                    @pl.when(k == step + 1)
                    def _():
                        turn(1, step)
            return 0

        lax.fori_loop(0, heads // 2, attend, 0)
        mid = tokens_ref[...].astype(F32) + dot(attended[...], w[:, early:])
        middle[...] = mid
        moe = (mid * lax.rsqrt(jnp.mean(mid * mid, axis=1, keepdims=True) + EPSILON) * gains[1:2]).astype(BF16)
        moe_in[...] = moe
        rows[...] = to_slots(moe)
        start_swaps(0, lambda p: (p < 4) | ((p % 4 == 0) & (p < 12)))
        xin[0] = rows[0]
        put(2, attended)
        put(3, middle)
        put(4, moe_in)
        put(5, w)
        logits = dot(moe, router[...])
        logits = jnp.where(lane < experts, logits, -1e30)
        powers = jnp.exp(logits - jnp.max(logits, axis=1, keepdims=True))
        chance[...] = powers / jnp.sum(powers, axis=1, keepdims=True)
        put(6, chance)
        if direct:
            for t in (0, 1):
                for r in far:
                    hop(t, 0, r).wait_send()
                for r in near:
                    hop(t, r, second).wait_send()
                    hop(t, r, third).wait_send()
                    hop(t, r + second, third).wait_send()

                def settle_sends(r, _):
                    to_sibling(t, r, dp).wait_send()
                    return 0

                lax.fori_loop(1, n, settle_sends, 0)
        for copy in puts:
            copy.wait()
        for k in range(heads // 2):
            put_probs(k).wait()

    def experts_both(win, wout, xt, rt, act, hgr):
        ff = win.shape[1]
        per = 256 // cap
        group_rows = per * cap
        chunk = 1024
        loads = [pltpu.make_async_copy(win_hbm, win, load_sem.at[0]), pltpu.make_async_copy(wout_hbm, wout, load_sem.at[1])]
        for load in loads:
            load.start()

        def packed_rows(ref, g):
            block = ref[pl.ds(g * per, per)].reshape(per * pad, width)
            if pad == cap:
                return block
            r = lax.broadcasted_iota(jnp.int32, (group_rows, per * pad), 0)
            c = lax.broadcasted_iota(jnp.int32, (group_rows, per * pad), 1)
            return dot(((r // cap) * pad + r % cap == c).astype(BF16), block).astype(BF16)

        def spread_rows(block):
            if pad == cap:
                return block.reshape(per, pad, width)
            r = lax.broadcasted_iota(jnp.int32, (per * pad, group_rows), 0)
            c = lax.broadcasted_iota(jnp.int32, (per * pad, group_rows), 1)
            pick = (r // pad == c // cap) & (r % pad == c % cap)
            return dot(pick.astype(BF16), block).astype(BF16).reshape(per, pad, width)

        def group(g, _):
            def over(first, act_on):
                def one(j, _):
                    @pl.when(g * per + j != 0)
                    def _():
                        act_on(g * per + j)
                    return 0

                lax.fori_loop(first, per, one, 0)

            @pl.when(g == 0)
            def _():
                for p in (1, 2, 3):
                    swap(0, p).wait_recv()
                start_swaps(0, lambda p: (p >= 4) & (p % 4 != 0) & (p < 12))
                for load in loads:
                    load.wait()
                over(4, lambda p: swap(0, p).wait_recv())

            @pl.when(g != 0)
            def _():
                over(0, lambda p: swap(0, p).wait_recv())

            @pl.when(g == 1)
            def _():
                start_swaps(0, lambda p: p >= 12)

            over(0, lambda p: swap(1, p).wait_recv())
            here = pl.ds(pl.multiple_of(g * group_rows, group_rows), group_rows)
            x = packed_rows(xin, g)
            logits = dot(x, router[...])
            lanes = lax.broadcasted_iota(jnp.int32, logits.shape, 1)
            logits = jnp.where(lanes < experts, logits, -1e30)
            powers = jnp.exp(logits - jnp.max(logits, axis=1, keepdims=True))
            gate = jnp.sum(jnp.where(lanes == me, powers, 0.0), axis=1, keepdims=True) / jnp.sum(
                powers, axis=1, keepdims=True)
            r = (gate * packed_rows(cin, g).astype(F32)).astype(BF16)
            xt[:, here] = x.T
            rt[:, here] = r.T

            def hidden_chunk(k, _):
                cols = pl.ds(pl.multiple_of(k * chunk, chunk), chunk)
                value, slope = gelu_parts(dot(x, win[:, cols]))
                act[here, cols] = value.astype(BF16)
                hgr[here, cols] = (dot(r, wout[:, cols]) * slope).astype(BF16)
                return 0

            lax.fori_loop(0, ff // chunk, hidden_chunk, 0)
            back = spread_rows(dot(hgr[here], win[...], NT).astype(BF16))
            over(0, lambda p: swap(0, p).wait_send())
            rows[pl.ds(g * per, per)] = back
            over(0, lambda p: swap(2, p).start())
            produced = dot(act[here], wout[...], NT).astype(BF16)
            tie = jnp.sum(r.astype(F32) * produced.astype(F32), axis=1, keepdims=True)
            for j in range(per):
                row = jnp.broadcast_to(tie[j * cap : (j + 1) * cap], (cap, 128)).T[0:8]
                ties[g * per + j] = jnp.concatenate([row, jnp.zeros((8, 128 - cap), F32)], axis=1)
            over(0, lambda p: swap(4, p).start())
            over(0, lambda p: swap(1, p).wait_send())
            cots[pl.ds(g * per, per)] = spread_rows(produced)

            @pl.when(g < n // per // 2)
            def _():
                over(0, lambda p: swap(3, p).start())

            return 0

        lax.fori_loop(0, n // per, group, 0)
        back_in[0] = rows[0]
        tie_in[0] = ties[0]
        returned[0] = cots[0]

        def partial(kind, owner, k):
            cols = pl.ds(pl.multiple_of(owner * half + k * WIDE, 128), WIDE)
            return dot(xt[...], hgr[:, cols]) if kind == 0 else dot(rt[...], act[:, cols])

        for kind, k in pieces:
            place = (kind * steps + k) * WIDE
            blocks[:, place : place + WIDE] = partial(kind, 1 - dp, k).astype(BF16)
            piece(kind, k).start()
        for kind, k in pieces:
            value = partial(kind, dp, k)
            piece(kind, k).wait_recv()
            sib_recv[kind, k] = (value + sib_recv[kind, k].astype(F32)).astype(BF16)
            out_piece(kind, k).start()

    def backward(w, packed, normed, attended, middle, moe_in, chance, prob, mid_grad, att_cot, packed_grad, normed_t, chunk,
                 strip, bias_rows, sib_out, mine, out1, keep, out2):
        loaded = (normed, packed, attended, middle, moe_in, w, chance)
        loads = [pltpu.make_async_copy(spilled[i], loaded[i], load_sem.at[i]) for i in range(SPILLS)]
        order = (6, 3, 5, 2, 4, 0, 1)
        for i in order:
            loads[i].start()

        def fetch(k):
            return pltpu.make_async_copy(probs_hbm.at[pl.ds(2 * k, 2)], prob.at[k % 2], prob_sem.at[k % 2])

        fetch(0).start()
        own = qkv_ref.shape[0]
        lead = (width + 256 + PART - 1) // PART
        chunks = lead + heads // 2

        if direct:
            half_rows = own * n

            def hop(stage, k, d):
                if stage == 0:
                    return remote(sib_out.at[k], sib_in.at[k], sib_s.at[k], sib_r.at[k], sibling)
                if stage == 1:
                    return remote(out1.at[k, d - 1], in1.at[k, d - 1], s1.at[k, d - 1], r1.at[k, d - 1], peer(d))
                return remote(out2.at[k, d - 1], in2.at[k, d - 1], s2.at[k, d - 1], r2.at[k, d - 1], peer(4 * d))

            def owners(k, d):
                places = [pl.multiple_of(flipped(me, d + 4 * z, n) * own, 8) for z in range(4)]
                return jnp.concatenate([mine[k % 2, pl.ds(place, own)] for place in places], axis=0)

            def stage(s, k):
                if s == 0:
                    there = pl.ds(pl.multiple_of((1 - dp) * half_rows, 8), half_rows)
                    here = pl.ds(pl.multiple_of(dp * half_rows, 8), half_rows)
                    sib_out[k] = chunk[there].astype(BF16)
                    hop(0, k, 0).start()
                    mine[k % 2] = chunk[here]
                elif s == 1:
                    hop(0, k, 0).wait_recv()
                    mine[k % 2] = mine[k % 2] + sib_in[k].astype(F32)
                    for d in (3, 1, 2):
                        out1[k, d - 1] = owners(k, d).astype(BF16)
                        hop(1, k, d).start()
                    keep[k] = owners(k, 0)
                elif s == 2:
                    for d in (1, 2, 3):
                        hop(1, k, d).wait_recv()
                    total_rows = keep[k] + (in1[k, 0].astype(F32) + in1[k, 1].astype(F32)) + in1[k, 2].astype(F32)
                    for z in (3, 2, 1):
                        block = total_rows[own * z : own * (z + 1)]
                        out2[k, z - 1] = jnp.concatenate(
                            [block[:, 128 * c : 128 * (c + 1)] for c in range(3)]
                            + [jnp.zeros((out2.shape[2] - 3 * own, 128), F32)], axis=0).astype(BF16)
                        hop(2, k, z).start()
                    keep[k, :own] = total_rows[:own]
                else:
                    for z in (1, 2, 3):
                        hop(2, k, z).wait_recv()
                    far = (in2[k, 0].astype(F32) + in2[k, 1].astype(F32)) + in2[k, 2].astype(F32)
                    keep[k, :own] = keep[k, :own] + jnp.concatenate(
                        [far[own * c : own * (c + 1)] for c in range(3)], axis=1)

            def advance(k):
                stage(0, k)
                for s in range(1, 4):
                    @pl.when((k - LAG[s] >= 0) & (k - LAG[s] < chunks))
                    def _():
                        stage(s, k - LAG[s])

            done = {k: max(s for s in range(4) if LAG[s] <= chunks - 1 - k) for k in range(chunks)}

            def drain(last, *which):
                for k in which or range(chunks):
                    while done[k] < last:
                        done[k] += 1
                        stage(done[k], k)

        else:
            def advance(k):
                copy = pltpu.make_async_copy(chunk, qkv_grad_ref.at[k], end_sem.at[0])
                copy.start()
                copy.wait()

            def drain(*_):
                pass

        expert_of = jnp.broadcast_to(routes_ref[...].astype(F32), (128, count)).T[:, 0:1].astype(jnp.int32)
        picked = expert_of == lane
        first = lax.broadcasted_iota(jnp.int32, (count, count), 0)
        other = lax.broadcasted_iota(jnp.int32, (count, count), 1)
        before = dot((other < first).astype(BF16), picked.astype(BF16))
        rank = jnp.sum(jnp.where(picked, before, 0.0), axis=1, keepdims=True).astype(jnp.int32)
        place = jnp.bitwise_xor(expert_of, me)
        hits = (place * pad + rank == lax.broadcasted_iota(jnp.int32, (count, total), 1)).astype(BF16)

        def each_peer(act_on):
            def one(p, _):
                act_on(p)
                return 0

            lax.fori_loop(1, n, one, 0)

        def arrive(p):
            swap(2, p).wait_recv()
            swap(4, p).wait_recv()

        each_peer(arrive)
        ties_row = exact((place == lax.broadcasted_iota(jnp.int32, (count, n), 1)).astype(F32), jnp.max(tie_in[...], axis=1))
        tie = jnp.sum(jnp.where(lane == rank, ties_row, 0.0), axis=1, keepdims=True)
        for i in order[:1]:
            loads[i].wait()
        logit_grad = (tie * (picked.astype(F32) - chance[...])).astype(BF16)
        grad = dot(hits, back_in[...].reshape(total, width))
        for i in order[1:]:
            loads[i].wait()
        grad = grad + dot(logit_grad, router[...], NT)
        mid = middle[...]
        root = lax.rsqrt(jnp.mean(mid * mid, axis=1, keepdims=True) + EPSILON)
        unit_mid = mid * root
        gain_rows = jnp.sum(grad * unit_mid, axis=0, keepdims=True)
        scaled = grad * gains[1:2]
        mid_g = cot_ref[...].astype(F32) + root * (scaled - unit_mid * jnp.mean(scaled * unit_mid, axis=1, keepdims=True))
        mid_grad[...] = mid_g
        attn_grad = mid_g.astype(BF16)
        att_cot[...] = dot(attn_grad, w[:, early:], NT).astype(BF16)
        attended_t = attended[...].T
        for k in range(lead):
            if (k + 1) * PART <= width:
                chunk[...] = dot(attended_t, attn_grad[:, k * PART : (k + 1) * PART])
            else:
                chunk[:, 0:128] = dot(moe_in[...].T, logit_grad)
                chunk[:, 128:256] = jnp.broadcast_to(gain_rows, (128, width)).T
                chunk[:, 256:] = jnp.zeros((width, PART - 256), F32)
            advance(k)
        normed_t[...] = normed[...].T
        each_peer(lambda p: swap(2, p).wait_send())
        start_swaps(3, lambda p: p >= n // 2)

        scale = (width // heads) ** -0.5

        def attend_back(k, _):
            fetch(k).wait()

            @pl.when(k + 1 < heads // 2)
            def _():
                fetch(k + 1).start()

            def part(c):
                return packed[:, pl.ds(pl.multiple_of(c * width + k * 128, 128), 128)]

            queries, keys, values = part(0), part(1), part(2)
            keys_t = (keys.astype(F32) * scale).T.astype(BF16)
            cot = att_cot[:, pl.ds(pl.multiple_of(k * 128, 128), 128)]
            query_t, key_g, value_g = [], None, None
            for h in (0, 1):
                mask = (lane < 64) == (h == 0)
                own_cot = jnp.where(mask, cot, jnp.zeros_like(cot))
                own_queries = jnp.where(mask, queries, jnp.zeros_like(queries))
                weights = prob[k % 2, h]
                chances = weights.astype(F32)
                product = chances * dot(values, own_cot, NT)
                score_grad = (product - chances * jnp.sum(product, axis=0, keepdims=True)).astype(BF16)
                wide = score_grad.astype(F32)
                for b in range(4):
                    block = wide[128 * b : 128 * b + 128]
                    cols = slice(384 - 128 * b, 896 - 128 * b)
                    if b == 0:
                        strip[:, cols] = block
                        strip[:, 0:384] = jnp.zeros((128, 384), F32)
                        strip[:, 896:1024] = jnp.zeros((128, 128), F32)
                    else:
                        strip[:, cols] += block
                have = 64
                folded = strip[...]
                while have >= 8:
                    folded = folded[:have] + pltpu.roll(folded[have:], 1024 - have, 1)
                    have //= 2
                for s in range(1, 8):
                    folded = jnp.where(lax.broadcasted_iota(jnp.int32, folded.shape, 0) == s,
                                       pltpu.roll(folded, 1024 - s, 1), folded)
                bias_rows[2 * k + h] = folded
                v = dot(weights, own_cot)
                q = dot(score_grad, own_queries)
                value_g = v if h == 0 else value_g + v
                key_g = q if h == 0 else key_g + q
                query_t.append(dot(keys_t[64 * h : 64 * h + 64], score_grad))
            query_g = jnp.concatenate(query_t, axis=0).T.astype(BF16)
            grads = jnp.concatenate([query_g, (key_g * scale).astype(BF16), value_g.astype(BF16)], axis=1)
            for c in range(3):
                packed_grad[:, pl.ds(pl.multiple_of(c * width + k * 128, 128), 128)] = grads[:, c * 128 : (c + 1) * 128]
            chunk[...] = dot(normed_t[...], grads)
            advance(k + lead)
            return 0

        lax.fori_loop(0, heads // 2, attend_back, 0)
        drain(1, chunks - 1)
        drain(2, *range(chunks - 1))
        sums = jnp.concatenate([jnp.sum(bias_rows[h], axis=0, keepdims=True) for h in range(heads)], axis=0)
        bias_out[...] = exact(sums, hot[...], NT)
        if direct:
            pair_hop = remote(bias_out, bias_pair, pair_sem.at[2], pair_sem.at[3], sibling)
            pair_hop.start()

            def bias_hop(p):
                return remote(bias_in.at[me], bias_in.at[me], bias_s.at[p], bias_r.at[p], peer(p))

            def bias_arrived(p):
                there = flipped(me, p, n)
                return remote(bias_in.at[there], bias_in.at[there], bias_s.at[p], bias_r.at[p], (dp, there))

        normed_grad = dot(packed_grad[...], w[:, : 3 * width], NT)
        drain(2)
        if direct:
            pair_hop.wait()
            bias_in[me] = bias_out[...] + bias_pair[...]
            each_peer(lambda p: bias_hop(p).start())
        x = tokens_ref[...].astype(F32)
        root = lax.rsqrt(jnp.mean(x * x, axis=1, keepdims=True) + EPSILON)
        unit_x = x * root
        scaled = normed_grad * gains[0:1]
        mid_grad[...] = mid_grad[...] + root * (scaled - unit_x * jnp.mean(scaled * unit_x, axis=1, keepdims=True))
        ends = [pltpu.make_async_copy(mid_grad, tokens_grad_hbm, end_sem.at[0]),
                pltpu.make_async_copy(att_cot, mixed_hbm, end_sem.at[1])]
        ends[0].start()
        each_peer(lambda p: swap(3, p).wait_recv())
        gate = jnp.sum(jnp.where(picked, chance[...], 0.0), axis=1, keepdims=True)
        att_cot[...] = (middle[...] + gate * dot(hits, returned[...].reshape(total, width))).astype(BF16)
        ends[1].start()
        if direct:
            drain(3)
            each_peer(lambda p: bias_arrived(p).wait_recv())
            total_bias = bias_in[0]
            for p in range(1, n):
                total_bias = total_bias + bias_in[p]
            bias_grad_ref[...] = total_bias
            for k in range(chunks):
                result = keep[k, :own]
                if k >= lead:
                    for c in range(3):
                        start = c * width + (k - lead) * 128
                        qkv_grad_ref[:, start : start + 128] = result[:, c * 128 : (c + 1) * 128]
                elif (k + 1) * PART <= width:
                    att_grad_ref[:, k * PART : (k + 1) * PART] = result
                else:
                    extra_grad_ref[...] = result[:, :256]
            total_gain = jnp.sum(qkv_grad_ref[...] * qkv_ref[...].astype(F32), axis=1, keepdims=True)
            gain_grad_ref[...] = jnp.broadcast_to(total_gain / extra_ref[128:256].T[:own, 0:1], gain_grad_ref.shape)

            def settle_sends(k, _):
                hop(0, k, 0).wait_send()
                for d in (1, 2, 3):
                    hop(1, k, d).wait_send()
                    hop(2, k, d).wait_send()
                return 0

            lax.fori_loop(0, chunks, settle_sends, 0)
            each_peer(lambda p: bias_hop(p).wait_send())
        else:
            bias_grad_ref[...] = bias_out[...]
        for kind in (3, 4):
            each_peer(lambda p: swap(kind, p).wait_send())
        for copy in ends:
            copy.wait()
        for kind, k in pieces:
            piece(kind, k).wait_send()
            out_piece(kind, k).wait()

    wide = w_columns(width)
    scratch = pltpu.VMEM
    shared = [
        scratch((width, wide), BF16), scratch((count, 3 * width), BF16), scratch((count, width), BF16),
        scratch((count, width), BF16), scratch((count, width), F32), scratch((count, width), BF16), scratch((count, 128), F32),
    ]
    own_rows = qkv_ref.shape[0]
    pl.run_scoped(
        forward, *shared, scratch((heads, count, count), BF16), scratch((128, 2 * count), F32),
        scratch((heads, 8, 2 * count), F32), scratch((2, count, 128), jnp.int32),
        scratch((own_rows, wide) if direct else (8, 128), F32))
    pl.run_scoped(
        experts_both, *[scratch((width, win_hbm.shape[1]), BF16) for _ in range(2)],
        *[scratch((width, n * cap), BF16) for _ in range(2)], *[scratch((n * cap, win_hbm.shape[1]), BF16) for _ in range(2)])
    all_chunks = (width + 256 + PART - 1) // PART + heads // 2

    def buffer(shape, kind):
        return scratch((all_chunks, *shape) if direct else (8, 128), kind)

    pl.run_scoped(
        backward, *shared, scratch((2, 2, count, count), BF16), scratch((count, width), F32), scratch((count, width), BF16),
        scratch((count, 3 * width), BF16), scratch((width, count), BF16), scratch((width, PART), F32),
        scratch((128, 2 * count), F32), scratch((heads, 8, 2 * count), F32),
        buffer((own_rows * n, PART), BF16), scratch((2, own_rows * n, PART), F32), buffer((3, 4 * own_rows, PART), BF16),
        buffer((4 * own_rows, PART), F32), buffer((3, -(-3 * own_rows // 16) * 16, 128), BF16))


def w_columns(width):
    return 4 * width + 256


def layer(n, cap, pad, experts, heads, direct, tokens, cotangent, qkv, att, extra, full, routes, table, buckets, win, wout):
    count, width = tokens.shape
    wide = w_columns(width)
    own = qkv.shape[0]
    kinds = table.shape[1]
    ff = win.shape[1]
    chunks = (width + 256 + PART - 1) // PART + heads // 2
    steps = ff // 2 // WIDE
    short = -(-3 * own // 16) * 16
    any_ = pl.BlockSpec(memory_space=pl.ANY)
    vmem = pl.BlockSpec(memory_space=pltpu.VMEM)
    dma = pltpu.SemaphoreType.DMA
    scratch = pltpu.VMEM
    shape = jax.ShapeDtypeStruct

    def landing(*rest):
        return scratch((chunks, *rest) if direct else (16, 128), BF16)

    outs = [
        (shape((count, width), BF16), any_), (shape((count, width), F32), any_),
        (shape((own, 3 * width), F32), vmem) if direct else (shape((chunks, width, PART), F32), any_),
        (shape((own, width), F32), vmem), (shape((own, 256), F32), vmem), (shape((own, 128), F32), vmem),
        (shape((heads, kinds), F32), vmem), (shape((width, ff // 2), BF16), any_), (shape((width, ff // 2), BF16), any_),
        (shape((heads, count, count), BF16), any_), (shape((count, width), BF16), any_),
        (shape((count, 3 * width), BF16), any_), (shape((count, width), BF16), any_), (shape((count, width), F32), any_),
        (shape((count, width), BF16), any_), (shape((width, wide), BF16), any_), (shape((count, 128), F32), any_),
    ]
    slots = scratch((n, pad, width), BF16)
    return pl.pallas_call(
        functools.partial(layer_kernel, n, cap, pad, experts, heads, direct),
        out_shape=tuple(o[0] for o in outs),
        in_specs=[vmem] * 5 + [any_, vmem, vmem, any_, any_, any_],
        out_specs=tuple(o[1] for o in outs),
        scratch_shapes=[
            scratch((width, max(wide, 2 * steps * WIDE)), BF16),
            scratch((own, wide) if direct else (8, 128), F32),
            scratch((8, width), F32), scratch((kinds, 2 * count), F32), scratch((width, 128), BF16),
            slots, slots, scratch((n, 8, 128), F32), slots, slots, slots, slots, scratch((n, 8, 128), F32),
            scratch((2, steps, width, WIDE), BF16),
            landing(own * n, PART), landing(3, 4 * own, PART), landing(3, short, 128),
            scratch((heads, kinds), F32), scratch((n, heads, kinds), F32), scratch((heads, kinds), F32),
            dma((SPILLS,)), dma((heads // 2,)), dma((SPILLS,)), dma((4,)), dma((5, n)), dma((5, n)),
            dma((2, n)), dma((2, n)), dma((2, n)), dma((2, n)),
            dma((2, steps)), dma((2, steps)), dma((2, steps)),
            dma((chunks,)), dma((chunks,)), *[dma((chunks, 3)) for _ in range(4)], dma((n,)), dma((n,)), dma((2,)),
        ],
        compiler_params=pltpu.CompilerParams(
            collective_id=1, has_side_effects=True, vmem_limit_bytes=63 * 1024 * 1024),
        name="layer",
    )(tokens, cotangent, qkv, att, extra, full, routes, table, buckets, win, wout)


def finish_kernel(
    mixed_in, tokens_in, in_hbm, out_hbm, qkv_in, att_in, extra_in, gain_in, bias_in,
    mixed_out, tokens_out, in_out, out_out, qkv_out, att_out, router_out, gain_out, gain_moe_out, bias_out,
    mixed, tokens, narrow, wide, sem, load_sem, store_sem,
):
    ins = [pltpu.make_async_copy(mixed_in, mixed, sem.at[0]), pltpu.make_async_copy(tokens_in, tokens, sem.at[1])]
    outs = [pltpu.make_async_copy(mixed, mixed_out, sem.at[2]), pltpu.make_async_copy(tokens, tokens_out, sem.at[3])]
    parts, rows = narrow.shape[1], narrow.shape[2]

    def load(kind, k):
        return pltpu.make_async_copy(
            (in_hbm, out_hbm)[kind].at[pl.ds(k * rows, rows)], narrow.at[kind, k], load_sem.at[kind, k])

    def store(kind, k):
        return pltpu.make_async_copy(
            wide.at[kind, k], (in_out, out_out)[kind].at[0, pl.ds(k * rows, rows)], store_sem.at[kind, k])

    for k in range(parts):
        for kind in (0, 1):
            load(kind, k).start()
    for copy in ins:
        copy.start()
    qkv_out[...] = qkv_in[...]
    att_out[...] = att_in[...]
    router_out[...] = extra_in[:, :128].T[: router_out.shape[0]]
    gain_out[...] = gain_in[...].T[0:1]
    gain_moe_out[...] = extra_in[:, 128:].T[0:1]
    bias_out[...] = bias_in[...]
    for k in range(parts):
        for kind in (0, 1):
            load(kind, k).wait()
            wide[kind, k] = narrow[kind, k].astype(F32)
            store(kind, k).start()
    for copy_in, copy_out in zip(ins, outs):
        copy_in.wait()
        copy_out.start()
    for k in range(parts):
        for kind in (0, 1):
            store(kind, k).wait()
    for copy in outs:
        copy.wait()


def finish(experts, mixed, tokens_grad, grad_in, grad_out, qkv, att, extra, gain, bias):
    any_ = pl.BlockSpec(memory_space=pl.ANY)
    vmem = pl.BlockSpec(memory_space=pltpu.VMEM)
    dma = pltpu.SemaphoreType.DMA
    parts = 8
    rows = grad_in.shape[0] // parts
    own = qkv.shape[0]
    shape = jax.ShapeDtypeStruct
    return pl.pallas_call(
        finish_kernel,
        out_shape=(
            shape(mixed.shape, BF16), shape(tokens_grad.shape, F32), shape((1, *grad_in.shape), F32),
            shape((1, *grad_out.shape), F32), shape(qkv.shape, F32), shape(att.shape, F32), shape((experts, own), F32),
            shape((1, own), F32), shape((1, own), F32), shape(bias.shape, F32),
        ),
        in_specs=[any_] * 4 + [vmem] * 5,
        out_specs=tuple([any_] * 4 + [vmem] * 6),
        scratch_shapes=[
            pltpu.VMEM(mixed.shape, BF16),
            pltpu.VMEM(tokens_grad.shape, F32),
            pltpu.VMEM((2, parts, rows, grad_in.shape[1]), BF16),
            pltpu.VMEM((2, parts, rows, grad_in.shape[1]), F32),
            dma((4,)), dma((2, parts)), dma((2, parts)),
        ],
        compiler_params=pltpu.CompilerParams(vmem_limit_bytes=60 * 1024 * 1024),
        name="finish",
    )(mixed, tokens_grad, grad_in, grad_out, qkv, att, extra, gain, bias)


def shards(
    n, tokens, cotangent, routes, buckets, gain_attn, w_qkv, w_att, rel_bias, gain_moe, w_router, w_in, w_out,
):
    axes = ("dp", "expert")
    count, width = tokens.shape
    experts = w_router.shape[1]
    heads = rel_bias.shape[1]
    own = w_qkv.shape[0]
    cap = max(2, 2 * count // experts)
    pad = max(16, cap)
    direct = n == 16 and own % 8 == 0
    extra = sum(jnp.pad(part.astype(F32), ((low, 256 - low - part.shape[0]), (0, 128 - own)))
                for low, part in ((0, w_router.T), (128, gain_attn[None]), (129, gain_moe[None])))
    full = w_att if direct else lax.all_gather(
        jnp.concatenate([w_qkv, extra[:, :own].T.astype(BF16), w_att], axis=1), axes, axis=0, tiled=True)
    mixed, grad_tokens, grad_qkv, grad_att, grad_extra, grad_gain, grad_bias, grad_in, grad_out = layer(
        n, cap, pad, experts, heads, direct, tokens, cotangent, w_qkv, w_att, extra, full, routes.T, rel_bias.T, buckets,
        w_in[0], w_out[0])[:9]
    if not direct:
        lead = grad_qkv.shape[0] - heads // 2
        early = jnp.concatenate([grad_qkv[k] for k in range(lead)], axis=1)
        late = [grad_qkv[lead:, :, c * 128 : (c + 1) * 128].transpose(1, 0, 2).reshape(width, width) for c in range(3)]
        both = lax.psum_scatter(jnp.concatenate([early, *late], axis=1), axes, scatter_dimension=0, tiled=True)
        grad_att, grad_extra = both[:, :width], both[:, width : width + 256]
        grad_qkv = both[:, early.shape[1] :]
        grad_gain = jnp.sum(grad_qkv * w_qkv.astype(F32), axis=1, keepdims=True) / gain_attn.astype(F32)[:, None]
        grad_gain = jnp.broadcast_to(grad_gain, (own, 128))
        grad_bias = lax.psum(grad_bias, axes)
    mixed, grad_tokens, grad_in, grad_out, grad_qkv, grad_att, grad_router, grad_gain, grad_gain_moe, grad_bias = finish(
        experts, mixed, grad_tokens, grad_in, grad_out, grad_qkv, grad_att, grad_extra, grad_gain, grad_bias)
    return (
        mixed, grad_tokens, grad_gain.reshape(own), grad_qkv, grad_att, grad_bias.T, grad_gain_moe.reshape(own), grad_router.T,
        grad_in, grad_out,
    )


def solution(mesh):
    both = P(("dp", "expert"))
    return jax.shard_map(
        functools.partial(shards, mesh.shape["expert"]),
        mesh=mesh,
        in_specs=(both, both, both, P(), both, both, both, P(), both, both, P("expert"), P("expert")),
        out_specs=(both, both, both, both, both, P(), both, both, P("expert", None, "dp"), P("expert", None, "dp")),
        check_vma=False,
    )
```

time: 697 us -> 205 us (0.29); the launches traced: 688 us -> 205 us
  blocking collectives: 217 us -> 0 us
  Pallas kernels: 0 us -> 203 us
  waiting for transfers between devices: 198 us -> 0 us
  matrix products: 130 us -> 0 us
  local copies, waits for them, and re-layouts: 71.1 us -> 0 us
  other arithmetic: 34.6 us -> 1.38 us
  starting transfers between devices: 22.5 us -> 0 us
  between operations: 15.1 us -> 0.83 us
    pallas_call x0 -> x2, Pallas kernels: none -> 203 us  [the longest x1 194 us: layer(): pl.pallas_call(functools.partial(layer_kernel, n, cap, pad, experts, head...]
    dot_general x23 -> x0, matrix products: 130 us -> none  [the longest x1 15.3 us: shards(): jnp.einsum('nmd,df->nmf', grad_rows, expert_out, preferred_element_type=j...]
    reduce_scatter x4 -> x0, waiting for transfers between devices: 111 us -> none  [the longest x1 111 us: shards(): lax.psum_scatter(qkv_weight_grad, ('dp', 'expert'), scatter_dimension=0,...]
    all_gather x1 -> x0, blocking collectives: 87.9 us -> none  [shards(): lax.all_gather(w_router, ('dp', 'expert'), axis=0, tiled=True)]
    unnamed x2 -> x0, blocking collectives: 86.1 us -> none
    all_to_all x4 -> x0, waiting for transfers between devices: 66.5 us -> none  [the longest x1 33.4 us: shards(): lax.all_to_all(row_back, 'expert', split_axis=0, concat_axis=0, tiled=True)]
    all_to_all x1 -> x0, blocking collectives: 42.6 us -> none  [shards(): lax.all_to_all(outgoing, 'expert', split_axis=0, concat_axis=0, tiled=True)]
    all_to_all x4 -> x0, starting transfers between devices: 22.3 us -> none  [the longest x1 7.05 us: shards(): lax.all_to_all(grad_slots, 'expert', split_axis=0, concat_axis=0, tiled=T...]
  transfers between devices with their start and end apart: 10 -> 0, of which waited for: 4 -> 0; matrix products, arithmetic and copies ran while one was open for 26% -> 0% of each run, Pallas kernels for 0% -> 0%
where the time goes in v4:
time: 205 us
  Pallas kernels  203 us (99%)
    pallas_call x1, Pallas kernels, layer(): pl.pallas_call(functools.partial(layer_kernel, n, cap, pad, experts, head...  194 us
    pallas_call x1, Pallas kernels, finish(): pl.pallas_call(finish_kernel, out_shape=(shape(mixed.shape, BF16), shape(...  8.9 us

profile of v4, /device:TPU:0, one launch (start us, length us, event | category | flops | bytes accessed | tf_op | source)
XLA Modules:
  0.0 205.1 jit_solution(4419017242036081483)
XLA Ops:
  0.6 1.4 convert_add_fusion.refs_4_
  2.0 194.0 %layer.1 = (bf16[512,768]{1,0:T(8,128)(2,1)}, f32[512,768]{1,0:T(8,128)}, f32[24,2304]{1,0:T(8,128)}, f32[24,768]{1,0:T(8,128)}, f32[24,256]{1,0:T(8,128)}, /*in...) custom-call(bf16[512,768]{1,0:T(8,128)(2,1)} %refs_0_.1, ...), custom_call_target="tpu_custom_call" | custom-call | tf_op jit(solution)/shard_map/layer/pallas_call | solution.py:765
  196.0 8.9 %finish.1 = (bf16[512,768]{1,0:T(8,128)(2,1)}, f32[512,768]{1,0:T(8,128)}, f32[1,768,1536]{2,1,0:T(8,128)}, f32[1,768,1536]{2,1,0:T(8,128)}, f32[24,2304]{1,0:T(...) custom-call(bf16[512,768]{1,0:T(8,128)(2,1)} %get-tuple-element.29.m, ...), custom_call_target="tpu_custom_call" | custom-call | tf_op jit(solution)/shard_map/finish/pallas_call | solution.py:840

commit v5 on v4

--- a/solution.py
+++ b/solution.py
@@ -12,7 +12,7 @@
 EPSILON = 1e-06
 PART = 384
 WIDE = 768
-LAG = (0, 1, 4, 99)
+LAG = (0, 1, 3, 5, 99, 99)
 
 
 def dot(a, b, dims=(((1,), (0,)), ((), ()))):
@@ -67,14 +67,16 @@
      gin_hbm, gout_hbm, probs_hbm, *rest) = refs
     spilled, rest = rest[:SPILLS], rest[SPILLS:]
     (blocks, shard, gains, hot, router, rows, cots, ties, xin, cin, back_in, returned, tie_in, sib_recv,
-     sib_in, in1, in2, bias_out, bias_in, bias_pair,
+     sib_in, in1, in2, in3, in4, bias_out, bias_in, bias_pair,
      put_sem, prob_sem, load_sem, pair_sem, swap_send, swap_recv, tree_send, tree_recv, turn_send, turn_recv,
-     piece_send, piece_recv, piece_out, sib_s, sib_r, s1, r1, s2, r2, bias_s, bias_r, end_sem) = rest
+     piece_send, piece_recv, piece_out, hop_send, sib_r, r1, r2, r3, r4, bias_sem, end_sem) = rest
     dp, me = lax.axis_index("dp"), lax.axis_index("expert")
     count, width = tokens_ref.shape
     total = n * pad
     early = 3 * width + 256
+    per = 256 // cap
     sibling = (1 - dp, me)
+    staged = per == 4
     lane = lax.broadcasted_iota(jnp.int32, (count, 128), 1)
 
     def peer(p):
@@ -86,7 +88,14 @@
 
     def swap(kind, p):
         src, dst = ((rows, xin), (cots, cin), (rows, back_in), (cots, returned), (ties, tie_in))[kind]
-        return remote(src.at[p], dst.at[p], swap_send.at[kind, p], swap_recv.at[kind, p], peer(p))
+        index = p // per if kind < 2 else 0
+        return remote(src.at[p], dst.at[p], swap_send.at[kind, index], swap_recv.at[kind, index], peer(p))
+
+    def swaps(kind, g=None):
+        src, dst = ((rows, xin), (cots, cin), (rows, back_in), (cots, returned), (ties, tie_in))[kind]
+        index, low, blocks_of = (0, 1, n - 1) if g is None else (0, 1, per - 1) if isinstance(g, int) else (g, g * per, per)
+        place = pl.ds(low, blocks_of)
+        return remote(src.at[place], dst.at[place], swap_send.at[kind, index], swap_recv.at[kind, index], peer(1))
 
     def start_swaps(kind, wanted):
         def one(p, _):
@@ -186,23 +195,29 @@
                                  pl.ds(pl.multiple_of(start + core * size, 128), size)]
 
             def hop(t, r, step):
-                return remote(at(t, r, dp), at(t, r, dp), tree_send.at[t, r + step], tree_recv.at[t, r + step], peer(step))
+                return remote(at(t, r, dp), at(t, r, dp), tree_send.at[t], tree_recv.at[t, r + step], peer(step))
 
             def arrived(t, r):
-                remote(at(t, r, dp), at(t, r, dp), tree_send.at[t, r], tree_recv.at[t, r], peer(r)).wait_recv()
+                remote(at(t, r, dp), at(t, r, dp), tree_send.at[t], tree_recv.at[t, r], peer(r)).wait_recv()
 
             def to_sibling(t, r, core):
-                return remote(at(t, r, core), at(t, r, core), turn_send.at[t, r], turn_recv.at[t, r], sibling)
+                return remote(at(t, r, core), at(t, r, core), turn_send.at[t], turn_recv.at[t], sibling)
+
+            def bulk(t, send, recv):
+                place = blocks.at[: (n - 1) * block, : (early // 2, width // 2)[t]]
+                return remote(place, place, send.at[t], recv.at[t] if recv is turn_recv else recv.at[t, 0], sibling)
 
             def turn(t, step):
                 if step == 0:
-                    for r in far:
-                        hop(t, 0, r).start()
+                    hop(t, 0, 8).start()
+                    hop(t, 0, 4).start()
                     hop(t, 0, third).start()
                     hop(t, 0, second).start()
                 elif step == 1:
-                    for r in far:
+                    for r in (8, 4, 12):
                         arrived(t, r)
+                        if r == 8:
+                            hop(t, 8, 4).start()
                         hop(t, r, third).start()
                         hop(t, r, second).start()
                         to_sibling(t, r, dp).start()
@@ -218,11 +233,7 @@
                         arrived(t, r + 3)
                         to_sibling(t, r + 3, dp).start()
                 else:
-                    def settle(r, _):
-                        to_sibling(t, r, 1 - dp).wait_recv()
-                        return 0
-
-                    lax.fori_loop(1, n, settle, 0)
+                    bulk(t, turn_send, turn_recv).wait_recv()
                     place = (slice(0, early), slice(early, w.shape[1]))[t]
                     for core in (0, 1):
                         for q in range(n // 2):
@@ -260,7 +271,7 @@
         scale = (width // heads) ** -0.5
 
         def put_probs(k):
-            return pltpu.make_async_copy(probs.at[pl.ds(2 * k, 2)], probs_hbm.at[pl.ds(2 * k, 2)], prob_sem.at[k])
+            return pltpu.make_async_copy(probs.at[pl.ds(2 * k, 2)], probs_hbm.at[pl.ds(2 * k, 2)], prob_sem.at[0])
 
         def attend(k, _):
             def part(c):
@@ -295,7 +306,7 @@
         moe = (mid * lax.rsqrt(jnp.mean(mid * mid, axis=1, keepdims=True) + EPSILON) * gains[1:2]).astype(BF16)
         moe_in[...] = moe
         rows[...] = to_slots(moe)
-        start_swaps(0, lambda p: (p < 4) | ((p % 4 == 0) & (p < 12)))
+        start_swaps(0, lambda p: (p < 4) | ((p % 4 == 0) & (p < 12)) if staged else p > 0)
         xin[0] = rows[0]
         put(2, attended)
         put(3, middle)
@@ -308,26 +319,14 @@
         put(6, chance)
         if direct:
             for t in (0, 1):
-                for r in far:
-                    hop(t, 0, r).wait_send()
-                for r in near:
-                    hop(t, r, second).wait_send()
-                    hop(t, r, third).wait_send()
-                    hop(t, r + second, third).wait_send()
-
-                def settle_sends(r, _):
-                    to_sibling(t, r, dp).wait_send()
-                    return 0
-
-                lax.fori_loop(1, n, settle_sends, 0)
+                bulk(t, tree_send, tree_recv).wait_send()
+                bulk(t, turn_send, turn_recv).wait_send()
         for copy in puts:
             copy.wait()
-        for k in range(heads // 2):
-            put_probs(k).wait()
+        pltpu.make_async_copy(probs, probs_hbm, prob_sem.at[0]).wait()
 
     def experts_both(win, wout, xt, rt, act, hgr):
         ff = win.shape[1]
-        per = 256 // cap
         group_rows = per * cap
         chunk = 1024
         loads = [pltpu.make_async_copy(win_hbm, win, load_sem.at[0]), pltpu.make_async_copy(wout_hbm, wout, load_sem.at[1])]
@@ -351,33 +350,39 @@
             return dot(pick.astype(BF16), block).astype(BF16).reshape(per, pad, width)
 
         def group(g, _):
-            def over(first, act_on):
+            def over(act_on):
                 def one(j, _):
                     @pl.when(g * per + j != 0)
                     def _():
                         act_on(g * per + j)
                     return 0
 
-                lax.fori_loop(first, per, one, 0)
+                lax.fori_loop(0, per, one, 0)
+
+            def all_of(kind, act_on):
+                @pl.when(g == 0)
+                def _():
+                    act_on(swaps(kind, 0))
+
+                @pl.when(g != 0)
+                def _():
+                    act_on(swaps(kind, g))
+
+            all_of(0, lambda copies: copies.wait_recv())
 
             @pl.when(g == 0)
             def _():
-                for p in (1, 2, 3):
-                    swap(0, p).wait_recv()
-                start_swaps(0, lambda p: (p >= 4) & (p % 4 != 0) & (p < 12))
+                if staged:
+                    start_swaps(0, lambda p: (p >= 4) & (p % 4 != 0) & (p < 12))
                 for load in loads:
                     load.wait()
-                over(4, lambda p: swap(0, p).wait_recv())
-
-            @pl.when(g != 0)
-            def _():
-                over(0, lambda p: swap(0, p).wait_recv())
-
-            @pl.when(g == 1)
-            def _():
-                start_swaps(0, lambda p: p >= 12)
-
-            over(0, lambda p: swap(1, p).wait_recv())
+
+            if staged:
+                @pl.when(g == 1)
+                def _():
+                    start_swaps(0, lambda p: p >= 12)
+
+            all_of(1, lambda copies: copies.wait_recv())
             here = pl.ds(pl.multiple_of(g * group_rows, group_rows), group_rows)
             x = packed_rows(xin, g)
             logits = dot(x, router[...])
@@ -399,21 +404,21 @@
 
             lax.fori_loop(0, ff // chunk, hidden_chunk, 0)
             back = spread_rows(dot(hgr[here], win[...], NT).astype(BF16))
-            over(0, lambda p: swap(0, p).wait_send())
+            all_of(0, lambda copies: copies.wait_send())
             rows[pl.ds(g * per, per)] = back
-            over(0, lambda p: swap(2, p).start())
+            over(lambda p: swap(2, p).start())
             produced = dot(act[here], wout[...], NT).astype(BF16)
             tie = jnp.sum(r.astype(F32) * produced.astype(F32), axis=1, keepdims=True)
             for j in range(per):
                 row = jnp.broadcast_to(tie[j * cap : (j + 1) * cap], (cap, 128)).T[0:8]
                 ties[g * per + j] = jnp.concatenate([row, jnp.zeros((8, 128 - cap), F32)], axis=1)
-            over(0, lambda p: swap(4, p).start())
-            over(0, lambda p: swap(1, p).wait_send())
+            over(lambda p: swap(4, p).start())
+            all_of(1, lambda copies: copies.wait_send())
             cots[pl.ds(g * per, per)] = spread_rows(produced)
 
             @pl.when(g < n // per // 2)
             def _():
-                over(0, lambda p: swap(3, p).start())
+                over(lambda p: swap(3, p).start())
 
             return 0
 
@@ -437,7 +442,7 @@
             out_piece(kind, k).start()
 
     def backward(w, packed, normed, attended, middle, moe_in, chance, prob, mid_grad, att_cot, packed_grad, normed_t, chunk,
-                 strip, bias_rows, sib_out, mine, out1, keep, out2):
+                 strip, bias_rows, mine, keep, out1, out2, out3, out4):
         loaded = (normed, packed, attended, middle, moe_in, w, chance)
         loads = [pltpu.make_async_copy(spilled[i], loaded[i], load_sem.at[i]) for i in range(SPILLS)]
         order = (6, 3, 5, 2, 4, 0, 1)
@@ -455,57 +460,70 @@
         if direct:
             half_rows = own * n
 
-            def hop(stage, k, d):
+            steps_out = ((out1, in1, r1), (out2, in2, r2), (out3, in3, r3), (out4, in4, r4))
+            ways = (1 + dp, 2 - dp, 4, 8)
+
+            def sib_out(k):
+                across = blocks.shape[1] // PART
+                return blocks.at[pl.ds(pl.multiple_of((k // across) * half_rows, 16), half_rows),
+                                 pl.ds(pl.multiple_of((k % across) * PART, 128), PART)]
+
+            def hop(stage, k):
                 if stage == 0:
-                    return remote(sib_out.at[k], sib_in.at[k], sib_s.at[k], sib_r.at[k], sibling)
-                if stage == 1:
-                    return remote(out1.at[k, d - 1], in1.at[k, d - 1], s1.at[k, d - 1], r1.at[k, d - 1], peer(d))
-                return remote(out2.at[k, d - 1], in2.at[k, d - 1], s2.at[k, d - 1], r2.at[k, d - 1], peer(4 * d))
-
-            def owners(k, d):
-                places = [pl.multiple_of(flipped(me, d + 4 * z, n) * own, 8) for z in range(4)]
+                    return remote(sib_out(k), sib_in.at[k], hop_send.at[0], sib_r.at[k], sibling)
+                src, dst, recv = steps_out[stage - 1]
+                return remote(src.at[k], dst.at[k], hop_send.at[stage], recv.at[k], peer(ways[stage - 1]))
+
+            def unit(k, u):
+                r = ways[0] * (u // 4) + ways[1] * ((u // 2) % 2) + ways[2] * (u % 2)
+                places = [pl.multiple_of(flipped(me, r + z, n) * own, 8) for z in (0, ways[3])]
                 return jnp.concatenate([mine[k % 2, pl.ds(place, own)] for place in places], axis=0)
 
             def stage(s, k):
                 if s == 0:
                     there = pl.ds(pl.multiple_of((1 - dp) * half_rows, 8), half_rows)
                     here = pl.ds(pl.multiple_of(dp * half_rows, 8), half_rows)
-                    sib_out[k] = chunk[there].astype(BF16)
-                    hop(0, k, 0).start()
+                    sib_out(k)[...] = chunk[there].astype(BF16)
+                    hop(0, k).start()
                     mine[k % 2] = chunk[here]
                 elif s == 1:
-                    hop(0, k, 0).wait_recv()
+                    hop(0, k).wait_recv()
                     mine[k % 2] = mine[k % 2] + sib_in[k].astype(F32)
-                    for d in (3, 1, 2):
-                        out1[k, d - 1] = owners(k, d).astype(BF16)
-                        hop(1, k, d).start()
-                    keep[k] = owners(k, 0)
-                elif s == 2:
-                    for d in (1, 2, 3):
-                        hop(1, k, d).wait_recv()
-                    total_rows = keep[k] + (in1[k, 0].astype(F32) + in1[k, 1].astype(F32)) + in1[k, 2].astype(F32)
-                    for z in (3, 2, 1):
-                        block = total_rows[own * z : own * (z + 1)]
-                        out2[k, z - 1] = jnp.concatenate(
-                            [block[:, 128 * c : 128 * (c + 1)] for c in range(3)]
-                            + [jnp.zeros((out2.shape[2] - 3 * own, 128), F32)], axis=0).astype(BF16)
-                        hop(2, k, z).start()
-                    keep[k, :own] = total_rows[:own]
+                    for u in range(4):
+                        out1[k, 2 * own * u : 2 * own * (u + 1)] = unit(k, u + 4).astype(BF16)
+                    hop(1, k).start()
+                    for u in range(4):
+                        keep[k, 2 * own * u : 2 * own * (u + 1)] = unit(k, u)
+                elif s in (2, 3):
+                    src, dst = steps_out[s - 1][0], steps_out[s - 2][1]
+                    left = 8 * own // (1 << (s - 1))
+                    hop(s - 1, k).wait_recv()
+                    value = keep[k, : 2 * left] + dst[k].astype(F32)
+                    src[k] = value[left:].astype(BF16)
+                    hop(s, k).start()
+                    keep[k, :left] = value[:left]
+                elif s == 4:
+                    hop(3, k).wait_recv()
+                    value = keep[k, : 2 * own] + in3[k].astype(F32)
+                    out4[k] = jnp.concatenate(
+                        [value[own:, 128 * c : 128 * (c + 1)] for c in range(3)]
+                        + [jnp.zeros((out4.shape[1] - 3 * own, 128), F32)], axis=0).astype(BF16)
+                    hop(4, k).start()
+                    keep[k, :own] = value[:own]
                 else:
-                    for z in (1, 2, 3):
-                        hop(2, k, z).wait_recv()
-                    far = (in2[k, 0].astype(F32) + in2[k, 1].astype(F32)) + in2[k, 2].astype(F32)
+                    hop(4, k).wait_recv()
+                    far = in4[k].astype(F32)
                     keep[k, :own] = keep[k, :own] + jnp.concatenate(
                         [far[own * c : own * (c + 1)] for c in range(3)], axis=1)
 
             def advance(k):
                 stage(0, k)
-                for s in range(1, 4):
+                for s in range(1, 6):
                     @pl.when((k - LAG[s] >= 0) & (k - LAG[s] < chunks))
                     def _():
                         stage(s, k - LAG[s])
 
-            done = {k: max(s for s in range(4) if LAG[s] <= chunks - 1 - k) for k in range(chunks)}
+            done = {k: max(s for s in range(6) if LAG[s] <= chunks - 1 - k) for k in range(chunks)}
 
             def drain(last, *which):
                 for k in which or range(chunks):
@@ -538,11 +556,10 @@
 
             lax.fori_loop(1, n, one, 0)
 
-        def arrive(p):
-            swap(2, p).wait_recv()
-            swap(4, p).wait_recv()
-
-        each_peer(arrive)
+        for kind, k in pieces:
+            piece(kind, k).wait_send()
+        swaps(2).wait_recv()
+        swaps(4).wait_recv()
         ties_row = exact((place == lax.broadcasted_iota(jnp.int32, (count, n), 1)).astype(F32), jnp.max(tie_in[...], axis=1))
         tie = jnp.sum(jnp.where(lane == rank, ties_row, 0.0), axis=1, keepdims=True)
         for i in order[:1]:
@@ -571,8 +588,8 @@
                 chunk[:, 256:] = jnp.zeros((width, PART - 256), F32)
             advance(k)
         normed_t[...] = normed[...].T
-        each_peer(lambda p: swap(2, p).wait_send())
-        start_swaps(3, lambda p: p >= n // 2)
+        swaps(2).wait_send()
+        start_swaps(3, lambda p: (p >= n // 2) & (p % 4 == 0))
 
         scale = (width // heads) ** -0.5
 
@@ -628,11 +645,25 @@
                 packed_grad[:, pl.ds(pl.multiple_of(c * width + k * 128, 128), 128)] = grads[:, c * 128 : (c + 1) * 128]
             chunk[...] = dot(normed_t[...], grads)
             advance(k + lead)
+
+            @pl.when(k ==  0)
+            def _():
+                start_swaps(3, lambda p: (p >= n // 2) & (p % 4 == 1))
+
+            @pl.when(k ==  0)
+            def _():
+                start_swaps(3, lambda p: (p >= n // 2) & (p % 4 == 2))
+
+            @pl.when(k ==  1)
+            def _():
+                start_swaps(3, lambda p: (p >= n // 2) & (p % 4 == 3))
+
             return 0
 
         lax.fori_loop(0, heads // 2, attend_back, 0)
         drain(1, chunks - 1)
         drain(2, *range(chunks - 1))
+        drain(3, *range(chunks - 3))
         sums = jnp.concatenate([jnp.sum(bias_rows[h], axis=0, keepdims=True) for h in range(heads)], axis=0)
         bias_out[...] = exact(sums, hot[...], NT)
         if direct:
@@ -640,14 +671,15 @@
             pair_hop.start()
 
             def bias_hop(p):
-                return remote(bias_in.at[me], bias_in.at[me], bias_s.at[p], bias_r.at[p], peer(p))
-
-            def bias_arrived(p):
-                there = flipped(me, p, n)
-                return remote(bias_in.at[there], bias_in.at[there], bias_s.at[p], bias_r.at[p], (dp, there))
+                return remote(bias_in.at[me], bias_in.at[me], bias_sem.at[0], bias_sem.at[1], peer(p))
+
+            place = bias_in.at[1:]
+            bias_all = remote(place, place, bias_sem.at[0], bias_sem.at[1], peer(1))
 
         normed_grad = dot(packed_grad[...], w[:, : 3 * width], NT)
         drain(2)
+        drain(3, *range(chunks - 1))
+        drain(4, *range(chunks - 4))
         if direct:
             pair_hop.wait()
             bias_in[me] = bias_out[...] + bias_pair[...]
@@ -660,13 +692,16 @@
         ends = [pltpu.make_async_copy(mid_grad, tokens_grad_hbm, end_sem.at[0]),
                 pltpu.make_async_copy(att_cot, mixed_hbm, end_sem.at[1])]
         ends[0].start()
-        each_peer(lambda p: swap(3, p).wait_recv())
+        drain(3)
+        drain(4, *range(chunks - 1))
+        swaps(3).wait_recv()
         gate = jnp.sum(jnp.where(picked, chance[...], 0.0), axis=1, keepdims=True)
         att_cot[...] = (middle[...] + gate * dot(hits, returned[...].reshape(total, width))).astype(BF16)
         ends[1].start()
         if direct:
-            drain(3)
-            each_peer(lambda p: bias_arrived(p).wait_recv())
+            drain(4)
+            drain(5)
+            bias_all.wait_recv()
             total_bias = bias_in[0]
             for p in range(1, n):
                 total_bias = total_bias + bias_in[p]
@@ -684,23 +719,16 @@
             total_gain = jnp.sum(qkv_grad_ref[...] * qkv_ref[...].astype(F32), axis=1, keepdims=True)
             gain_grad_ref[...] = jnp.broadcast_to(total_gain / extra_ref[128:256].T[:own, 0:1], gain_grad_ref.shape)
 
-            def settle_sends(k, _):
-                hop(0, k, 0).wait_send()
-                for d in (1, 2, 3):
-                    hop(1, k, d).wait_send()
-                    hop(2, k, d).wait_send()
-                return 0
-
-            lax.fori_loop(0, chunks, settle_sends, 0)
-            each_peer(lambda p: bias_hop(p).wait_send())
+            for s, sent in enumerate((sib_in, out1, out2, out3, out4)):
+                remote(sent, sent, hop_send.at[s], sib_r.at[0], sibling).wait_send()
+            bias_all.wait_send()
         else:
             bias_grad_ref[...] = bias_out[...]
         for kind in (3, 4):
-            each_peer(lambda p: swap(kind, p).wait_send())
+            swaps(kind).wait_send()
         for copy in ends:
             copy.wait()
         for kind, k in pieces:
-            piece(kind, k).wait_send()
             out_piece(kind, k).wait()
 
     wide = w_columns(width)
@@ -726,8 +754,8 @@
         backward, *shared, scratch((2, 2, count, count), BF16), scratch((count, width), F32), scratch((count, width), BF16),
         scratch((count, 3 * width), BF16), scratch((width, count), BF16), scratch((width, PART), F32),
         scratch((128, 2 * count), F32), scratch((heads, 8, 2 * count), F32),
-        buffer((own_rows * n, PART), BF16), scratch((2, own_rows * n, PART), F32), buffer((3, 4 * own_rows, PART), BF16),
-        buffer((4 * own_rows, PART), F32), buffer((3, -(-3 * own_rows // 16) * 16, 128), BF16))
+        scratch((2, own_rows * n, PART), F32), buffer((8 * own_rows, PART), F32),
+        *[buffer((own_rows << s, PART), BF16) for s in (3, 2, 1)], buffer((-(-3 * own_rows // 16) * 16, 128), BF16))
 
 
 def w_columns(width):
@@ -773,12 +801,12 @@
             scratch((8, width), F32), scratch((kinds, 2 * count), F32), scratch((width, 128), BF16),
             slots, slots, scratch((n, 8, 128), F32), slots, slots, slots, slots, scratch((n, 8, 128), F32),
             scratch((2, steps, width, WIDE), BF16),
-            landing(own * n, PART), landing(3, 4 * own, PART), landing(3, short, 128),
+            landing(own * n, PART), *[landing(own << s, PART) for s in (3, 2, 1)], landing(short, 128),
             scratch((heads, kinds), F32), scratch((n, heads, kinds), F32), scratch((heads, kinds), F32),
-            dma((SPILLS,)), dma((heads // 2,)), dma((SPILLS,)), dma((4,)), dma((5, n)), dma((5, n)),
-            dma((2, n)), dma((2, n)), dma((2, n)), dma((2, n)),
+            dma((SPILLS,)), dma((2,)), dma((SPILLS,)), dma((4,)), dma((5, n * cap // 256)), dma((5, n * cap // 256)),
+            dma((2,)), dma((2, n)), dma((2,)), dma((2,)),
             dma((2, steps)), dma((2, steps)), dma((2, steps)),
-            dma((chunks,)), dma((chunks,)), *[dma((chunks, 3)) for _ in range(4)], dma((n,)), dma((n,)), dma((2,)),
+            dma((5,)), *[dma((chunks,)) for _ in range(5)], dma((2,)), dma((2,)),
         ],
         compiler_params=pltpu.CompilerParams(
             collective_id=1, has_side_effects=True, vmem_limit_bytes=63 * 1024 * 1024),

time: 205 us -> 191 us (0.932)
  Pallas kernels: 203 us -> 189 us
    pallas_call x1, Pallas kernels: 194 us -> 180 us  [layer(): pl.pallas_call(functools.partial(layer_kernel, n, cap, pad, experts, head...]
where the time goes in v5:
time: 191 us
  Pallas kernels  189 us (99%)
    pallas_call x1, Pallas kernels, layer(): pl.pallas_call(functools.partial(layer_kernel, n, cap, pad, experts, head...  180 us
    pallas_call x1, Pallas kernels, finish(): pl.pallas_call(finish_kernel, out_shape=(shape(mixed.shape, BF16), shape(...  8.9 us

profile of v5, /device:TPU:0, one launch (start us, length us, event | category | flops | bytes accessed | tf_op | source)
XLA Modules:
  0.0 191.1 jit_solution(2913219406783441957)
XLA Ops:
  0.6 1.4 convert_add_fusion.refs_4_
  2.0 180.0 %layer.1 = (bf16[512,768]{1,0:T(8,128)(2,1)}, f32[512,768]{1,0:T(8,128)}, f32[24,2304]{1,0:T(8,128)}, f32[24,768]{1,0:T(8,128)}, f32[24,256]{1,0:T(8,128)}, /*in...) custom-call(bf16[512,768]{1,0:T(8,128)(2,1)} %refs_0_.1, ...), custom_call_target="tpu_custom_call" | custom-call | tf_op jit(solution)/shard_map/layer/pallas_call | solution.py:793
  182.0 8.9 %finish.1 = (bf16[512,768]{1,0:T(8,128)(2,1)}, f32[512,768]{1,0:T(8,128)}, f32[1,768,1536]{2,1,0:T(8,128)}, f32[1,768,1536]{2,1,0:T(8,128)}, f32[24,2304]{1,0:T(...) custom-call(bf16[512,768]{1,0:T(8,128)(2,1)} %get-tuple-element.29.m, ...), custom_call_target="tpu_custom_call" | custom-call | tf_op jit(solution)/shard_map/finish/pallas_call | solution.py:868

commit v6 on v5

--- a/solution.py
+++ b/solution.py
@@ -62,14 +62,20 @@
 
 
 def layer_kernel(n, cap, pad, experts, heads, direct, *refs):
-    (tokens_ref, cot_ref, qkv_ref, att_ref, extra_ref, full_hbm, routes_ref, table_ref, buckets_hbm, win_hbm, wout_hbm,
-     mixed_hbm, tokens_grad_hbm, qkv_grad_ref, att_grad_ref, extra_grad_ref, gain_grad_ref, bias_grad_ref,
-     gin_hbm, gout_hbm, probs_hbm, *rest) = refs
+    given, (full_hbm, buckets_hbm, win_hbm, wout_hbm), refs = refs[:7], refs[7:11], refs[11:]
+    (mixed_hbm, tokens_grad_hbm, qkv_grad_hbm, *small_hbm), refs = refs[:7], refs[7:]
+    (gin_hbm, gout_hbm, probs_hbm, *rest) = refs
     spilled, rest = rest[:SPILLS], rest[SPILLS:]
     (blocks, shard, gains, hot, router, rows, cots, ties, xin, cin, back_in, returned, tie_in, sib_recv,
      sib_in, in1, in2, in3, in4, bias_out, bias_in, bias_pair,
+     tokens_ref, cot_ref, qkv_ref, att_ref, extra_ref, routes_ref, table_ref,
+     qkv_grad_ref, att_grad_ref, extra_grad_ref, gain_grad_ref, bias_grad_ref,
      put_sem, prob_sem, load_sem, pair_sem, swap_send, swap_recv, tree_send, tree_recv, turn_send, turn_recv,
-     piece_send, piece_recv, piece_out, hop_send, sib_r, r1, r2, r3, r4, bias_sem, end_sem) = rest
+     piece_send, piece_recv, piece_out, hop_send, sib_r, r1, r2, r3, r4, bias_sem, end_sem, given_sem, small_sem) = rest
+    held = (tokens_ref, cot_ref, qkv_ref, att_ref, extra_ref, routes_ref, table_ref)
+    fetches = [pltpu.make_async_copy(src, dst, given_sem.at[i]) for i, (src, dst) in enumerate(zip(given, held))]
+    for copy in fetches:
+        copy.start()
     dp, me = lax.axis_index("dp"), lax.axis_index("expert")
     count, width = tokens_ref.shape
     total = n * pad
@@ -106,7 +112,7 @@
 
         lax.fori_loop(1, n, one, 0)
 
-    def greet_all():
+    def greet_all(prepare):
         barrier = pltpu.get_barrier_semaphore()
 
         def greet(p, _):
@@ -115,6 +121,7 @@
 
         lax.fori_loop(1, n, greet, 0)
         pl.semaphore_signal(barrier, inc=1, device_id=sibling, device_id_type=MESH)
+        prepare()
         pl.semaphore_wait(barrier, n)
 
     half = win_hbm.shape[1] // 2
@@ -141,11 +148,15 @@
                    for i, c in enumerate((0, count - 128))]
         for copy in offsets:
             copy.start()
-        if direct:
-            weights[:, : 3 * width] = qkv_ref[...].astype(F32)
-            weights[:, 3 * width : early] = extra_ref[...].T[: weights.shape[0]]
-            weights[:, early:] = att_ref[...].astype(F32)
-        greet_all()
+        def prepare():
+            for copy in fetches:
+                copy.wait()
+            if direct:
+                weights[:, : 3 * width] = qkv_ref[...].astype(F32)
+                weights[:, 3 * width : early] = extra_ref[...].T[: weights.shape[0]]
+                weights[:, early:] = att_ref[...].astype(F32)
+
+        greet_all(prepare)
         if direct:
             own = weights.shape[0]
             block = 2 * own
@@ -533,7 +544,7 @@
 
         else:
             def advance(k):
-                copy = pltpu.make_async_copy(chunk, qkv_grad_ref.at[k], end_sem.at[0])
+                copy = pltpu.make_async_copy(chunk, qkv_grad_hbm.at[k], end_sem.at[0])
                 copy.start()
                 copy.wait()
 
@@ -724,6 +735,12 @@
             bias_all.wait_send()
         else:
             bias_grad_ref[...] = bias_out[...]
+        small = [*zip((att_grad_ref, extra_grad_ref, gain_grad_ref, bias_grad_ref), small_hbm)]
+        if direct:
+            small.append((qkv_grad_ref, qkv_grad_hbm))
+        for i, (src, dst) in enumerate(small):
+            ends.append(pltpu.make_async_copy(src, dst, small_sem.at[i]))
+            ends[-1].start()
         for kind in (3, 4):
             swaps(kind).wait_send()
         for copy in ends:
@@ -772,7 +789,6 @@
     steps = ff // 2 // WIDE
     short = -(-3 * own // 16) * 16
     any_ = pl.BlockSpec(memory_space=pl.ANY)
-    vmem = pl.BlockSpec(memory_space=pltpu.VMEM)
     dma = pltpu.SemaphoreType.DMA
     scratch = pltpu.VMEM
     shape = jax.ShapeDtypeStruct
@@ -780,20 +796,21 @@
     def landing(*rest):
         return scratch((chunks, *rest) if direct else (16, 128), BF16)
 
+    small = ((own, width), (own, 256), (own, 128), (heads, kinds))
     outs = [
         (shape((count, width), BF16), any_), (shape((count, width), F32), any_),
-        (shape((own, 3 * width), F32), vmem) if direct else (shape((chunks, width, PART), F32), any_),
-        (shape((own, width), F32), vmem), (shape((own, 256), F32), vmem), (shape((own, 128), F32), vmem),
-        (shape((heads, kinds), F32), vmem), (shape((width, ff // 2), BF16), any_), (shape((width, ff // 2), BF16), any_),
+        (shape((own, 3 * width) if direct else (chunks, width, PART), F32), any_),
+        *[(shape(dims, F32), any_) for dims in small], (shape((width, ff // 2), BF16), any_), (shape((width, ff // 2), BF16), any_),
         (shape((heads, count, count), BF16), any_), (shape((count, width), BF16), any_),
         (shape((count, 3 * width), BF16), any_), (shape((count, width), BF16), any_), (shape((count, width), F32), any_),
         (shape((count, width), BF16), any_), (shape((width, wide), BF16), any_), (shape((count, 128), F32), any_),
     ]
     slots = scratch((n, pad, width), BF16)
+    given = (tokens, cotangent, qkv, att, extra, routes, table)
     return pl.pallas_call(
         functools.partial(layer_kernel, n, cap, pad, experts, heads, direct),
         out_shape=tuple(o[0] for o in outs),
-        in_specs=[vmem] * 5 + [any_, vmem, vmem, any_, any_, any_],
+        in_specs=[any_] * 11,
         out_specs=tuple(o[1] for o in outs),
         scratch_shapes=[
             scratch((width, max(wide, 2 * steps * WIDE)), BF16),
@@ -803,22 +820,28 @@
             scratch((2, steps, width, WIDE), BF16),
             landing(own * n, PART), *[landing(own << s, PART) for s in (3, 2, 1)], landing(short, 128),
             scratch((heads, kinds), F32), scratch((n, heads, kinds), F32), scratch((heads, kinds), F32),
+            *[scratch(a.shape, a.dtype) for a in given], scratch((own, 3 * width), F32), *[scratch(dims, F32) for dims in small],
             dma((SPILLS,)), dma((2,)), dma((SPILLS,)), dma((4,)), dma((5, n * cap // 256)), dma((5, n * cap // 256)),
             dma((2,)), dma((2, n)), dma((2,)), dma((2,)),
             dma((2, steps)), dma((2, steps)), dma((2, steps)),
-            dma((5,)), *[dma((chunks,)) for _ in range(5)], dma((2,)), dma((2,)),
+            dma((5,)), *[dma((chunks,)) for _ in range(5)], dma((2,)), dma((2,)), dma((7,)), dma((5,)),
         ],
         compiler_params=pltpu.CompilerParams(
             collective_id=1, has_side_effects=True, vmem_limit_bytes=63 * 1024 * 1024),
         name="layer",
-    )(tokens, cotangent, qkv, att, extra, full, routes, table, buckets, win, wout)
+    )(*given, full, buckets, win, wout)
 
 
 def finish_kernel(
-    mixed_in, tokens_in, in_hbm, out_hbm, qkv_in, att_in, extra_in, gain_in, bias_in,
-    mixed_out, tokens_out, in_out, out_out, qkv_out, att_out, router_out, gain_out, gain_moe_out, bias_out,
-    mixed, tokens, narrow, wide, sem, load_sem, store_sem,
+    mixed_in, tokens_in, in_hbm, out_hbm, *refs,
 ):
+    small_ins, (mixed_out, tokens_out, in_out, out_out), small_outs, refs = refs[:5], refs[5:9], refs[9:15], refs[15:]
+    (mixed, tokens, narrow, wide, sem, load_sem, store_sem, small_sem) , held = refs[:8], refs[8:]
+    fetches = [pltpu.make_async_copy(src, dst, small_sem.at[i]) for i, (src, dst) in enumerate(zip(small_ins, held[:5]))]
+    leaves = [pltpu.make_async_copy(src, dst, small_sem.at[5 + i]) for i, (src, dst) in enumerate(zip(held[5:], small_outs))]
+    qkv_in, att_in, extra_in, gain_in, bias_in, qkv_out, att_out, router_out, gain_out, gain_moe_out, bias_out = held
+    for copy in fetches:
+        copy.start()
     ins = [pltpu.make_async_copy(mixed_in, mixed, sem.at[0]), pltpu.make_async_copy(tokens_in, tokens, sem.at[1])]
     outs = [pltpu.make_async_copy(mixed, mixed_out, sem.at[2]), pltpu.make_async_copy(tokens, tokens_out, sem.at[3])]
     parts, rows = narrow.shape[1], narrow.shape[2]
@@ -836,50 +859,54 @@
             load(kind, k).start()
     for copy in ins:
         copy.start()
+    for k in range(parts):
+        for kind in (0, 1):
+            load(kind, k).wait()
+            wide[kind, k] = narrow[kind, k].astype(F32)
+            store(kind, k).start()
+    for copy in fetches:
+        copy.wait()
     qkv_out[...] = qkv_in[...]
     att_out[...] = att_in[...]
     router_out[...] = extra_in[:, :128].T[: router_out.shape[0]]
     gain_out[...] = gain_in[...].T[0:1]
     gain_moe_out[...] = extra_in[:, 128:].T[0:1]
     bias_out[...] = bias_in[...]
-    for k in range(parts):
-        for kind in (0, 1):
-            load(kind, k).wait()
-            wide[kind, k] = narrow[kind, k].astype(F32)
-            store(kind, k).start()
+    for copy in leaves:
+        copy.start()
     for copy_in, copy_out in zip(ins, outs):
         copy_in.wait()
         copy_out.start()
     for k in range(parts):
         for kind in (0, 1):
             store(kind, k).wait()
-    for copy in outs:
+    for copy in outs + leaves:
         copy.wait()
 
 
 def finish(experts, mixed, tokens_grad, grad_in, grad_out, qkv, att, extra, gain, bias):
     any_ = pl.BlockSpec(memory_space=pl.ANY)
-    vmem = pl.BlockSpec(memory_space=pltpu.VMEM)
     dma = pltpu.SemaphoreType.DMA
     parts = 8
     rows = grad_in.shape[0] // parts
     own = qkv.shape[0]
     shape = jax.ShapeDtypeStruct
+    small = (qkv.shape, att.shape, (experts, own), (1, own), (1, own), bias.shape)
     return pl.pallas_call(
         finish_kernel,
         out_shape=(
             shape(mixed.shape, BF16), shape(tokens_grad.shape, F32), shape((1, *grad_in.shape), F32),
-            shape((1, *grad_out.shape), F32), shape(qkv.shape, F32), shape(att.shape, F32), shape((experts, own), F32),
-            shape((1, own), F32), shape((1, own), F32), shape(bias.shape, F32),
+            shape((1, *grad_out.shape), F32), *[shape(dims, F32) for dims in small],
         ),
-        in_specs=[any_] * 4 + [vmem] * 5,
-        out_specs=tuple([any_] * 4 + [vmem] * 6),
+        in_specs=[any_] * 9,
+        out_specs=tuple([any_] * 10),
         scratch_shapes=[
             pltpu.VMEM(mixed.shape, BF16),
             pltpu.VMEM(tokens_grad.shape, F32),
             pltpu.VMEM((2, parts, rows, grad_in.shape[1]), BF16),
             pltpu.VMEM((2, parts, rows, grad_in.shape[1]), F32),
-            dma((4,)), dma((2, parts)), dma((2, parts)),
+            dma((4,)), dma((2, parts)), dma((2, parts)), dma((11,)),
+            *[pltpu.VMEM(dims, F32) for dims in (*[a.shape for a in (qkv, att, extra, gain, bias)], *small)],
         ],
         compiler_params=pltpu.CompilerParams(vmem_limit_bytes=60 * 1024 * 1024),
         name="finish",

time: 191 us -> 189 us (0.990)
  Pallas kernels: 189 us -> 186 us
where the time goes in v6:
time: 189 us; the launch traced here: 188 us
  Pallas kernels  186 us (98%)
    pallas_call x1, Pallas kernels, layer(): pl.pallas_call(functools.partial(layer_kernel, n, cap, pad, experts, head...  178 us
    pallas_call x1, Pallas kernels, finish(): pl.pallas_call(finish_kernel, out_shape=(shape(mixed.shape, BF16), shape(...  7.62 us

profile of v6, /device:TPU:0, one launch (start us, length us, event | category | flops | bytes accessed | tf_op | source)
XLA Modules:
  0.0 188.0 jit_solution(8926449188216423384)
XLA Ops:
  0.6 1.4 convert_add_fusion.refs_4_
  2.0 178.2 %layer.1 = (bf16[512,768]{1,0:T(8,128)(2,1)}, f32[512,768]{1,0:T(8,128)}, f32[24,2304]{1,0:T(8,128)}, f32[24,768]{1,0:T(8,128)}, f32[24,256]{1,0:T(8,128)}, /*in...) custom-call(bf16[512,768]{1,0:T(8,128)(2,1)} %refs_0_.1, ...), custom_call_target="tpu_custom_call" | custom-call | tf_op jit(solution)/shard_map/layer/pallas_call | solution.py:810
  180.2 7.6 %finish.1 = (bf16[512,768]{1,0:T(8,128)(2,1)}, f32[512,768]{1,0:T(8,128)}, f32[1,768,1536]{2,1,0:T(8,128)}, f32[1,768,1536]{2,1,0:T(8,128)}, f32[24,2304]{1,0:T(...) custom-call(bf16[512,768]{1,0:T(8,128)(2,1)} %get-tuple-element.29.m, ...), custom_call_target="tpu_custom_call" | custom-call | tf_op jit(solution)/shard_map/finish/pallas_call | solution.py:895

commit v7 on v6

--- a/solution.py
+++ b/solution.py
@@ -62,17 +62,17 @@
 
 
 def layer_kernel(n, cap, pad, experts, heads, direct, *refs):
-    given, (full_hbm, buckets_hbm, win_hbm, wout_hbm), refs = refs[:7], refs[7:11], refs[11:]
+    given, (full_hbm, buckets_hbm, win_hbm, wout_hbm), refs = refs[:9], refs[9:13], refs[13:]
     (mixed_hbm, tokens_grad_hbm, qkv_grad_hbm, *small_hbm), refs = refs[:7], refs[7:]
     (gin_hbm, gout_hbm, probs_hbm, *rest) = refs
     spilled, rest = rest[:SPILLS], rest[SPILLS:]
     (blocks, shard, gains, hot, router, rows, cots, ties, xin, cin, back_in, returned, tie_in, sib_recv,
      sib_in, in1, in2, in3, in4, bias_out, bias_in, bias_pair,
-     tokens_ref, cot_ref, qkv_ref, att_ref, extra_ref, routes_ref, table_ref,
+     tokens_ref, cot_ref, qkv_ref, att_ref, router_own, gain_one, gain_two, routes_ref, table_ref, extra_ref,
      qkv_grad_ref, att_grad_ref, extra_grad_ref, gain_grad_ref, bias_grad_ref,
      put_sem, prob_sem, load_sem, pair_sem, swap_send, swap_recv, tree_send, tree_recv, turn_send, turn_recv,
      piece_send, piece_recv, piece_out, hop_send, sib_r, r1, r2, r3, r4, bias_sem, end_sem, given_sem, small_sem) = rest
-    held = (tokens_ref, cot_ref, qkv_ref, att_ref, extra_ref, routes_ref, table_ref)
+    held = (tokens_ref, cot_ref, qkv_ref, att_ref, router_own, gain_one, gain_two, routes_ref, table_ref)
     fetches = [pltpu.make_async_copy(src, dst, given_sem.at[i]) for i, (src, dst) in enumerate(zip(given, held))]
     for copy in fetches:
         copy.start()
@@ -153,7 +153,12 @@
                 copy.wait()
             if direct:
                 weights[:, : 3 * width] = qkv_ref[...].astype(F32)
-                weights[:, 3 * width : early] = extra_ref[...].T[: weights.shape[0]]
+                here = weights.shape[0]
+                extra_ref[...] = jnp.zeros_like(extra_ref)
+                extra_ref[0:experts, 0:here] = router_own[...].astype(F32)
+                for i, one in enumerate((gain_one, gain_two)):
+                    extra_ref[128 + i : 129 + i, 0:here] = one[...].astype(F32).reshape(1, here)
+                weights[:, 3 * width : early] = extra_ref[...].T[:here]
                 weights[:, early:] = att_ref[...].astype(F32)
 
         greet_all(prepare)
@@ -657,15 +662,15 @@
             chunk[...] = dot(normed_t[...], grads)
             advance(k + lead)
 
-            @pl.when(k ==  0)
+            @pl.when(k == 0)
             def _():
                 start_swaps(3, lambda p: (p >= n // 2) & (p % 4 == 1))
 
-            @pl.when(k ==  0)
+            @pl.when(k == 0)
             def _():
                 start_swaps(3, lambda p: (p >= n // 2) & (p % 4 == 2))
 
-            @pl.when(k ==  1)
+            @pl.when(k == 0)
             def _():
                 start_swaps(3, lambda p: (p >= n // 2) & (p % 4 == 3))
 
@@ -779,7 +784,8 @@
     return 4 * width + 256
 
 
-def layer(n, cap, pad, experts, heads, direct, tokens, cotangent, qkv, att, extra, full, routes, table, buckets, win, wout):
+def layer(n, cap, pad, experts, heads, direct, tokens, cotangent, qkv, att, router, one, two, full, routes, table, buckets,
+          win, wout):
     count, width = tokens.shape
     wide = w_columns(width)
     own = qkv.shape[0]
@@ -806,11 +812,11 @@
         (shape((count, width), BF16), any_), (shape((width, wide), BF16), any_), (shape((count, 128), F32), any_),
     ]
     slots = scratch((n, pad, width), BF16)
-    given = (tokens, cotangent, qkv, att, extra, routes, table)
+    given = (tokens, cotangent, qkv, att, router, one, two, routes, table)
     return pl.pallas_call(
         functools.partial(layer_kernel, n, cap, pad, experts, heads, direct),
         out_shape=tuple(o[0] for o in outs),
-        in_specs=[any_] * 11,
+        in_specs=[any_] * 13,
         out_specs=tuple(o[1] for o in outs),
         scratch_shapes=[
             scratch((width, max(wide, 2 * steps * WIDE)), BF16),
@@ -820,11 +826,11 @@
             scratch((2, steps, width, WIDE), BF16),
             landing(own * n, PART), *[landing(own << s, PART) for s in (3, 2, 1)], landing(short, 128),
             scratch((heads, kinds), F32), scratch((n, heads, kinds), F32), scratch((heads, kinds), F32),
-            *[scratch(a.shape, a.dtype) for a in given], scratch((own, 3 * width), F32), *[scratch(dims, F32) for dims in small],
+            *[scratch(a.shape, a.dtype) for a in given], scratch((256, 128), F32), scratch((own, 3 * width), F32), *[scratch(dims, F32) for dims in small],
             dma((SPILLS,)), dma((2,)), dma((SPILLS,)), dma((4,)), dma((5, n * cap // 256)), dma((5, n * cap // 256)),
             dma((2,)), dma((2, n)), dma((2,)), dma((2,)),
             dma((2, steps)), dma((2, steps)), dma((2, steps)),
-            dma((5,)), *[dma((chunks,)) for _ in range(5)], dma((2,)), dma((2,)), dma((7,)), dma((5,)),
+            dma((5,)), *[dma((chunks,)) for _ in range(5)], dma((2,)), dma((2,)), dma((9,)), dma((5,)),
         ],
         compiler_params=pltpu.CompilerParams(
             collective_id=1, has_side_effects=True, vmem_limit_bytes=63 * 1024 * 1024),
@@ -924,13 +930,16 @@
     cap = max(2, 2 * count // experts)
     pad = max(16, cap)
     direct = n == 16 and own % 8 == 0
-    extra = sum(jnp.pad(part.astype(F32), ((low, 256 - low - part.shape[0]), (0, 128 - own)))
-                for low, part in ((0, w_router.T), (128, gain_attn[None]), (129, gain_moe[None])))
-    full = w_att if direct else lax.all_gather(
-        jnp.concatenate([w_qkv, extra[:, :own].T.astype(BF16), w_att], axis=1), axes, axis=0, tiled=True)
+    if direct:
+        full = w_att
+    else:
+        extra = jnp.concatenate(
+            [w_router, jnp.zeros((own, 128 - experts), BF16), gain_attn[:, None], gain_moe[:, None],
+             jnp.zeros((own, 126), BF16)], axis=1)
+        full = lax.all_gather(jnp.concatenate([w_qkv, extra, w_att], axis=1), axes, axis=0, tiled=True)
     mixed, grad_tokens, grad_qkv, grad_att, grad_extra, grad_gain, grad_bias, grad_in, grad_out = layer(
-        n, cap, pad, experts, heads, direct, tokens, cotangent, w_qkv, w_att, extra, full, routes.T, rel_bias.T, buckets,
-        w_in[0], w_out[0])[:9]
+        n, cap, pad, experts, heads, direct, tokens, cotangent, w_qkv, w_att, w_router.T, gain_attn, gain_moe, full, routes.T,
+        rel_bias.T, buckets,        w_in[0], w_out[0])[:9]
     if not direct:
         lead = grad_qkv.shape[0] - heads // 2
         early = jnp.concatenate([grad_qkv[k] for k in range(lead)], axis=1)

time: 189 us -> 187 us (0.989)
  no operation moved by 1% of the time
where the time goes in v7:
time: 187 us
  Pallas kernels  186 us (99%)
    pallas_call x1, Pallas kernels, layer(): pl.pallas_call(functools.partial(layer_kernel, n, cap, pad, experts, head...  179 us
    pallas_call x1, Pallas kernels, finish(): pl.pallas_call(finish_kernel, out_shape=(shape(mixed.shape, BF16), shape(...  7.62 us

profile of v7, /device:TPU:0, one launch (start us, length us, event | category | flops | bytes accessed | tf_op | source)
XLA Modules:
  0.0 187.1 jit_solution(5485223499988433371)
XLA Ops:
  0.6 178.6 %layer.1 = (bf16[512,768]{1,0:T(8,128)(2,1)}, f32[512,768]{1,0:T(8,128)}, f32[24,2304]{1,0:T(8,128)}, f32[24,768]{1,0:T(8,128)}, f32[24,256]{1,0:T(8,128)}, /*in...) custom-call(bf16[512,768]{1,0:T(8,128)(2,1)} %refs_0_.1, ...), custom_call_target="tpu_custom_call" | custom-call | tf_op jit(solution)/shard_map/layer/pallas_call | solution.py:816
  179.3 7.6 %finish.1 = (bf16[512,768]{1,0:T(8,128)(2,1)}, f32[512,768]{1,0:T(8,128)}, f32[1,768,1536]{2,1,0:T(8,128)}, f32[1,768,1536]{2,1,0:T(8,128)}, f32[24,2304]{1,0:T(...) custom-call(bf16[512,768]{1,0:T(8,128)(2,1)} %get-tuple-element.29.m, ...), custom_call_target="tpu_custom_call" | custom-call | tf_op jit(solution)/shard_map/finish/pallas_call | solution.py:901

commit v8 on v7

--- a/solution.py
+++ b/solution.py
@@ -860,16 +860,20 @@
         return pltpu.make_async_copy(
             wide.at[kind, k], (in_out, out_out)[kind].at[0, pl.ds(k * rows, rows)], store_sem.at[kind, k])
 
+    for copy in ins:
+        copy.start()
     for k in range(parts):
         for kind in (0, 1):
             load(kind, k).start()
-    for copy in ins:
-        copy.start()
     for k in range(parts):
         for kind in (0, 1):
             load(kind, k).wait()
             wide[kind, k] = narrow[kind, k].astype(F32)
             store(kind, k).start()
+        if k == 1:
+            for copy_in, copy_out in zip(ins, outs):
+                copy_in.wait()
+                copy_out.start()
     for copy in fetches:
         copy.wait()
     qkv_out[...] = qkv_in[...]
@@ -880,9 +884,6 @@
     bias_out[...] = bias_in[...]
     for copy in leaves:
         copy.start()
-    for copy_in, copy_out in zip(ins, outs):
-        copy_in.wait()
-        copy_out.start()
     for k in range(parts):
         for kind in (0, 1):
             store(kind, k).wait()

time: 187 us -> 187 us (level)
  no operation moved by 1% of the time
where the time goes in v8:
time: 187 us
  Pallas kernels  186 us (99%)
    pallas_call x1, Pallas kernels, layer(): pl.pallas_call(functools.partial(layer_kernel, n, cap, pad, experts, head...  179 us
    pallas_call x1, Pallas kernels, finish(): pl.pallas_call(finish_kernel, out_shape=(shape(mixed.shape, BF16), shape(...  7.79 us

profile of v8, /device:TPU:0, one launch (start us, length us, event | category | flops | bytes accessed | tf_op | source)
XLA Modules:
  0.0 187.3 jit_solution(14527286677219062719)
XLA Ops:
  0.6 178.6 %layer.1 = (bf16[512,768]{1,0:T(8,128)(2,1)}, f32[512,768]{1,0:T(8,128)}, f32[24,2304]{1,0:T(8,128)}, f32[24,768]{1,0:T(8,128)}, f32[24,256]{1,0:T(8,128)}, /*in...) custom-call(bf16[512,768]{1,0:T(8,128)(2,1)} %refs_0_.1, ...), custom_call_target="tpu_custom_call" | custom-call | tf_op jit(solution)/shard_map/layer/pallas_call | solution.py:816
  179.3 7.8 %finish.1 = (bf16[512,768]{1,0:T(8,128)(2,1)}, f32[512,768]{1,0:T(8,128)}, f32[1,768,1536]{2,1,0:T(8,128)}, f32[1,768,1536]{2,1,0:T(8,128)}, f32[24,2304]{1,0:T(...) custom-call(bf16[512,768]{1,0:T(8,128)(2,1)} %get-tuple-element.29.m, ...), custom_call_target="tpu_custom_call" | custom-call | tf_op jit(solution)/shard_map/finish/pallas_call | solution.py:902
